TPU v7x, 32 devices: a whole 2x2x4 slice. The times are simulated.
32 devices in a mesh: seq: 32 (over z, y, x, core).
Axes of the slice: x: 2, y: 2, z: 4, core: 2. Of those that a mesh axis runs over, the one named last changes fastest.
Arguments:
- tokens_in: bfloat16 [16384, 1024], P('seq'), may hold values from -6 to 6
- w_router: bfloat16 [1024], replicated, may hold values from -0.1875 to 0.1875
- gain_attn: bfloat16 [1024], replicated, may hold values from 0.25 to 1.75
- w_query: bfloat16 [1024, 1024], replicated, may hold values from -0.1875 to 0.1875
- w_key: bfloat16 [1024, 1024], replicated, may hold values from -0.1875 to 0.1875
- w_value: bfloat16 [1024, 1024], replicated, may hold values from -0.1875 to 0.1875
- w_out: bfloat16 [1024, 1024], replicated, may hold values from -3 to 3
- gain_mlp: bfloat16 [1024], replicated, may hold values from 0.25 to 1.75
- w_up: bfloat16 [1024, 4096], replicated, may hold values from -0.1875 to 0.1875
- w_down: bfloat16 [4096, 1024], replicated, may hold values from -0.09375 to 0.09375
- out_grad: bfloat16 [16384, 1024], P('seq'), may hold values from -6 to 6
- lengths: int32 [4], replicated, may hold values from 96 to 16000, as said below
- counts: int32 [32], replicated, may hold values from 16 to 64, as said below
- chosen: int32 [2048], replicated, may hold values from 0 to 511, as said below
Outputs:
- output: bfloat16 [16384, 1024], P('seq')
- input_grad: bfloat16 [16384, 1024], P('seq')
- grad_router: float32 [1024], P('seq')
- grad_gain_attn: float32 [1024], P('seq')
- grad_query: float32 [1024, 1024], P('seq')
- grad_key: float32 [1024, 1024], P('seq')
- grad_value: float32 [1024, 1024], P('seq')
- grad_out: float32 [1024, 1024], P('seq')
- grad_gain_mlp: float32 [1024], P('seq')
- grad_up: float32 [1024, 4096], P('seq')
- grad_down: float32 [4096, 1024], P('seq')
Inputs may be any that keep to these rules, and one draw needn't show every extreme that they name: The lengths sum to 16384; one sequence, at a place drawn from the seed, starts among the first device's tokens and ends among the last device's. `counts`: every block holds at most 64 routed tokens, and some block exactly 64. `chosen`: each block's 64 slots hold distinct offsets; its first counts slots are the routed tokens in rising order, the others are unused.
All inputs are finite; a program needn't handle non-finite values.
Results may differ from a plain program's by a relative error of at most 0.023.
Values may be sent and summed in bfloat16 or wider, within the bound.
No kernel may reach another device: no remote copies, remote signals or barrier semaphores. Data moves between devices by JAX's collectives and lax.ppermute only.
A program may use at most 256 MiB of HBM per device.

v0:
```python
import functools
import jax
import jax.numpy as jnp
from jax import lax
from jax.experimental import pallas as pl
from jax.experimental.pallas import tpu as pltpu
from jax.sharding import PartitionSpec as P

HEADS = 16
HEAD_DIM = 64
LANES = 128
BLOCK = 128

masked_score = -1e30
eps_norm = 1e-05
far_away = 1e9

f32 = jnp.float32
bf16 = jnp.bfloat16


def nt(left, right):
    return lax.dot_general(left, right, (((1,), (1,)), ((), ())), preferred_element_type=f32)


def nn(left, right):
    return lax.dot_general(left, right, (((1,), (0,)), ((), ())), preferred_element_type=f32)


def rms_scale(values, gain):
    return values * lax.rsqrt(jnp.mean(values * values, axis=-1, keepdims=True) + eps_norm) * gain


def three_parts(value):
    high = lax.reduce_precision(value, 8, 7)
    rest = value - high
    middle = lax.reduce_precision(rest, 8, 7)
    return jnp.stack([high, middle, rest - middle]).astype(bf16)


def spread_rows(packed, upper):
    lanes = lax.broadcasted_iota(jnp.int32, packed.shape, 1)
    zero = jnp.zeros_like(packed)
    rolled = jnp.concatenate([packed[:, HEAD_DIM:], packed[:, :HEAD_DIM]], axis=1)
    if upper:
        return jnp.concatenate(
            [jnp.where(lanes >= HEAD_DIM, rolled, zero), jnp.where(lanes >= HEAD_DIM, packed, zero)], axis=0
        )
    return jnp.concatenate(
        [jnp.where(lanes < HEAD_DIM, packed, zero), jnp.where(lanes < HEAD_DIM, rolled, zero)], axis=0
    )


def pack_columns(turned):
    return jnp.concatenate([turned[:, :BLOCK], turned[:, BLOCK:]], axis=0)


def key_columns(kpos_ref, member, extent):
    row = kpos_ref[member : member + 1, :extent]
    column = jnp.transpose(jnp.broadcast_to(row, (LANES, extent)))
    return jnp.concatenate([column, column], axis=1)


def attend_core(factor, load_query, load_kv, members, blocks, key_rows, kpos_ref, qpos_ref, qlow_ref, mixed_ref, turned_ref, lse_ref):
    kv_turned = [jnp.transpose(load_kv(m, key_rows)) for m in range(members)]
    for b in range(blocks):
        extent = key_rows * (b + 1) // blocks
        packed = (load_query(b).astype(f32) * factor).astype(bf16)
        wide = spread_rows(packed, False)
        qpos = qpos_ref[b : b + 1, :]
        qlow = qlow_ref[b : b + 1, :]
        scores = []
        for m in range(members):
            score = nt(load_kv(m, extent), wide)
            kpos = key_columns(kpos_ref, m, extent)
            score = jnp.where((kpos <= qpos) & (kpos >= qlow), score, masked_score)
            scores.append(score)
        peak = jnp.max(scores[0], axis=0, keepdims=True)
        for score in scores[1:]:
            peak = jnp.maximum(peak, jnp.max(score, axis=0, keepdims=True))
        peak = jnp.maximum(peak, 0.1 * masked_score)
        total = jnp.zeros_like(peak)
        mixed = jnp.zeros((LANES, 2 * BLOCK), f32)
        for m in range(members):
            prob = jnp.exp(scores[m] - peak)
            total = total + jnp.sum(prob, axis=0, keepdims=True)
            mixed = mixed + nn(kv_turned[m][:, :extent], prob.astype(bf16))
        safe = jnp.where(total > 0, total, 1.0)
        lse_ref[b : b + 1, :] = peak + jnp.log(safe)
        turned = pack_columns(mixed[HEAD_DIM:, :] / safe)
        turned_ref[b * BLOCK : (b + 1) * BLOCK, :] = turned
        mixed_ref[b * BLOCK : (b + 1) * BLOCK, :] = jnp.transpose(turned).astype(bf16)


def attend_back_core(
    factor, load_query, load_grad, load_kv, members, blocks, key_rows, kpos_ref, qpos_ref, qlow_ref, turned_ref, lse_ref,
    dq_ref, add_dkv,
):
    kv_turned = [jnp.transpose(load_kv(m, key_rows)) for m in range(members)]
    for b in range(blocks - 1, -1, -1):
        extent = key_rows * (b + 1) // blocks
        rows = slice(b * BLOCK, (b + 1) * BLOCK)
        packed = (load_query(b).astype(f32) * factor).astype(bf16)
        grads = load_grad(b)
        wide = jnp.concatenate([spread_rows(packed, False), spread_rows(grads, True)], axis=0)
        product = jnp.transpose(grads.astype(f32)) * turned_ref[rows, :]
        delta = jnp.concatenate(
            [
                jnp.sum(product[:HEAD_DIM], axis=0, keepdims=True),
                jnp.sum(product[HEAD_DIM:], axis=0, keepdims=True),
            ],
            axis=1,
        )
        qpos = qpos_ref[b : b + 1, :]
        qlow = qlow_ref[b : b + 1, :]
        lse = lse_ref[b : b + 1, :]
        dquery = jnp.zeros((LANES, 2 * BLOCK), f32)
        for m in range(members):
            both = nt(load_kv(m, extent), wide)
            kpos = key_columns(kpos_ref, m, extent)
            prob = jnp.exp(
                jnp.where((kpos <= qpos) & (kpos >= qlow), both[:, : 2 * BLOCK] - lse, masked_score)
            )
            dlogit = (prob * (both[:, 2 * BLOCK :] - delta)).astype(bf16)
            dquery = dquery + nn(kv_turned[m][:, :extent], dlogit)
            add_dkv(m, extent, b == blocks - 1, nn(jnp.concatenate([dlogit, prob.astype(bf16)], axis=1), wide))
        dq_ref[rows, :] = jnp.transpose(pack_columns(dquery[:HEAD_DIM, :] * factor)).astype(bf16)


def attend_kernel(factor, q_ref, kv_ref, kpos_ref, qpos_ref, qlow_ref, mixed_ref, turned_ref, lse_ref):
    members, key_rows, _ = kv_ref.shape
    attend_core(
        factor,
        lambda b: q_ref[b * BLOCK : (b + 1) * BLOCK, :],
        lambda m, extent: kv_ref[m, :extent, :],
        members, q_ref.shape[0] // BLOCK, key_rows, kpos_ref, qpos_ref, qlow_ref, mixed_ref, turned_ref, lse_ref,
    )


def attend_back_kernel(
    factor, q_ref, do_ref, kv_ref, kpos_ref, qpos_ref, qlow_ref, turned_ref, lse_ref, dq_ref, dkv_ref
):
    members, key_rows, _ = kv_ref.shape

    def add_dkv(m, extent, first, update):
        if first:
            dkv_ref[m, :extent, :] = update
        else:
            dkv_ref[m, :extent, :] += update

    attend_back_core(
        factor,
        lambda b: q_ref[b * BLOCK : (b + 1) * BLOCK, :],
        lambda b: do_ref[b * BLOCK : (b + 1) * BLOCK, :],
        lambda m, extent: kv_ref[m, :extent, :],
        members, q_ref.shape[0] // BLOCK, key_rows, kpos_ref, qpos_ref, qlow_ref, turned_ref, lse_ref, dq_ref, add_dkv,
    )


vmem = pl.BlockSpec(memory_space=pltpu.VMEM)
vmem_limit = 56 * 1024 * 1024


def attend(factor, queries, kv, kpos, qpos, qlow):
    rows = queries.shape[0]
    return pl.pallas_call(
        functools.partial(attend_kernel, factor),
        out_shape=(
            jax.ShapeDtypeStruct((rows, LANES), bf16),
            jax.ShapeDtypeStruct((rows, LANES), f32),
            jax.ShapeDtypeStruct(qpos.shape, f32),
        ),
        in_specs=[vmem] * 5,
        out_specs=(vmem,) * 3,
        compiler_params=pltpu.CompilerParams(vmem_limit_bytes=vmem_limit),
        name="attend",
    )(queries, kv, kpos, qpos, qlow)


def attend_back(factor, queries, dmixed, kv, kpos, qpos, qlow, turned, lse):
    rows = queries.shape[0]
    return pl.pallas_call(
        functools.partial(attend_back_kernel, factor),
        out_shape=(
            jax.ShapeDtypeStruct((rows, LANES), bf16),
            jax.ShapeDtypeStruct(kv.shape, f32),
        ),
        in_specs=[vmem] * 8,
        out_specs=(vmem,) * 2,
        compiler_params=pltpu.CompilerParams(vmem_limit_bytes=vmem_limit),
        name="attend_back",
    )(queries, dmixed, kv, kpos, qpos, qlow, turned, lse)


def general(
    tokens_in,
    w_router,
    gain_attn,
    w_query,
    w_key,
    w_value,
    w_out,
    gain_mlp,
    w_up,
    w_down,
    out_grad,
    lengths,
    counts,
    chosen,
):
    devices = lax.axis_size("seq")
    own = lax.axis_index("seq")
    capacity = chosen.shape[0] // devices
    tok_rows, width = tokens_in.shape
    hidden_width = w_up.shape[1]
    group = devices // HEADS
    share = capacity // group
    half = share // 2
    member = own % group
    slots = devices * capacity
    factor = HEAD_DIM ** (-0.5)
    attn_gain = gain_attn.astype(f32)
    mlp_gain = gain_mlp.astype(f32)

    def swap(value):
        return lax.all_to_all(value, "seq", split_axis=0, concat_axis=0, tiled=True)

    groups = [[h * group + m for m in range(group)] for h in range(HEADS)]

    def across_group(value):
        if group == 2:
            other = lax.ppermute(value, "seq", [(s, s ^ 1) for s in range(devices)])
            return jnp.stack([value, other])
        return lax.all_gather(value, "seq", axis_index_groups=groups)

    def sum_over_group(value):
        if group == 2:
            return value[0] + lax.ppermute(value[1], "seq", [(s, s ^ 1) for s in range(devices)])
        return lax.psum_scatter(value, "seq", scatter_dimension=0, axis_index_groups=groups)

    def member_order(value):
        if group == 2:
            return jnp.where(member == 0, value, value[::-1])
        return value

    slot_ids = jnp.arange(capacity, dtype=jnp.int32)
    places = jnp.arange(devices, dtype=jnp.int32)[:, None] * tok_rows + chosen.reshape(devices, capacity)
    live_all = slot_ids[None, :] < counts[:, None]
    seq_ends = jnp.cumsum(lengths)
    starts = jnp.max(jnp.where(places[..., None] >= seq_ends, seq_ends, 0), axis=-1)
    kpos = jnp.where(live_all, places.astype(f32), far_away)
    kpos = member_order(kpos.reshape(devices, group, share).swapaxes(0, 1).reshape(group, devices * share))
    blocks = devices * half // BLOCK

    def query_order(value):
        value = lax.dynamic_index_in_dim(value.reshape(devices, group, share), member, 1, False)
        return value.reshape(blocks, devices // blocks, 2, half).swapaxes(1, 2).reshape(blocks, 2 * BLOCK)

    qpos = query_order(jnp.where(live_all, places, -1).astype(f32))
    qlow = query_order(starts.astype(f32))

    offsets = lax.dynamic_slice_in_dim(chosen, own * capacity, capacity)
    live = slot_ids < counts[own]
    pick = (offsets[:, None] == jnp.arange(tok_rows, dtype=jnp.int32)[None, :]).astype(bf16)
    routed = nn(pick, tokens_in)
    upstream = jnp.where(live[:, None], nn(pick, out_grad), 0.0)
    gate = jax.nn.sigmoid(jnp.sum(routed * w_router.astype(f32)[None, :], axis=1))
    gate_sum = jnp.sum(jnp.where(live, gate, 0.0))
    normed = rms_scale(routed, attn_gain).astype(bf16)
    normed_all = lax.all_gather(normed, "seq", axis=0, tiled=True)
    queries = nn(normed, w_query).astype(bf16)
    keys = nn(normed, w_key).astype(bf16)
    values = nn(normed, w_value).astype(bf16)

    def note(value):
        parts = jnp.pad(three_parts(value), (0, LANES - 3))
        return jnp.broadcast_to(parts, (devices, 8, LANES))

    def read_note(rows):
        return jnp.sum(rows[:, 0, :3].astype(f32))

    def to_heads(value, per_row):
        if per_row == 2:
            value = value.reshape(group, 2, half, HEADS, HEAD_DIM).transpose(3, 0, 2, 1, 4)
            return value.reshape(devices, half, LANES)
        return value

    def pair_to_heads(first, second):
        both = jnp.stack([first, second], axis=1).reshape(group, share, 2, HEADS, HEAD_DIM)
        return both.transpose(3, 0, 1, 2, 4).reshape(devices, share, LANES)

    def from_heads(value):
        value = value.reshape(HEADS, group, half, 2, HEAD_DIM).transpose(1, 3, 2, 0, 4)
        return value.reshape(capacity, HEADS * HEAD_DIM)

    def pair_from_heads(value):
        value = value.reshape(HEADS, group, share, 2, HEAD_DIM).transpose(3, 1, 2, 0, 4)
        value = value.reshape(2, capacity, HEADS * HEAD_DIM)
        return value[0], value[1]

    sent = jnp.concatenate([to_heads(queries, 2), pair_to_heads(keys, values), note(gate_sum)], axis=1)
    got = swap(sent)
    score_total = read_note(got[:, half + share :])
    chosen_total = jnp.sum(counts).astype(f32)
    ratio = chosen_total / score_total
    scaling = gate * ratio
    head_queries = got[:, :half].reshape(devices * half, LANES)
    kv = across_group(got[:, half : half + share].reshape(devices * share, LANES))
    mixed_packed, mixed_turned, lse = attend(factor, head_queries, kv, kpos, qpos, qlow)
    mixed = from_heads(swap(mixed_packed.reshape(devices, half, LANES)))

    attn_out = nn(mixed, w_out)
    middle = routed + attn_out
    normed_mlp = rms_scale(middle, mlp_gain).astype(bf16)
    dbranch = scaling[:, None] * upstream
    dmlp = dbranch.astype(bf16)
    gathered = lax.all_gather(
        jnp.concatenate([mixed, normed_mlp, dmlp], axis=1), "seq", axis=0, tiled=True
    )
    mixed_all = gathered[:, :width]
    normed_mlp_all = gathered[:, width : 2 * width]
    dmlp_all = gathered[:, 2 * width :]
    hidden = nn(normed_mlp, w_up)
    active = jax.nn.gelu(hidden, approximate=True).astype(bf16)
    branch = attn_out + nn(active, w_down)
    dweight = jnp.sum(upstream * branch, axis=1)

    def gelu_of(values):
        return jax.nn.gelu(values, approximate=True)

    dactive = nt(dmlp, w_down)
    dhidden = jax.vjp(gelu_of, hidden)[1](dactive)[0].astype(bf16)
    dnormed_mlp = nt(dhidden, w_up)
    dmiddle = jax.vjp(lambda v: rms_scale(v, mlp_gain), middle)[1](dnormed_mlp)[0]
    dattn = (dbranch + dmiddle).astype(bf16)
    dmixed = nt(dattn, w_out).astype(bf16)
    out_cols = width // devices
    dattn_split = dattn.reshape(capacity, devices, out_cols).swapaxes(0, 1)
    dattn_split = dattn_split.reshape(devices, capacity * out_cols // LANES, LANES)
    got = swap(
        jnp.concatenate(
            [to_heads(dmixed, 2), dattn_split, note(jnp.sum(jnp.where(live, dweight * gate, 0.0)))], axis=1
        )
    )
    dattn_own = got[:, half : half + capacity * out_cols // LANES].reshape(slots, out_cols)
    coefficient = read_note(got[:, half + capacity * out_cols // LANES :])
    dq_packed, dkv_parts = attend_back(
        factor,
        head_queries,
        got[:, :half].reshape(devices * half, LANES),
        kv,
        kpos,
        qpos,
        qlow,
        mixed_turned,
        lse,
    )
    dkv = sum_over_group(dkv_parts).astype(bf16)

    dscore = dweight * ratio - coefficient * chosen_total / (score_total * score_total)
    dlogit_router = jnp.where(live, dscore * gate * (1.0 - gate), 0.0)
    router_part = jnp.sum(dlogit_router[:, None] * routed, axis=0).reshape(devices, out_cols)
    router_parts = three_parts(router_part).swapaxes(0, 1).reshape(devices, 1, 3 * out_cols)
    router_note = jnp.pad(router_parts, ((0, 0), (0, 7), (0, LANES - 3 * out_cols)))
    got = swap(
        jnp.concatenate(
            [dq_packed.reshape(devices, half, LANES), dkv.reshape(devices, share, LANES), router_note], axis=1
        )
    )
    dquery = from_heads(got[:, :half])
    dkey, dvalue = pair_from_heads(got[:, half : half + share])
    grad_router = jnp.sum(got[:, half + share, : 3 * out_cols].astype(f32), axis=0)
    grad_router = jnp.sum(grad_router.reshape(3, out_cols), axis=0)

    normed_own = lax.dynamic_index_in_dim(normed_all.reshape(devices, group, share, width), member, 1, False)
    normed_own = normed_own.reshape(devices * share, width)
    dq_rows = dq_packed.reshape(devices, half, 2, HEAD_DIM).swapaxes(1, 2).reshape(devices * share, HEAD_DIM)
    dqkv = jnp.concatenate([dq_rows, dkv], axis=1)
    grad_qkv = lax.dot_general(normed_own, dqkv, (((0,), (0,)), ((), ())), preferred_element_type=f32)
    head_cols = 3 * HEAD_DIM // group
    grad_qkv = member_order(grad_qkv.reshape(width, group, head_cols).swapaxes(0, 1))
    grad_qkv = sum_over_group(grad_qkv).astype(bf16)
    grad_out = lax.dot_general(mixed_all, dattn_own, (((0,), (0,)), ((), ())), preferred_element_type=f32)

    hidden_cols = hidden_width // devices
    up_own = lax.dynamic_slice_in_dim(w_up, own * hidden_cols, hidden_cols, 1)
    down_own = lax.dynamic_slice_in_dim(w_down, own * hidden_cols, hidden_cols, 0)
    hidden_own = nn(normed_mlp_all, up_own)
    dactive_own = nt(dmlp_all, down_own)
    active_own, gelu_back = jax.vjp(gelu_of, hidden_own)
    dhidden_own = gelu_back(dactive_own)[0].astype(bf16)
    active_own = active_own.astype(bf16)
    grad_down = lax.dot_general(active_own, dmlp_all, (((0,), (0,)), ((), ())), preferred_element_type=f32)
    grad_up = lax.dot_general(
        normed_mlp_all, dhidden_own, (((0,), (0,)), ((), ())), preferred_element_type=f32
    )
    sent = jnp.concatenate([grad_up.astype(bf16), grad_qkv, grad_out.astype(bf16)], axis=1)
    got = swap(sent.reshape(devices, out_cols, sent.shape[1])).astype(f32)
    grad_up = got[:, :, :hidden_cols].swapaxes(0, 1).reshape(out_cols, hidden_width)
    grad_qkv = got[:, :, hidden_cols : hidden_cols + head_cols].reshape(HEADS, group, out_cols, head_cols)
    grad_qkv = grad_qkv.transpose(2, 0, 1, 3).reshape(out_cols, HEADS, 3, HEAD_DIM)
    grad_query = grad_qkv[:, :, 0].reshape(out_cols, width)
    grad_key = grad_qkv[:, :, 1].reshape(out_cols, width)
    grad_value = grad_qkv[:, :, 2].reshape(out_cols, width)
    grad_out = got[:, :, hidden_cols + head_cols :].swapaxes(0, 1).reshape(out_cols, width)

    def own_rows(value):
        return lax.dynamic_slice_in_dim(value, own * out_cols, out_cols, 0).astype(f32)

    grad_gain_attn = jnp.sum(
        own_rows(w_query) * grad_query + own_rows(w_key) * grad_key + own_rows(w_value) * grad_value, axis=1
    ) / own_rows(attn_gain)
    grad_gain_mlp = jnp.sum(own_rows(w_up) * grad_up, axis=1) / own_rows(mlp_gain)

    dnormed = nt(dquery, w_query) + nt(dkey, w_key) + nt(dvalue, w_value)
    drows = jax.vjp(lambda v: rms_scale(v, attn_gain), routed)[1](dnormed)[0]
    droutes = drows + dmiddle + dlogit_router[:, None] * w_router.astype(f32)[None, :]
    new_rows = (routed + scaling[:, None] * branch).astype(bf16)
    new_grads = (upstream + droutes).astype(bf16)
    put = (jnp.arange(tok_rows, dtype=jnp.int32)[:, None] == offsets[None, :]) & live[None, :]
    hit = jnp.any(put, axis=1, keepdims=True)
    put = put.astype(bf16)
    output = jnp.where(hit, nn(put, new_rows).astype(bf16), tokens_in)
    input_grad = jnp.where(hit, nn(put, new_grads).astype(bf16), out_grad)
    return (
        output,
        input_grad,
        grad_router,
        grad_gain_attn,
        grad_query,
        grad_key,
        grad_value,
        grad_out,
        grad_gain_mlp,
        grad_up,
        grad_down,
    )


SHARE = 64
HALF = 32
NOTE = 8
OUT_HALF = 16
OUT_ROWS = 32
TILES = 2
AT_OUT = TILES * OUT_ROWS
AT_QUERY = AT_OUT + OUT_HALF
AT_PAIR = AT_QUERY + OUT_HALF
AT_NOTE = AT_PAIR + OUT_ROWS
GRAD_ROWS = AT_NOTE + NOTE


def swapped(tile):
    return jnp.concatenate([tile[..., HEAD_DIM:], tile[..., :HEAD_DIM]], axis=-1)


def joined(left, right):
    return jnp.concatenate([left[..., :HEAD_DIM], right[..., HEAD_DIM:]], axis=-1)


def pack_rows(target, first, value):
    for pair in range(HEADS // 2):
        tile = value[:, pair * LANES : (pair + 1) * LANES]
        turned = swapped(tile)
        target[2 * pair, first : first + HALF, :] = joined(tile[:HALF], turned[HALF:])
        target[2 * pair + 1, first : first + HALF, :] = joined(turned[:HALF], tile[HALF:])


def pack_pairs(target, first, left, right):
    for pair in range(HEADS // 2):
        lanes = slice(pair * LANES, (pair + 1) * LANES)
        one, two = left[:, lanes], right[:, lanes]
        target[2 * pair, first : first + SHARE, :] = joined(one, swapped(two))
        target[2 * pair + 1, first : first + SHARE, :] = joined(swapped(one), two)


def unpack_rows(source, first, half):
    columns = []
    for pair in range(HEADS // 2):
        even = source[2 * pair, first : first + half, :]
        odd = source[2 * pair + 1, first : first + half, :]
        columns.append(jnp.concatenate([joined(even, swapped(odd)), joined(swapped(even), odd)], axis=0))
    return jnp.concatenate(columns, axis=1)


def unpack_pairs(source, first, rows):
    left, right = [], []
    for pair in range(HEADS // 2):
        even = source[2 * pair, first : first + rows, :]
        odd = source[2 * pair + 1, first : first + rows, :]
        left.append(joined(even, swapped(odd)))
        right.append(joined(swapped(even), odd))
    return jnp.concatenate(left, axis=1), jnp.concatenate(right, axis=1)


def in_parts(value):
    high = value.astype(bf16).astype(f32)
    rest = value - high
    middle = rest.astype(bf16).astype(f32)
    row = lax.broadcasted_iota(jnp.int32, value.shape, len(value.shape) - 2)
    parts = jnp.where(row == 0, high, jnp.where(row == 1, middle, jnp.where(row == 2, rest - middle, 0.0)))
    return parts.astype(bf16)


def write_note(target, first, value):
    rows = in_parts(jnp.broadcast_to(value, (NOTE, LANES)))
    for k in range(target.shape[0]):
        target[k, first : first + NOTE, :] = rows


def read_note(source, first):
    rows = source[:, first : first + NOTE, :].astype(f32)
    return jnp.sum(jnp.sum(rows, axis=0), axis=0, keepdims=True)[:, :1]


def one_hot(own_ref, counts_ref, chosen_ref, tok_rows, live_only):
    offsets = chosen_ref[pl.ds(own_ref[0], 1), :]
    capacity = offsets.shape[1]
    rows = lax.broadcasted_iota(jnp.int32, (tok_rows, capacity), 0)
    hot = rows == offsets
    if live_only:
        slot = lax.broadcasted_iota(jnp.int32, (tok_rows, capacity), 1)
        hot = hot & (slot < counts_ref[own_ref[0]])
    return jnp.where(hot, 1.0, 0.0)


def live_column(own_ref, counts_ref, capacity):
    return lax.broadcasted_iota(jnp.int32, (capacity, 1), 0) < counts_ref[own_ref[0]]


def gate_of(rows, vectors_ref):
    return jax.nn.sigmoid(jnp.sum(rows * vectors_ref[0:1, :], axis=1, keepdims=True))


def inverse_rms(values):
    return lax.rsqrt(jnp.mean(values * values, axis=-1, keepdims=True) + eps_norm)


def total_count(counts_ref):
    return lax.fori_loop(0, counts_ref.shape[0], lambda i, s: s + counts_ref[i], 0).astype(f32)


def gelu_pair(u):
    c = 0.7978845608028654
    square = u * u
    t = jnp.tanh(c * (u + 0.044715 * (square * u)))
    value = 0.5 * u * (1.0 + t)
    slope = 0.5 * (1.0 + t) + (0.5 * u) * ((1.0 - t * t) * (c + (3.0 * 0.044715 * c) * square))
    return value, slope


def chip_of(own_ref, k):
    return jnp.bitwise_xor(own_ref[0] // 2, (k // 4) ^ (4 * (k % 4)))


def row_of(column):
    wide = jnp.broadcast_to(column, (column.shape[0], LANES))
    filled = jnp.concatenate([wide, jnp.zeros((LANES - column.shape[0], LANES), f32)], axis=0)
    return jnp.transpose(filled)[:1, : column.shape[0]]


def fetch_kernel(own_ref, counts_ref, chosen_ref, tokens_ref, grads_ref, both_ref):
    hot = one_hot(own_ref, counts_ref, chosen_ref, tokens_ref.shape[0], False)
    capacity = hot.shape[1]
    pick = jnp.transpose(jnp.concatenate([hot, jnp.zeros_like(hot)], axis=1))[:capacity].astype(bf16)
    live = live_column(own_ref, counts_ref, capacity)
    both_ref[0, :capacity, :] = nn(pick, tokens_ref[...]).astype(bf16)
    both_ref[0, capacity:, :] = jnp.where(live, nn(pick, grads_ref[...]), 0.0).astype(bf16)


def prepare_kernel(own_ref, counts_ref, both_ref, vectors_ref, wq_ref, wk_ref, wv_ref, sent_ref, wq, wk, wv, sems):
    copies = [
        pltpu.make_async_copy(source, target, sems.at[i])
        for i, (source, target) in enumerate(((wq_ref, wq), (wk_ref, wk), (wv_ref, wv)))
    ]
    for copy in copies:
        copy.start()
    capacity = both_ref.shape[1] // 2
    rows = both_ref[0, :capacity, :].astype(f32)
    live = live_column(own_ref, counts_ref, capacity)
    gate_sum = jnp.sum(jnp.where(live, gate_of(rows, vectors_ref), 0.0), axis=0, keepdims=True)
    write_note(sent_ref, HALF + SHARE, gate_sum)
    normed = (rows * inverse_rms(rows) * vectors_ref[1:2, :]).astype(bf16)
    copies[0].wait()
    pack_rows(sent_ref, 0, nn(normed, wq[...]).astype(bf16))
    copies[1].wait()
    keys = nn(normed, wk[...]).astype(bf16)
    copies[2].wait()
    pack_pairs(sent_ref, HALF, keys, nn(normed, wv[...]).astype(bf16))


def unpack_kernel(got_ref, mixed_ref):
    mixed_ref[0] = unpack_rows(got_ref, 0, HALF)


CHUNKS = 4
PIECES = 1


def middle_kernel(
    own_ref, counts_ref, mixed_ref, total_ref, both_ref, vectors_ref, out_ref, up_ref, down_ref,
    sent_ref, new_ref, dmiddle_ref, dweight_ref, w_out, w_up, w_down, hidden_ref, active_ref, sems,
):
    width, total_cols = up_ref.shape
    cols = total_cols // CHUNKS
    copies = [pltpu.make_async_copy(out_ref, w_out, sems.at[0])]
    for c in range(CHUNKS):
        part = pl.ds(c * cols, cols)
        copies.append(pltpu.make_async_copy(up_ref.at[:, part], w_up.at[:, part], sems.at[1 + c]))
    for c in range(CHUNKS):
        part = pl.ds(c * cols, cols)
        copies.append(pltpu.make_async_copy(down_ref.at[part, :], w_down.at[part, :], sems.at[1 + CHUNKS + c]))
    for copy in copies:
        copy.start()
    capacity = mixed_ref.shape[1]
    rows = both_ref[0, :capacity, :].astype(f32)
    upstream = both_ref[0, capacity:, :].astype(f32)
    live = live_column(own_ref, counts_ref, capacity)
    gate = gate_of(rows, vectors_ref)
    ratio = total_count(counts_ref) / total_ref[:1, :1]
    scaling = gate * ratio
    gain = vectors_ref[2:3, :]
    dbranch = scaling * upstream
    dmlp = dbranch.astype(bf16)
    copies[0].wait()
    attn_out = nn(mixed_ref[0], w_out[...])
    middle = rows + attn_out
    scale = inverse_rms(middle)
    normed = (middle * scale * gain).astype(bf16)
    for c in range(CHUNKS):
        copies[1 + c].wait()
        hidden_ref[:, c * cols : (c + 1) * cols] = nn(normed, w_up[:, c * cols : (c + 1) * cols])
    dnormed = jnp.zeros((capacity, width), f32)
    for c in range(CHUNKS):
        part = slice(c * cols, (c + 1) * cols)
        copies[1 + CHUNKS + c].wait()
        hidden = hidden_ref[:, part]
        value, slope = gelu_pair(hidden)
        active_ref[:, part] = value.astype(bf16)
        dhidden = (nt(dmlp, w_down[part, :]) * slope).astype(bf16)
        dnormed = dnormed + nt(dhidden, w_up[:, part])
    branch = attn_out + nn(active_ref[...], w_down[...])
    new_ref[...] = (rows + scaling * branch).astype(bf16)
    dweight = jnp.sum(upstream * branch, axis=1, keepdims=True)
    dweight_ref[...] = jnp.broadcast_to(dweight, dweight_ref.shape)
    scaled = gain * dnormed
    dmiddle = scale * scaled - middle * (scale * scale * scale) * jnp.mean(scaled * middle, axis=-1, keepdims=True)
    dmiddle_ref[...] = dmiddle
    dattn = (dbranch + dmiddle).astype(bf16)
    pack_rows(sent_ref, 0, nt(dattn, w_out[...]).astype(bf16))
    pack_rows(sent_ref, HALF, dattn)
    write_note(sent_ref, 2 * HALF, jnp.sum(jnp.where(live, dweight * gate, 0.0), axis=0, keepdims=True))


def put_kernel(own_ref, counts_ref, chosen_ref, old_ref, new_ref, result_ref):
    put_rows(own_ref, counts_ref, chosen_ref, old_ref, new_ref[...], result_ref)


def put_rows(own_ref, counts_ref, chosen_ref, old_ref, new, result_ref):
    hot = one_hot(own_ref, counts_ref, chosen_ref, old_ref.shape[0], True)
    hit = jnp.sum(hot, axis=1, keepdims=True) > 0.5
    placed = nn(hot.astype(bf16), new)
    result_ref[...] = jnp.where(hit, placed, old_ref[...].astype(f32)).astype(bf16)


def router_slope(own_ref, counts_ref, rows, dweight_ref, total_ref, coef_ref, vectors_ref):
    gate = gate_of(rows, vectors_ref)
    live = live_column(own_ref, counts_ref, rows.shape[0])
    count = total_count(counts_ref)
    total = total_ref[:1, :1]
    dscore = dweight_ref[:, :1] * (count / total) - coef_ref[:1, :1] * count / (total * total)
    return jnp.where(live, dscore * gate * (1.0 - gate), 0.0)


def keys_kernel(dq_ref, dkv_ref, moved_ref, coef_ref, sent_ref, sum_ref):
    rows = dkv_ref.shape[0]
    sent_ref[:, :HALF, :] = dq_ref[...]
    dkv = dkv_ref[...] + moved_ref[:rows, :]
    sent_ref[:, HALF:, :] = dkv.astype(bf16).reshape(sent_ref.shape[0], SHARE, LANES)
    sum_ref[...] = coef_ref[...] + moved_ref[rows:, :]


def units_kernel(
    own_ref, counts_ref, got_ref, dqkv_ref, total_ref, coef_ref, vectors_ref, rows_ref, dweight_ref,
    out_ref, up_ref, down_ref, *rest,
):
    boths, mixeds, rest = rest[:PIECES], rest[PIECES : PIECES + 4], rest[PIECES + 4 :]
    down_keep_ref, down_give_ref, keep_ref, give_ref, rest = *rest[:4], rest[4:]
    both, mixed_slots, grad_up, grad_down, grad_out, grad_q, grad_kv, ratio_ref, both_sems, mixed_sems = rest
    step = pl.program_id(0)
    steps = pl.num_programs(0)
    _, sources, twice, width = both.shape
    capacity = twice // 2
    core = own_ref[0] % 2
    slot = step % 2

    def both_copies(k, at):
        if PIECES == 4:
            return [pltpu.make_async_copy(boths[k], both.at[at], both_sems.at[at, 0])]
        return [
            pltpu.make_async_copy(boths[0].at[chip_of(own_ref, 4 * k + j)], both.at[at, j], both_sems.at[at, j])
            for j in range(4)
        ]

    def copies(k):
        return both_copies(k, k % 2) + [
            pltpu.make_async_copy(mixeds[k], mixed_slots.at[k % 2], mixed_sems.at[k % 2])
        ]

    for k in range(4):

        @pl.when(step == max(k - 1, 0))
        def _(k=k):
            for copy in copies(k):
                copy.start()

    @pl.when(step == 0)
    def _():
        for ref in (grad_up, grad_down, grad_out, grad_q, grad_kv):
            ref[...] = jnp.zeros_like(ref)
        ratio_ref[...] = jnp.broadcast_to(total_count(counts_ref) / total_ref[:1, :1], ratio_ref.shape)

    for k in range(4):

        @pl.when(step == k)
        def _(k=k):
            for copy in copies(k):
                copy.wait()

    def halves(ref, first):
        blocks = [ref[chip_of(own_ref, 4 * step + j), first : first + HALF, :] for j in range(sources)]
        turned = jnp.transpose(jnp.concatenate(blocks, axis=0).astype(f32)).astype(bf16)
        return turned[:HEAD_DIM], turned[HEAD_DIM:]

    def low_high(value):
        value = value.reshape(sources, capacity, width)
        return value[:, :HALF, :].reshape(sources * HALF, width), value[:, HALF:, :].reshape(sources * HALF, width)

    rows = both[slot, :, :capacity, :].reshape(sources * capacity, width).astype(f32)
    upstream = both[slot, :, capacity:, :].reshape(sources * capacity, width).astype(f32)
    mixed = mixed_slots[slot].reshape(sources * capacity, width)
    normed_attn = (rows * inverse_rms(rows) * vectors_ref[1:2, :]).astype(bf16)
    low_query, high_query = halves(dqkv_ref, 0)
    low_rows, high_rows = low_high(normed_attn)
    grad_q[...] += nn(low_query, low_rows) + nn(high_query, high_rows)
    blocks = [dqkv_ref[chip_of(own_ref, 4 * step + j), HALF:, :] for j in range(sources)]
    pairs_turned = jnp.transpose(jnp.concatenate(blocks, axis=0).astype(f32)).astype(bf16)
    grad_kv[...] += nn(pairs_turned, normed_attn)
    low_attn, high_attn = halves(got_ref, HALF)
    low_mixed, high_mixed = low_high(mixed)
    grad_out[...] += nn(low_attn, low_mixed) + nn(high_attn, high_mixed)
    middle = rows + nn(mixed, out_ref[...])
    normed = (middle * inverse_rms(middle) * vectors_ref[2:3, :]).astype(bf16)
    dmlp = (gate_of(rows, vectors_ref) * ratio_ref[:1, :1] * upstream).astype(bf16)
    value, slope = gelu_pair(nn(normed, up_ref[...]))
    dhidden = nt(dmlp, down_ref[...]) * slope
    grad_down[...] += nn(jnp.transpose(value).astype(bf16), dmlp)
    grad_up[...] += nn(jnp.transpose(dhidden).astype(bf16), normed)

    @pl.when(step == steps - 1)
    def _():
        chips = keep_ref.shape[0]

        def split(value):
            value = value.reshape(chips, 2, OUT_ROWS, LANES)
            even, odd = value[:, 0], value[:, 1]
            return jnp.where(core == 0, even, odd), jnp.where(core == 0, odd, even)

        def store(first, kept, given):
            keep_ref[:, first : first + kept.shape[1], :] = kept
            give_ref[:, first : first + kept.shape[1], :] = given.astype(bf16)

        for t in range(TILES):
            store(t * OUT_ROWS, *split(jnp.transpose(grad_up[t * LANES : (t + 1) * LANES, :])))

        def two_in_one(value):
            return joined(value[:, :OUT_HALF], swapped(value[:, OUT_HALF:]))

        both_turned = jnp.transpose(jnp.concatenate([grad_out[...], grad_q[...]], axis=0))
        kept, given = split(both_turned)
        store(AT_OUT, two_in_one(kept), two_in_one(given))
        store(AT_QUERY, two_in_one(swapped(kept)), two_in_one(swapped(given)))
        store(AT_PAIR, *split(jnp.transpose(grad_kv[...])))
        own_rows = rows_ref[0, :capacity, :].astype(f32)
        dlogit = router_slope(own_ref, counts_ref, own_rows, dweight_ref, total_ref, coef_ref, vectors_ref)
        part = jnp.broadcast_to(jnp.sum(dlogit * own_rows, axis=0, keepdims=True), (NOTE, width))
        per_tile = LANES // OUT_ROWS
        for c in range(chips):
            tile = part[:, (2 * c) // per_tile * LANES : ((2 * c) // per_tile + 1) * LANES]
            shift = (2 * c) % per_tile * OUT_ROWS
            if shift:
                tile = jnp.concatenate([tile[:, shift:], tile[:, :shift]], axis=1)
            after = jnp.concatenate([tile[:, OUT_ROWS:], tile[:, :OUT_ROWS]], axis=1)
            keep_ref[c, AT_NOTE:, :] = jnp.where(core == 0, tile, after)
            give_ref[c, AT_NOTE:, :] = in_parts(jnp.where(core == 0, after, tile))
        down = grad_down[...]
        half = down.shape[0] // 2
        down_keep_ref[...] = jnp.where(core == 0, down[:half], down[half:])
        down_give_ref[...] = jnp.where(core == 0, down[half:], down[:half]).astype(bf16)


def merge_kernel(keep_ref, moved_ref, down_keep_ref, down_moved_ref, sent_ref, down_ref):
    sent_ref[:, :AT_NOTE, :] = (keep_ref[:, :AT_NOTE, :] + moved_ref[:, :AT_NOTE, :].astype(f32)).astype(bf16)
    note = keep_ref[:, AT_NOTE:, :] + jnp.sum(moved_ref[:, AT_NOTE:, :].astype(f32), axis=1, keepdims=True)
    sent_ref[:, AT_NOTE:, :] = in_parts(note)
    down_ref[...] = down_keep_ref[...] + down_moved_ref[...].astype(f32)


def rows_kernel(
    own_ref, counts_ref, chosen_ref, got_ref, both_ref, dmiddle_ref, dweight_ref, total_ref, coef_ref, vectors_ref,
    old_ref, wq_ref, wk_ref, wv_ref, grads_ref, wq, wk, wv, sems,
):
    copies = [
        pltpu.make_async_copy(source, target, sems.at[i])
        for i, (source, target) in enumerate(((wq_ref, wq), (wk_ref, wk), (wv_ref, wv)))
    ]
    for copy in copies:
        copy.start()
    capacity = dmiddle_ref.shape[0]
    rows = both_ref[0, :capacity, :].astype(f32)
    upstream = both_ref[0, capacity:, :].astype(f32)
    gain = vectors_ref[1:2, :]
    dlogit = router_slope(own_ref, counts_ref, rows, dweight_ref, total_ref, coef_ref, vectors_ref)
    partial = upstream + dmiddle_ref[...] + dlogit * vectors_ref[0:1, :]
    dquery = unpack_rows(got_ref, 0, HALF)
    dkey, dvalue = unpack_pairs(got_ref, HALF, SHARE)
    copies[0].wait()
    dnormed = jnp.zeros_like(partial) + nt(dquery, wq[...])
    copies[1].wait()
    dnormed = dnormed + nt(dkey, wk[...])
    copies[2].wait()
    dnormed = dnormed + nt(dvalue, wv[...])
    scale = inverse_rms(rows)
    scaled = gain * dnormed
    drows = scale * scaled - rows * (scale * scale * scale) * jnp.mean(scaled * rows, axis=-1, keepdims=True)
    put_rows(own_ref, counts_ref, chosen_ref, old_ref, (partial + drows).astype(bf16), grads_ref)


def finish_kernel(
    own_ref, got_ref, own_gain_ref, up_ref, wq_ref, wk_ref, wv_ref,
    grad_up_ref, grad_out_ref, grad_q_ref, grad_k_ref, grad_v_ref, router_ref, gain_attn_ref, gain_mlp_ref,
):
    total = jnp.zeros((OUT_ROWS, LANES), f32)
    for c in range(got_ref.shape[0]):
        for t in range(TILES):
            lanes = slice((TILES * c + t) * LANES, (TILES * c + t + 1) * LANES)
            part = got_ref[c, t * OUT_ROWS : (t + 1) * OUT_ROWS, :].astype(f32)
            grad_up_ref[:, lanes] = part
            total = total + part * up_ref[:, lanes].astype(f32)
    gain_mlp_ref[...] = row_of(jnp.sum(total, axis=1, keepdims=True)) / own_gain_ref[2:3, :]
    grad_out_ref[...] = unpack_rows(got_ref, AT_OUT, OUT_HALF).astype(f32)
    grad_q = unpack_rows(got_ref, AT_QUERY, OUT_HALF).astype(f32)
    grad_k, grad_v = (value.astype(f32) for value in unpack_pairs(got_ref, AT_PAIR, OUT_ROWS))
    grad_q_ref[...] = grad_q
    grad_k_ref[...] = grad_k
    grad_v_ref[...] = grad_v
    products = wq_ref[...].astype(f32) * grad_q + wk_ref[...].astype(f32) * grad_k + wv_ref[...].astype(f32) * grad_v
    gain_attn_ref[...] = row_of(jnp.sum(products, axis=1, keepdims=True)) / own_gain_ref[1:2, :]
    notes = jnp.sum(got_ref[:, AT_NOTE:, :].astype(f32), axis=0)
    router_ref[...] = jnp.sum(notes, axis=0, keepdims=True)[:, :OUT_ROWS]


def pair_attend_kernel(factor, got_ref, other_ref, kpos_ref, qpos_ref, qlow_ref, mixed_ref, turned_ref, lse_ref, total_ref):
    lists = (got_ref, other_ref)
    chips = got_ref.shape[0]
    blocks = chips * HALF // BLOCK
    sources = chips // blocks
    total = read_note(got_ref, HALF + SHARE) + read_note(other_ref, HALF + SHARE)
    total_ref[...] = jnp.broadcast_to(total, total_ref.shape)
    attend_core(
        factor,
        lambda b: got_ref[b * sources : (b + 1) * sources, :HALF, :].reshape(BLOCK, LANES),
        lambda m, extent: lists[m][: extent // SHARE, HALF : HALF + SHARE, :].reshape(extent, LANES),
        2, blocks, chips * SHARE, kpos_ref, qpos_ref, qlow_ref, mixed_ref, turned_ref, lse_ref,
    )


def pair_attend_back_kernel(
    factor, got_ref, other_ref, grad_ref, kpos_ref, qpos_ref, qlow_ref, turned_ref, lse_ref,
    dq_ref, own_ref, moved_ref, coef_ref,
):
    lists = (got_ref, other_ref)
    sums = (own_ref, moved_ref)
    chips = got_ref.shape[0]
    blocks = chips * HALF // BLOCK
    sources = chips // blocks
    coef = jnp.broadcast_to(read_note(grad_ref, 2 * HALF), coef_ref.shape)
    coef_ref[...] = coef
    moved_ref[chips * SHARE :, :] = coef

    def add_dkv(m, extent, first, update):
        if first:
            sums[m][:extent, :] = update
        else:
            sums[m][:extent, :] += update

    attend_back_core(
        factor,
        lambda b: got_ref[b * sources : (b + 1) * sources, :HALF, :].reshape(BLOCK, LANES),
        lambda b: grad_ref[b * sources : (b + 1) * sources, :HALF, :].reshape(BLOCK, LANES),
        lambda m, extent: lists[m][: extent // SHARE, HALF : HALF + SHARE, :].reshape(extent, LANES),
        2, blocks, chips * SHARE, kpos_ref, qpos_ref, qlow_ref, turned_ref, lse_ref, dq_ref, add_dkv,
    )


smem = pl.BlockSpec(memory_space=pltpu.SMEM)
hbm = pl.BlockSpec(memory_space=pl.ANY)
params = pltpu.CompilerParams(vmem_limit_bytes=vmem_limit)


def shaped(shape, dtype):
    return jax.ShapeDtypeStruct(shape, dtype)


def call(kernel, name, in_specs, out_shape, arguments, scratch=()):
    return pl.pallas_call(
        kernel,
        out_shape=out_shape,
        in_specs=in_specs,
        out_specs=jax.tree.map(lambda _: vmem, out_shape),
        scratch_shapes=list(scratch),
        compiler_params=params,
        name=name,
    )(*arguments)


def pairs(
    tokens_in,
    w_router,
    gain_attn,
    w_query,
    w_key,
    w_value,
    w_out,
    gain_mlp,
    w_up,
    w_down,
    out_grad,
    lengths,
    counts,
    chosen,
):
    devices = lax.axis_size("seq")
    chips = devices // 2
    own = lax.axis_index("seq")
    capacity = chosen.shape[0] // devices
    tok_rows, width = tokens_in.shape
    hidden_width = w_up.shape[1]
    out_rows = width // devices
    factor = HEAD_DIM ** (-0.5)
    core = own % 2
    own_id = own.astype(jnp.int32).reshape(1)
    chosen = chosen.reshape(devices, capacity)
    vectors = jnp.stack([w_router, gain_attn, gain_mlp]).astype(f32)
    own_gains = lax.dynamic_slice_in_dim(vectors, own * out_rows, out_rows, 1)
    cores = [[2 * c + k for c in range(chips)] for k in range(2)]

    def swap(value):
        return lax.all_to_all(value, "seq", split_axis=0, concat_axis=0, tiled=True, axis_index_groups=cores)

    def across(value, bits):
        return lax.ppermute(value, "seq", [(s, s ^ bits) for s in range(devices)])

    def gathered(block):
        line = jnp.concatenate([block] + [across(block, 8 * k) for k in (1, 2, 3)], axis=0)
        return [line] + [across(line, 2 * k) for k in (1, 2, 3)]

    slot_ids = jnp.arange(capacity, dtype=jnp.int32)
    places = jnp.arange(devices, dtype=jnp.int32)[:, None] * tok_rows + chosen
    live_all = slot_ids[None, :] < counts[:, None]
    seq_ends = jnp.cumsum(lengths)
    starts = jnp.max(jnp.where(places[..., None] >= seq_ends, seq_ends, 0), axis=-1)
    kpos = jnp.where(live_all, places.astype(f32), far_away).reshape(chips, 2, SHARE)
    kpos = jnp.where(core == 0, kpos, kpos[:, ::-1]).swapaxes(0, 1).reshape(2, chips * SHARE)
    blocks = chips * HALF // BLOCK

    def query_order(value):
        value = lax.dynamic_index_in_dim(value.reshape(chips, 2, SHARE), core, 1, False)
        return value.reshape(blocks, chips // blocks, 2, HALF).swapaxes(1, 2).reshape(blocks, 2 * BLOCK)

    qpos = query_order(jnp.where(live_all, places, -1).astype(f32))
    qlow = query_order(starts.astype(f32))

    square = pltpu.VMEM((width, width), bf16)
    both = call(
        fetch_kernel, "fetch", [smem, smem] + [vmem] * 3, shaped((1, 2 * capacity, width), bf16),
        (own_id, counts, chosen, tokens_in, out_grad),
    )
    both_all = [lax.all_gather(both[0], "seq", axis=0, axis_index_groups=cores)]
    sent = call(
        prepare_kernel, "prepare", [smem, smem] + [vmem] * 2 + [hbm] * 3,
        shaped((chips, HALF + SHARE + NOTE, LANES), bf16),
        (own_id, counts, both, vectors, w_query, w_key, w_value),
        [square] * 3 + [pltpu.SemaphoreType.DMA((3,))],
    )
    got = swap(sent)
    other = across(got, 1)
    mixed_packed, turned, lse, total = call(
        functools.partial(pair_attend_kernel, factor), "attend", [vmem] * 5,
        (
            shaped((chips * HALF, LANES), bf16),
            shaped((chips * HALF, LANES), f32),
            shaped((blocks, 2 * BLOCK), f32),
            shaped((8, LANES), f32),
        ),
        (got, other, kpos, qpos, qlow),
    )
    mixed_got = swap(mixed_packed.reshape(chips, HALF, LANES))
    mixed = call(unpack_kernel, "unpack", [vmem], shaped((1, capacity, width), bf16), (mixed_got,))
    mixed_all = gathered(mixed)
    sent, new_rows, dmiddle, dweight = call(
        middle_kernel, "middle", [smem, smem] + [vmem] * 4 + [hbm] * 3,
        (
            shaped((chips, 2 * HALF + NOTE, LANES), bf16),
            shaped((capacity, width), bf16),
            shaped((capacity, width), f32),
            shaped((capacity, LANES), f32),
        ),
        (own_id, counts, mixed, total, both, vectors, w_out, w_up, w_down),
        [
            square,
            pltpu.VMEM((width, hidden_width), bf16),
            pltpu.VMEM((hidden_width, width), bf16),
            pltpu.VMEM((capacity, hidden_width), f32),
            pltpu.VMEM((capacity, hidden_width), bf16),
            pltpu.SemaphoreType.DMA((1 + 2 * CHUNKS,)),
        ],
    )
    grads_got = swap(sent)
    output = call(
        put_kernel, "put", [smem, smem] + [vmem] * 3, shaped((tok_rows, width), bf16),
        (own_id, counts, chosen, tokens_in, new_rows),
    )
    dq, dkv_own, dkv_other, coef = call(
        functools.partial(pair_attend_back_kernel, factor), "attend_back", [vmem] * 8,
        (
            shaped((chips * HALF, LANES), bf16),
            shaped((chips * SHARE, LANES), f32),
            shaped((chips * SHARE + 8, LANES), f32),
            shaped((8, LANES), f32),
        ),
        (got, other, grads_got, kpos, qpos, qlow, turned, lse),
    )
    dqkv, coef = call(
        keys_kernel, "keys", [vmem] * 4,
        (shaped((chips, HALF + SHARE, LANES), bf16), shaped((8, LANES), f32)),
        (dq.reshape(chips, HALF, LANES), dkv_own, across(dkv_other, 1), coef),
    )
    got = swap(dqkv)
    sources = 4
    hidden_cols = hidden_width // chips
    whole = lambda *shape: pl.BlockSpec(shape, lambda i, o: (0,) * len(shape))
    down_keep, down_give, keep, give = pl.pallas_call(
        units_kernel,
        out_shape=(
            shaped((hidden_cols // 2, width), f32),
            shaped((hidden_cols // 2, width), bf16),
            shaped((chips, GRAD_ROWS, LANES), f32),
            shaped((chips, GRAD_ROWS, LANES), bf16),
        ),
        grid_spec=pltpu.PrefetchScalarGridSpec(
            num_scalar_prefetch=1,
            grid=(chips // sources,),
            in_specs=[
                smem,
                whole(chips, 2 * HALF + NOTE, LANES),
                whole(chips, HALF + SHARE, LANES),
                whole(8, LANES),
                whole(8, LANES),
                whole(3, width),
                whole(1, 2 * capacity, width),
                whole(capacity, LANES),
                whole(width, width),
                pl.BlockSpec((width, hidden_cols), lambda i, o: (0, o[0] // 2)),
                pl.BlockSpec((hidden_cols, width), lambda i, o: (o[0] // 2, 0)),
            ]
            + [hbm] * (PIECES + 4),
            out_specs=(
                whole(hidden_cols // 2, width),
                whole(hidden_cols // 2, width),
                whole(chips, GRAD_ROWS, LANES),
                whole(chips, GRAD_ROWS, LANES),
            ),
            scratch_shapes=[
                pltpu.VMEM((2, sources, 2 * capacity, width), bf16),
                pltpu.VMEM((2, sources, capacity, width), bf16),
                pltpu.VMEM((hidden_cols, width), f32),
                pltpu.VMEM((hidden_cols, width), f32),
                pltpu.VMEM((HEAD_DIM, width), f32),
                pltpu.VMEM((HEAD_DIM, width), f32),
                pltpu.VMEM((2 * HEAD_DIM, width), f32),
                pltpu.VMEM((8, LANES), f32),
                pltpu.SemaphoreType.DMA((2, 4)),
                pltpu.SemaphoreType.DMA((2,)),
            ],
        ),
        compiler_params=params,
        name="units",
    )(own_id, counts, grads_got, dqkv, total, coef, vectors, both, dweight, w_out, w_up, w_down, *both_all, *mixed_all)
    sent, grad_down = call(
        merge_kernel, "merge", [vmem] * 4,
        (shaped((chips, GRAD_ROWS, LANES), bf16), shaped((hidden_cols // 2, width), f32)),
        (keep, across(give, 1), down_keep, across(down_give, 1)),
    )
    last = swap(sent)
    input_grad = call(
        rows_kernel, "rows", [smem, smem] + [vmem] * 9 + [hbm] * 3, shaped((tok_rows, width), bf16),
        (
            own_id, counts, chosen, got, both, dmiddle, dweight, total, coef, vectors, out_grad,
            w_query, w_key, w_value,
        ),
        [square] * 3 + [pltpu.SemaphoreType.DMA((3,))],
    )
    block = shaped((out_rows, width), f32)
    row = shaped((1, out_rows), f32)
    own_rows = pl.BlockSpec((out_rows, width), lambda i, o: (o[0], 0))
    grad_up, grad_out, grad_query, grad_key, grad_value, grad_router, grad_gain_attn, grad_gain_mlp = pl.pallas_call(
        finish_kernel,
        out_shape=(shaped((out_rows, hidden_width), f32), block, block, block, block, row, row, row),
        grid_spec=pltpu.PrefetchScalarGridSpec(
            num_scalar_prefetch=1,
            grid=(1,),
            in_specs=[
                whole(chips, GRAD_ROWS, LANES),
                whole(3, out_rows),
                pl.BlockSpec((out_rows, hidden_width), lambda i, o: (o[0], 0)),
                own_rows,
                own_rows,
                own_rows,
            ],
            out_specs=(whole(out_rows, hidden_width),) + (whole(out_rows, width),) * 4 + (whole(1, out_rows),) * 3,
        ),
        compiler_params=params,
        name="finish",
    )(own_id, last, own_gains, w_up, w_query, w_key, w_value)
    return (
        output,
        input_grad,
        grad_router.reshape(out_rows),
        grad_gain_attn.reshape(out_rows),
        grad_query,
        grad_key,
        grad_value,
        grad_out,
        grad_gain_mlp.reshape(out_rows),
        grad_up,
        grad_down,
    )


def per_device(*arguments):
    w_up, chosen = arguments[8], arguments[13]
    devices = lax.axis_size("seq")
    width, hidden_width = w_up.shape
    paired = (
        devices == 2 * HEADS
        and chosen.shape[0] == devices * SHARE
        and width == devices * OUT_ROWS
        and width == HEADS * HEAD_DIM
        and hidden_width == devices // 2 * TILES * LANES
    )
    return (pairs if paired else general)(*arguments)


def solution(mesh):
    placed = (P("seq", None),) + (P(),) * 9 + (P("seq", None),) + (P(),) * 3
    rows = P("seq", None)
    return jax.shard_map(
        per_device,
        mesh=mesh,
        in_specs=placed,
        out_specs=(rows, rows, P("seq"), P("seq"), rows, rows, rows, rows, P("seq"), rows, rows),
        check_vma=False,
    )
```

profile of v0, /device:TPU:0, one launch (start us, length us, event | category | flops | bytes accessed | tf_op | source)
XLA Modules:
  0.0 195.3 jit_solution(15795531649648195238)
XLA Ops:
  8.6 2.8 %fetch.1.both_ref.rows_ref = bf16[1,128,1024]{2,1,0:T(8,128)(2,1)} custom-call(s32[1]{0:T(128)} %bitcast.own_ref, s32[32]{0:T(128)} %counts_ref.11, s32[32,64]{1,0:T(8,128)} %reshape.144.chosen_ref, bf16[512,1024]{1,0:T(8,128)(2,1)} %old_ref.2, bf16[512,1024]{1,0:T(8,128)(2,1)} %old_ref.3), custom_call_target="tpu_custom_call" | custom-call | tf_op jit(solution)/shard_map/fetch/pallas_call | solution.py:916
  12.1 5.2 %prepare.1 = bf16[16,104,128]{2,1,0:T(8,128)(2,1)} custom-call(s32[1]{0:T(128)} %bitcast.own_ref, s32[32]{0:T(128)} %counts_ref.11, bf16[1,128,1024]{2,1,0:T(8,128)(2,1)} %fetch.1.both_ref.rows_ref, f32[3,1024]{1,0:T(4,128)} %maximum_convert_fusion.vectors_ref, bf16[1024,1024]{1,0:T(8,128)(2,1)} %wq_ref.5, bf16[1024,1024]{1,0:T(8,128)(2,1)} %wk_ref.5, ...), custom_call_target="tpu_custom_call" | custom-call | tf_op jit(solution)/shard_map/prepare/pallas_call | solution.py:916
  17.4 8.3 %all-to-all-start = ((bf16[16,104,128]{2,1,0:T(8,128)(2,1)}), bf16[16,104,128]{2,1,0:T(8,128)(2,1)S(1)}, u32[]{:S(2)}, u32[]{:S(2)}) async-start(bf16[16,104,128]{2,1,0:T(8,128)(2,1)} %prepare.1), calls=%async_computation | async-start | bytes 851968 | tf_op jit(solution)/shard_map/all_to_all | solution.py:959
  26.4 16.1 %all-to-all-done.got_ref = bf16[16,104,128]{2,1,0:T(8,128)(2,1)S(1)} async-done(((bf16[16,104,128]{2,1,0:T(8,128)(2,1)}), bf16[16,104,128]{2,1,0:T(8,128)(2,1)S(1)}, u32[]{:S(2)}, u32[]{:S(2)}) %all-to-all-start) | async-done | bytes 426016 | tf_op jit(solution)/shard_map/all_to_all | solution.py:959
  45.7 4.8 %attend.1 = (bf16[512,128]{1,0:T(8,128)(2,1)}, f32[512,128]{1,0:T(8,128)}, f32[4,256]{1,0:T(4,128)}, f32[8,128]{1,0:T(8,128)}) custom-call(bf16[16,104,128]{2,1,0:T(8,128)(2,1)} %copy-done, bf16[16,104,128]{2,1,0:T(8,128)(2,1)} %copy-done.4, f32[2,1024]{1,0:T(2,128)} %reshape.146.kpos_ref, f32[4,256]{1,0:T(4,128)} %reshape.148.qpos_ref, ...), custom_call_target="tpu_custom_call" | custom-call | tf_op jit(solution)/shard_map/attend/pallas_call | solution.py:916
  50.5 14.2 %all_to_all.25.got_ref = bf16[16,32,128]{2,1,0:T(8,128)(2,1)} all-to-all(bf16[16,32,128]{2,1,0:T(8,128)(2,1)} %bitcast.14), channel_id=1, replica_groups={{0,2,4,6,8,10,12,14,16,18,20,22,24,26,28,30},{1,3,5,7,9,11,13,15,17,19,..., dimensions={0} | all-to-all | bytes 262144 | tf_op jit(solution)/shard_map/all_to_all | solution.py:959
  66.4 14.9 %middle.1 = (bf16[16,72,128]{2,1,0:T(8,128)(2,1)}, bf16[64,1024]{1,0:T(8,128)(2,1)}, f32[64,1024]{1,0:T(8,128)}, f32[64,128]{1,0:T(8,128)}) custom-call(s32[1]{0:T(128)} %bitcast.own_ref, s32[32]{0:T(128)} %counts_ref.11, bf16[1,64,1024]{2,1,0:T(8,128)(2,1)} %unpack.1.mixed_ref, f32[8,128]{1,0:T(8,128)} %get-tuple-element.40.total_ref, ...), custom_call_target="tpu_custom_call" | custom-call | tf_op jit(solution)/shard_map/middle/pallas_call | solution.py:916
  81.2 4.0 %all-to-all-start.2 = ((bf16[16,72,128]{2,1,0:T(8,128)(2,1)}), bf16[16,72,128]{2,1,0:T(8,128)(2,1)S(1)}, u32[]{:S(2)}, u32[]{:S(2)}) async-start(bf16[16,72,128]{2,1,0:T(8,128)(2,1)} %get-tuple-element.42), calls=%async_computation.2 | async-start | bytes 589824 | tf_op jit(solution)/shard_map/all_to_all | solution.py:959
  87.3 2.4 %collective-permute-start.3 = (bf16[1,64,1024]{2,1,0:T(8,128)(2,1)S(1)}, bf16[1,64,1024]{2,1,0:T(8,128)(2,1)S(1)}, u32[]{:S(2)}, u32[]{:S(2)}) collective-permute-start(bf16[1,64,1024]{2,1,0:T(8,128)(2,1)S(1)} %copy-done.6), channel_id=1, source_target_pairs={{0,16},{1,17},{2,18},{3,19},{4,20},{5,21},{6,22},{7,23},{8,24},{9,... | collective-permute-start | bytes 393224 | tf_op jit(solution)/shard_map/ppermute | solution.py:962
  89.7 10.9 %all-to-all-done.2.grad_ref.got_ref = bf16[16,72,128]{2,1,0:T(8,128)(2,1)S(1)} async-done(((bf16[16,72,128]{2,1,0:T(8,128)(2,1)}), bf16[16,72,128]{2,1,0:T(8,128)(2,1)S(1)}, u32[]{:S(2)}, u32[]{:S(2)}) %all-to-all-start.2) | async-done | bytes 294944 | tf_op jit(solution)/shard_map/all_to_all | solution.py:959
  101.4 5.9 %attend_back.1 = (bf16[512,128]{1,0:T(8,128)(2,1)}, f32[1024,128]{1,0:T(8,128)}, f32[1032,128]{1,0:T(8,128)}, f32[8,128]{1,0:T(8,128)}) custom-call(bf16[16,104,128]{2,1,0:T(8,128)(2,1)} %copy-done, bf16[16,104,128]{2,1,0:T(8,128)(2,1)} %copy-done.4, bf16[16,72,128]{2,1,0:T(8,128)(2,1)} %copy-done.1, f32[2,1024]{1,0:T(2,128)} %reshape.146.kpos_ref, ...), custom_call_target="tpu_custom_call" | custom-call | tf_op jit(solution)/shard_map/attend_back/pallas_call | solution.py:916
  107.3 4.1 %collective-permute-done.3 = bf16[1,64,1024]{2,1,0:T(8,128)(2,1)S(1)} collective-permute-done((bf16[1,64,1024]{2,1,0:T(8,128)(2,1)S(1)}, bf16[1,64,1024]{2,1,0:T(8,128)(2,1)S(1)}, u32[]{:S(2)}, u32[]{:S(2)}) %collective-permute-start.3) | collective-permute-done | bytes 131104 | tf_op jit(solution)/shard_map/ppermute | solution.py:962
  115.8 2.1 %keys.1 = (bf16[16,96,128]{2,1,0:T(8,128)(2,1)}, f32[8,128]{1,0:T(8,128)}) custom-call(bf16[16,32,128]{2,1,0:T(8,128)(2,1)} %bitcast.13, f32[1024,128]{1,0:T(8,128)} %get-tuple-element.46.dkv_ref, f32[1032,128]{1,0:T(8,128)} %copy-done.8, f32[8,128]{1,0:T(8,128)} %get-tuple-element.48.coef_ref), custom_call_target="tpu_custom_call" | custom-call | tf_op jit(solution)/shard_map/keys/pallas_call | solution.py:916
  117.9 5.4 %all-to-all-start.3 = ((bf16[16,96,128]{2,1,0:T(8,128)(2,1)}), bf16[16,96,128]{2,1,0:T(8,128)(2,1)S(1)}, u32[]{:S(2)}, u32[]{:S(2)}) async-start(bf16[16,96,128]{2,1,0:T(8,128)(2,1)} %get-tuple-element.49.dqkv_ref), calls=%async_computation.3 | async-start | bytes 786432 | tf_op jit(solution)/shard_map/all_to_all | solution.py:959
  123.4 3.1 %collective-permute-done.5.rest_2_ = bf16[4,64,1024]{2,1,0:T(8,128)(2,1)S(1)} collective-permute-done((bf16[4,64,1024]{2,1,0:T(8,128)(2,1)S(1)}, bf16[4,64,1024]{2,1,0:T(8,128)(2,1)S(1)}, u32[]{:S(2)}, u32[]{:S(2)}) %collective-permute-start.5) | collective-permute-done | bytes 524320 | tf_op jit(solution)/shard_map/ppermute | solution.py:962
  126.4 13.2 %collective-permute-done.6.rest_3_ = bf16[4,64,1024]{2,1,0:T(8,128)(2,1)S(1)} collective-permute-done((bf16[4,64,1024]{2,1,0:T(8,128)(2,1)S(1)}, bf16[4,64,1024]{2,1,0:T(8,128)(2,1)S(1)}, u32[]{:S(2)}, u32[]{:S(2)}) %collective-permute-start.6) | collective-permute-done | bytes 524320 | tf_op jit(solution)/shard_map/ppermute | solution.py:962
  141.7 15.6 %units.1 = (f32[128,1024]{1,0:T(8,128)}, bf16[128,1024]{1,0:T(8,128)(2,1)}, f32[16,136,128]{2,1,0:T(8,128)}, bf16[16,136,128]{2,1,0:T(8,128)(2,1)}) custom-call(s32[1]{0:T(128)} %bitcast.own_ref, s32[32]{0:T(128)} %counts_ref.11, bf16[16,72,128]{2,1,0:T(8,128)(2,1)} %copy-done.1, bf16[16,96,128]{2,1,0:T(8,128)(2,1)} %get-tuple-element.49.dqkv_ref, ...), custom_call_target="tpu_custom_call" | custom-call | tf_op jit(solution)/shard_map/units/pallas_call | solution.py:1053
  157.9 2.0 %collective-permute-done.9.down_moved_ref = bf16[128,1024]{1,0:T(8,128)(2,1)S(1)} collective-permute-done((bf16[128,1024]{1,0:T(8,128)(2,1)}, bf16[128,1024]{1,0:T(8,128)(2,1)S(1)}, u32[]{:S(2)}, u32[]{:S(2)}) %collective-permute-start.9) | collective-permute-done | bytes 262176 | tf_op jit(solution)/shard_map/ppermute | solution.py:962
  160.8 2.7 %merge.1 = (bf16[16,136,128]{2,1,0:T(8,128)(2,1)}, f32[128,1024]{1,0:T(8,128)}) custom-call(f32[16,136,128]{2,1,0:T(8,128)} %get-tuple-element.53.keep_ref, bf16[16,136,128]{2,1,0:T(8,128)(2,1)} %copy-done.7, f32[128,1024]{1,0:T(8,128)} %get-tuple-element.55.down_keep_ref, bf16[128,1024]{1,0:T(8,128)(2,1)} %copy-done.13), custom_call_target="tpu_custom_call" | custom-call | tf_op jit(solution)/shard_map/merge/pallas_call | solution.py:916
  163.5 5.8 %all-to-all-start.4 = ((bf16[16,136,128]{2,1,0:T(8,128)(2,1)}), bf16[16,136,128]{2,1,0:T(8,128)(2,1)S(1)}, u32[]{:S(2)}, u32[]{:S(2)}) async-start(bf16[16,136,128]{2,1,0:T(8,128)(2,1)} %get-tuple-element.57), calls=%async_computation.4 | async-start | bytes 1114112 | tf_op jit(solution)/shard_map/all_to_all | solution.py:959
  170.7 2.6 %put.1 = bf16[512,1024]{1,0:T(8,128)(2,1)} custom-call(s32[1]{0:T(128)} %bitcast.own_ref, s32[32]{0:T(128)} %counts_ref.11, s32[32,64]{1,0:T(8,128)} %reshape.144.chosen_ref, bf16[512,1024]{1,0:T(8,128)(2,1)} %old_ref.2, bf16[64,1024]{1,0:T(8,128)(2,1)} %get-tuple-element.41.new_ref), custom_call_target="tpu_custom_call" | custom-call | tf_op jit(solution)/shard_map/put/pallas_call | solution.py:916
  173.3 7.3 %rows.1 = bf16[512,1024]{1,0:T(8,128)(2,1)} custom-call(s32[1]{0:T(128)} %bitcast.own_ref, s32[32]{0:T(128)} %counts_ref.11, s32[32,64]{1,0:T(8,128)} %reshape.144.chosen_ref, bf16[16,96,128]{2,1,0:T(8,128)(2,1)} %copy-done.5, bf16[1,128,1024]{2,1,0:T(8,128)(2,1)} %fetch.1.both_ref.rows_ref, f32[64,1024]{1,0:T(8,128)} %get-tuple-element.50.dmiddle_ref, ...), custom_call_target="tpu_custom_call" | custom-call | tf_op jit(solution)/shard_map/rows/pallas_call | solution.py:916
  180.7 4.7 %all-to-all-done.4.got_ref = bf16[16,136,128]{2,1,0:T(8,128)(2,1)S(1)} async-done(((bf16[16,136,128]{2,1,0:T(8,128)(2,1)}), bf16[16,136,128]{2,1,0:T(8,128)(2,1)S(1)}, u32[]{:S(2)}, u32[]{:S(2)}) %all-to-all-start.4) | async-done | bytes 557088 | tf_op jit(solution)/shard_map/all_to_all | solution.py:959
  186.1 2.3 %finish.1 = (f32[32,4096]{1,0:T(8,128)}, f32[32,1024]{1,0:T(8,128)}, f32[32,1024]{1,0:T(8,128)}, f32[32,1024]{1,0:T(8,128)}, f32[32,1024]{1,0:T(8,128)}, /*index...) custom-call(s32[1]{0:T(128)} %bitcast.own_ref, bf16[16,136,128]{2,1,0:T(8,128)(2,1)} %copy-done.2, ...), custom_call_target="tpu_custom_call" | custom-call | tf_op jit(solution)/shard_map/finish/pallas_call | solution.py:1117
  (88 shorter events, 20.4 us)
Async XLA Ops:
  7.2 4.3 %copy-start.18 = (bf16[1024]{0:T(1024)(128)(2,1)S(1)}, bf16[1024]{0:T(1024)(128)(2,1)}, u32[]{:S(2)}) copy-start(bf16[1024]{0:T(1024)(128)(2,1)} %param.21) | copy-start | bytes 6148
  7.2 133.6 %all-gather.2.cloned.1.call-start = ((), (), s32[]{:S(2)}) async-start(), calls=%async_computation.5 | async-start | bytes 4456448 | tf_op jit(solution)/shard_map/all_gather | solution.py:989
  12.1 13.6 %copy-start.15 = (s32[32]{0:T(128)S(1)}, s32[32]{0:T(128)}, u32[]{:S(2)}) copy-start(s32[32]{0:T(128)} %counts_ref.11) | copy-start | bytes 388
  12.1 13.7 %copy-start.14 = (s32[2048]{0:T(1024)S(1)}, s32[2048]{0:T(1024)}, u32[]{:S(2)}) copy-start(s32[2048]{0:T(1024)} %param.27) | copy-start | bytes 24580
  12.1 13.8 %copy-start.19 = (s32[4]{0:T(128)S(1)}, s32[4]{0:T(128)}, u32[]{:S(2)}) copy-start(s32[4]{0:T(128)} %param.25) | copy-start | bytes 52
  12.1 13.9 %copy-start.12 = (s32[32,64]{1,0:T(8,128)S(1)}, s32[32,64]{1,0:T(8,128)}, u32[]{:S(2)}) copy-start(s32[32,64]{1,0:T(8,128)} %reshape.144.chosen_ref) | copy-start | bytes 24580
  17.4 25.1 %all-to-all-start = ((bf16[16,104,128]{2,1,0:T(8,128)(2,1)}), bf16[16,104,128]{2,1,0:T(8,128)(2,1)S(1)}, u32[]{:S(2)}, u32[]{:S(2)}) async-start(bf16[16,104,128]{2,1,0:T(8,128)(2,1)} %prepare.1), calls=%async_computation | async-start | bytes 851968 | tf_op jit(solution)/shard_map/all_to_all | solution.py:959
  42.5 2.5 %collective-permute-start = (bf16[16,104,128]{2,1,0:T(8,128)(2,1)S(1)}, bf16[16,104,128]{2,1,0:T(8,128)(2,1)S(1)}, u32[]{:S(2)}, u32[]{:S(2)}) collective-permute-start(bf16[16,104,128]{2,1,0:T(8,128)(2,1)S(1)} %all-to-all-done.got_ref), channel_id=1, source_target_pairs={{0,1},{1,0},{2,3},{3,2},{4,5},{5,4},{6,7},{7,6},{8,9},{9,8},{10,11... | collective-permute-start | bytes 1277960 | tf_op jit(solution)/shard_map/ppermute | solution.py:962
  66.4 18.9 %copy-start.6 = (bf16[1,64,1024]{2,1,0:T(8,128)(2,1)S(1)}, bf16[1,64,1024]{2,1,0:T(8,128)(2,1)}, u32[]{:S(2)}) copy-start(bf16[1,64,1024]{2,1,0:T(8,128)(2,1)} %unpack.1.mixed_ref) | copy-start | bytes 393220
  81.2 19.4 %all-to-all-start.2 = ((bf16[16,72,128]{2,1,0:T(8,128)(2,1)}), bf16[16,72,128]{2,1,0:T(8,128)(2,1)S(1)}, u32[]{:S(2)}, u32[]{:S(2)}) async-start(bf16[16,72,128]{2,1,0:T(8,128)(2,1)} %get-tuple-element.42), calls=%async_computation.2 | async-start | bytes 589824 | tf_op jit(solution)/shard_map/all_to_all | solution.py:959
  85.3 22.0 %collective-permute-start.2 = (bf16[1,64,1024]{2,1,0:T(8,128)(2,1)S(1)}, bf16[1,64,1024]{2,1,0:T(8,128)(2,1)S(1)}, u32[]{:S(2)}, u32[]{:S(2)}) collective-permute-start(bf16[1,64,1024]{2,1,0:T(8,128)(2,1)S(1)} %copy-done.6), channel_id=1, source_target_pairs={{0,8},{1,9},{2,10},{3,11},{4,12},{5,13},{6,14},{7,15},{8,0},{9,1},... | collective-permute-start | bytes 393224 | tf_op jit(solution)/shard_map/ppermute | solution.py:962
  87.3 24.1 %collective-permute-start.3 = (bf16[1,64,1024]{2,1,0:T(8,128)(2,1)S(1)}, bf16[1,64,1024]{2,1,0:T(8,128)(2,1)S(1)}, u32[]{:S(2)}, u32[]{:S(2)}) collective-permute-start(bf16[1,64,1024]{2,1,0:T(8,128)(2,1)S(1)} %copy-done.6), channel_id=1, source_target_pairs={{0,16},{1,17},{2,18},{3,19},{4,20},{5,21},{6,22},{7,23},{8,24},{9,... | collective-permute-start | bytes 393224 | tf_op jit(solution)/shard_map/ppermute | solution.py:962
  89.6 21.8 %collective-permute-start.4 = (bf16[1,64,1024]{2,1,0:T(8,128)(2,1)S(1)}, bf16[1,64,1024]{2,1,0:T(8,128)(2,1)S(1)}, u32[]{:S(2)}, u32[]{:S(2)}) collective-permute-start(bf16[1,64,1024]{2,1,0:T(8,128)(2,1)S(1)} %copy-done.6), channel_id=1, source_target_pairs={{0,24},{1,25},{2,26},{3,27},{4,28},{5,29},{6,30},{7,31},{8,16},{9,... | collective-permute-start | bytes 393224 | tf_op jit(solution)/shard_map/ppermute | solution.py:962
  107.3 7.8 %collective-permute-start.1 = (f32[1032,128]{1,0:T(8,128)}, f32[1032,128]{1,0:T(8,128)S(1)}, u32[]{:S(2)}, u32[]{:S(2)}) collective-permute-start(f32[1032,128]{1,0:T(8,128)} %get-tuple-element.47), channel_id=1, source_target_pairs={{0,1},{1,0},{2,3},{3,2},{4,5},{5,4},{6,7},{7,6},{8,9},{9,8},{10,11... | collective-permute-start | bytes 1585160 | tf_op jit(solution)/shard_map/ppermute | solution.py:962
  111.5 29.4 %copy-start.3 = (bf16[4,64,1024]{2,1,0:T(8,128)(2,1)}, bf16[4,64,1024]{2,1,0:T(8,128)(2,1)S(1)}, u32[]{:S(2)}) copy-start(bf16[4,64,1024]{2,1,0:T(8,128)(2,1)S(1)} %pad_maximum_fusion.rest_1_) | copy-start | bytes 1572868
  111.5 14.9 %collective-permute-start.5 = (bf16[4,64,1024]{2,1,0:T(8,128)(2,1)S(1)}, bf16[4,64,1024]{2,1,0:T(8,128)(2,1)S(1)}, u32[]{:S(2)}, u32[]{:S(2)}) collective-permute-start(bf16[4,64,1024]{2,1,0:T(8,128)(2,1)S(1)} %pad_maximum_fusion.rest_1_), channel_id=1, source_target_pairs={{0,2},{1,3},{2,0},{3,1},{4,6},{5,7},{6,4},{7,5},{8,10},{9,11},{10,... | collective-permute-start | bytes 1572872 | tf_op jit(solution)/shard_map/ppermute | solution.py:962
  113.1 26.6 %collective-permute-start.6 = (bf16[4,64,1024]{2,1,0:T(8,128)(2,1)S(1)}, bf16[4,64,1024]{2,1,0:T(8,128)(2,1)S(1)}, u32[]{:S(2)}, u32[]{:S(2)}) collective-permute-start(bf16[4,64,1024]{2,1,0:T(8,128)(2,1)S(1)} %pad_maximum_fusion.rest_1_), channel_id=1, source_target_pairs={{0,4},{1,5},{2,6},{3,7},{4,0},{5,1},{6,2},{7,3},{8,12},{9,13},{10,... | collective-permute-start | bytes 1572872 | tf_op jit(solution)/shard_map/ppermute | solution.py:962
  113.5 27.4 %collective-permute-start.7 = (bf16[4,64,1024]{2,1,0:T(8,128)(2,1)S(1)}, bf16[4,64,1024]{2,1,0:T(8,128)(2,1)S(1)}, u32[]{:S(2)}, u32[]{:S(2)}) collective-permute-start(bf16[4,64,1024]{2,1,0:T(8,128)(2,1)S(1)} %pad_maximum_fusion.rest_1_), channel_id=1, source_target_pairs={{0,6},{1,7},{2,4},{3,5},{4,2},{5,3},{6,0},{7,1},{8,14},{9,15},{10,... | collective-permute-start | bytes 1572872 | tf_op jit(solution)/shard_map/ppermute | solution.py:962
  117.9 45.6 %all-to-all-start.3 = ((bf16[16,96,128]{2,1,0:T(8,128)(2,1)}), bf16[16,96,128]{2,1,0:T(8,128)(2,1)S(1)}, u32[]{:S(2)}, u32[]{:S(2)}) async-start(bf16[16,96,128]{2,1,0:T(8,128)(2,1)} %get-tuple-element.49.dqkv_ref), calls=%async_computation.3 | async-start | bytes 786432 | tf_op jit(solution)/shard_map/all_to_all | solution.py:959
  126.4 14.4 %copy-start.9 = (bf16[4,64,1024]{2,1,0:T(8,128)(2,1)}, bf16[4,64,1024]{2,1,0:T(8,128)(2,1)S(1)}, u32[]{:S(2)}) copy-start(bf16[4,64,1024]{2,1,0:T(8,128)(2,1)S(1)} %collective-permute-done.5.rest_2_) | copy-start | bytes 1572868
  157.3 2.6 %collective-permute-start.8 = (bf16[16,136,128]{2,1,0:T(8,128)(2,1)}, bf16[16,136,128]{2,1,0:T(8,128)(2,1)S(1)}, u32[]{:S(2)}, u32[]{:S(2)}) collective-permute-start(bf16[16,136,128]{2,1,0:T(8,128)(2,1)} %get-tuple-element.54), channel_id=1, source_target_pairs={{0,1},{1,0},{2,3},{3,2},{4,5},{5,4},{6,7},{7,6},{8,9},{9,8},{10,11... | collective-permute-start | bytes 1671176 | tf_op jit(solution)/shard_map/ppermute | solution.py:962
  157.4 2.5 %collective-permute-start.9 = (bf16[128,1024]{1,0:T(8,128)(2,1)}, bf16[128,1024]{1,0:T(8,128)(2,1)S(1)}, u32[]{:S(2)}, u32[]{:S(2)}) collective-permute-start(bf16[128,1024]{1,0:T(8,128)(2,1)} %get-tuple-element.56), channel_id=1, source_target_pairs={{0,1},{1,0},{2,3},{3,2},{4,5},{5,4},{6,7},{7,6},{8,9},{9,8},{10,11... | collective-permute-start | bytes 786440 | tf_op jit(solution)/shard_map/ppermute | solution.py:962
  163.5 9.8 %copy-start.5 = (bf16[16,96,128]{2,1,0:T(8,128)(2,1)}, bf16[16,96,128]{2,1,0:T(8,128)(2,1)S(1)}, u32[]{:S(2)}) copy-start(bf16[16,96,128]{2,1,0:T(8,128)(2,1)S(1)} %all-to-all-done.3.got_ref) | copy-start | bytes 1179652
  163.5 21.8 %all-to-all-start.4 = ((bf16[16,136,128]{2,1,0:T(8,128)(2,1)}), bf16[16,136,128]{2,1,0:T(8,128)(2,1)S(1)}, u32[]{:S(2)}, u32[]{:S(2)}) async-start(bf16[16,136,128]{2,1,0:T(8,128)(2,1)} %get-tuple-element.57), calls=%async_computation.4 | async-start | bytes 1114112 | tf_op jit(solution)/shard_map/all_to_all | solution.py:959
  (11 other events, 17.7 us)
Sparse Core Ops, SparseCore 0:
  11.6 92.7 all-gather.1
where the time goes:
time: 196 us; the launch traced here: 195 us
  Pallas kernels  67.9 us (35%)
  waiting for transfers between devices  55.4 us (28%)
  starting transfers between devices  32.2 us (16%)
  between operations  14.4 us (7%)
  blocking collectives  14.2 us (7%)
  local copies, waits for them, and re-layouts  9.94 us (5%)
    pallas_call x10, Pallas kernels, call(): pl.pallas_call(kernel, out_shape=out_shape, in_specs=in_specs, out_specs=...  49.9 us
    all_to_all x4, waiting for transfers between devices, swap(): lax.all_to_all(value, 'seq', split_axis=0, concat_axis=0, tiled=True, axi...  31.7 us
    ppermute x10, waiting for transfers between devices, across(): return lax.ppermute(value, 'seq', [(s, s ^ bits) for s in range(devices)])  23.7 us
    all_to_all x4, starting transfers between devices, swap(): lax.all_to_all(value, 'seq', split_axis=0, concat_axis=0, tiled=True, axi...  23.6 us
    pallas_call x1, Pallas kernels, pairs(): pl.pallas_call(units_kernel, out_shape=(shaped((hidden_cols // 2, width),...  15.6 us
    all_to_all x1, blocking collectives, swap(): lax.all_to_all(value, 'seq', split_axis=0, concat_axis=0, tiled=True, axi...  14.2 us
    ppermute x10, starting transfers between devices, across(): return lax.ppermute(value, 'seq', [(s, s ^ bits) for s in range(devices)])  8.58 us
    unnamed x40, local copies, waits for them, and re-layouts  4.81 us
  transfers between devices with their start and end apart: 15, of which 8 were waited for; matrix products, arithmetic and copies ran while one was open for 3% of the time, Pallas kernels for 32%

commit v1 on v0

--- a/solution.py
+++ b/solution.py
@@ -557,6 +557,45 @@
     wide = jnp.broadcast_to(column, (column.shape[0], LANES))
     filled = jnp.concatenate([wide, jnp.zeros((LANES - column.shape[0], LANES), f32)], axis=0)
     return jnp.transpose(filled)[:1, : column.shape[0]]
+
+
+def places_kernel(own_ref, counts_ref, lengths_ref, chosen_ref, kpos_ref, qpos_ref, qlow_ref):
+    core = own_ref[0] % 2
+    devices, capacity = chosen_ref.shape
+    tok_rows = lengths_ref[lengths_ref.shape[0] - 1]
+    slot = lax.broadcasted_iota(jnp.int32, (1, capacity), 1)
+    ends = []
+    for k in range(lengths_ref.shape[0] - 1):
+        ends.append(lengths_ref[k] + (ends[-1] if ends else 0))
+
+    def place(device):
+        value = device * tok_rows + chosen_ref[pl.ds(device, 1), :]
+        return value, slot < counts_ref[device]
+
+    def key_row(device):
+        value, live = place(device)
+        return jnp.where(live, value.astype(f32), far_away)
+
+    for m in range(2):
+        parity = jnp.bitwise_xor(core, m)
+        for c in range(0, devices // 2, 2):
+            tile = jnp.concatenate([key_row(2 * c + parity), key_row(2 * c + 2 + parity)], axis=1)
+            kpos_ref[m : m + 1, c * capacity : (c + 2) * capacity] = tile
+    blocks = qpos_ref.shape[0]
+    sources = devices // 2 // blocks
+    for b in range(blocks):
+        lows, highs = [], []
+        for c in range(b * sources, (b + 1) * sources):
+            value, live = place(2 * c + core)
+            low = jnp.zeros_like(value)
+            for end in ends:
+                low = jnp.maximum(low, jnp.where(value >= end, end, 0))
+            both = jnp.concatenate([jnp.where(live, value, -1), low], axis=0).astype(f32)
+            lows.append(both[:, :HALF])
+            highs.append(both[:, HALF:])
+        both = jnp.concatenate(lows + highs, axis=1)
+        qpos_ref[b : b + 1, :] = both[:1]
+        qlow_ref[b : b + 1, :] = both[1:]
 
 
 def fetch_kernel(own_ref, counts_ref, chosen_ref, tokens_ref, grads_ref, both_ref):
@@ -684,7 +723,7 @@
     own_ref, counts_ref, got_ref, dqkv_ref, total_ref, coef_ref, vectors_ref, rows_ref, dweight_ref,
     out_ref, up_ref, down_ref, *rest,
 ):
-    boths, mixeds, rest = rest[:PIECES], rest[PIECES : PIECES + 4], rest[PIECES + 4 :]
+    boths, mixeds, rest = rest[:PIECES], rest[PIECES : PIECES + 5], rest[PIECES + 5 :]
     down_keep_ref, down_give_ref, keep_ref, give_ref, rest = *rest[:4], rest[4:]
     both, mixed_slots, grad_up, grad_down, grad_out, grad_q, grad_kv, ratio_ref, both_sems, mixed_sems = rest
     step = pl.program_id(0)
@@ -695,17 +734,24 @@
     slot = step % 2
 
     def both_copies(k, at):
-        if PIECES == 4:
-            return [pltpu.make_async_copy(boths[k], both.at[at], both_sems.at[at, 0])]
+        if PIECES == 5:
+            return piece_copies(boths, both, both_sems, k)
         return [
             pltpu.make_async_copy(boths[0].at[chip_of(own_ref, 4 * k + j)], both.at[at, j], both_sems.at[at, j])
             for j in range(4)
         ]
 
+    def piece_copies(pieces, slots, sems, k):
+        at = k % 2
+        if k < 3:
+            return [pltpu.make_async_copy(pieces[k], slots.at[at], sems.at[at, 0])]
+        return [
+            pltpu.make_async_copy(pieces[k + half], slots.at[at, 2 * half : 2 * half + 2], sems.at[at, half])
+            for half in range(2)
+        ]
+
     def copies(k):
-        return both_copies(k, k % 2) + [
-            pltpu.make_async_copy(mixeds[k], mixed_slots.at[k % 2], mixed_sems.at[k % 2])
-        ]
+        return both_copies(k, k % 2) + piece_copies(mixeds, mixed_slots, mixed_sems, k)
 
     for k in range(4):
 
@@ -837,7 +883,7 @@
 
 
 def finish_kernel(
-    own_ref, got_ref, own_gain_ref, up_ref, wq_ref, wk_ref, wv_ref,
+    got_ref, own_gain_ref, up_ref, wq_ref, wk_ref, wv_ref,
     grad_up_ref, grad_out_ref, grad_q_ref, grad_k_ref, grad_v_ref, router_ref, gain_attn_ref, gain_mlp_ref,
 ):
     total = jnp.zeros((OUT_ROWS, LANES), f32)
@@ -905,11 +951,28 @@
 
 smem = pl.BlockSpec(memory_space=pltpu.SMEM)
 hbm = pl.BlockSpec(memory_space=pl.ANY)
-params = pltpu.CompilerParams(vmem_limit_bytes=vmem_limit)
+megabytes = {
+    "places": 4, "fetch": 56, "prepare": 56, "attend": 20, "unpack": 4, "middle": 56, "put": 56, "attend_back": 24,
+    "keys": 8, "units": 56, "merge": 10, "rows": 56, "finish": 12,
+}
+
+
+def params_of(name):
+    return pltpu.CompilerParams(vmem_limit_bytes=megabytes[name] * 1024 * 1024)
 
 
 def shaped(shape, dtype):
     return jax.ShapeDtypeStruct(shape, dtype)
+
+
+microseconds = {
+    "places": 1, "fetch": 3, "prepare": 5, "attend": 5, "unpack": 2, "middle": 15, "put": 3, "attend_back": 6, "keys": 2,
+    "units": 16, "merge": 3, "rows": 7, "finish": 2,
+}
+
+
+def cost_of(name):
+    return pl.CostEstimate(flops=0, transcendentals=0, bytes_accessed=microseconds[name] * 3_300_000)
 
 
 def call(kernel, name, in_specs, out_shape, arguments, scratch=()):
@@ -919,7 +982,8 @@
         in_specs=in_specs,
         out_specs=jax.tree.map(lambda _: vmem, out_shape),
         scratch_shapes=list(scratch),
-        compiler_params=params,
+        compiler_params=params_of(name),
+        cost_estimate=cost_of(name),
         name=name,
     )(*arguments)
 
@@ -961,26 +1025,16 @@
     def across(value, bits):
         return lax.ppermute(value, "seq", [(s, s ^ bits) for s in range(devices)])
 
-    def gathered(block):
-        line = jnp.concatenate([block] + [across(block, 8 * k) for k in (1, 2, 3)], axis=0)
-        return [line] + [across(line, 2 * k) for k in (1, 2, 3)]
-
-    slot_ids = jnp.arange(capacity, dtype=jnp.int32)
-    places = jnp.arange(devices, dtype=jnp.int32)[:, None] * tok_rows + chosen
-    live_all = slot_ids[None, :] < counts[:, None]
-    seq_ends = jnp.cumsum(lengths)
-    starts = jnp.max(jnp.where(places[..., None] >= seq_ends, seq_ends, 0), axis=-1)
-    kpos = jnp.where(live_all, places.astype(f32), far_away).reshape(chips, 2, SHARE)
-    kpos = jnp.where(core == 0, kpos, kpos[:, ::-1]).swapaxes(0, 1).reshape(2, chips * SHARE)
+    def line_of(block):
+        return jnp.concatenate([block] + [across(block, 8 * k) for k in (1, 2, 3)], axis=0)
+
+    def sides_of(line):
+        return [line, across(line, 2), across(line, 4)]
+
+    def gathered(sides):
+        return sides + [across(sides[2][:2], 2), across(sides[1][2:], 4)]
+
     blocks = chips * HALF // BLOCK
-
-    def query_order(value):
-        value = lax.dynamic_index_in_dim(value.reshape(chips, 2, SHARE), core, 1, False)
-        return value.reshape(blocks, chips // blocks, 2, HALF).swapaxes(1, 2).reshape(blocks, 2 * BLOCK)
-
-    qpos = query_order(jnp.where(live_all, places, -1).astype(f32))
-    qlow = query_order(starts.astype(f32))
-
     square = pltpu.VMEM((width, width), bf16)
     both = call(
         fetch_kernel, "fetch", [smem, smem] + [vmem] * 3, shaped((1, 2 * capacity, width), bf16),
@@ -992,6 +1046,16 @@
         shaped((chips, HALF + SHARE + NOTE, LANES), bf16),
         (own_id, counts, both, vectors, w_query, w_key, w_value),
         [square] * 3 + [pltpu.SemaphoreType.DMA((3,))],
+    )
+    chosen_after, _ = lax.optimization_barrier((chosen, sent))
+    kpos, qpos, qlow = call(
+        places_kernel, "places", [smem] * 3 + [vmem],
+        (
+            shaped((2, chips * SHARE), f32),
+            shaped((blocks, 2 * BLOCK), f32),
+            shaped((blocks, 2 * BLOCK), f32),
+        ),
+        (own_id, counts, jnp.append(lengths, tok_rows), chosen_after),
     )
     got = swap(sent)
     other = across(got, 1)
@@ -1007,7 +1071,7 @@
     )
     mixed_got = swap(mixed_packed.reshape(chips, HALF, LANES))
     mixed = call(unpack_kernel, "unpack", [vmem], shaped((1, capacity, width), bf16), (mixed_got,))
-    mixed_all = gathered(mixed)
+    mixed_line = line_of(mixed)
     sent, new_rows, dmiddle, dweight = call(
         middle_kernel, "middle", [smem, smem] + [vmem] * 4 + [hbm] * 3,
         (
@@ -1026,7 +1090,10 @@
             pltpu.SemaphoreType.DMA((1 + 2 * CHUNKS,)),
         ],
     )
+    mixed_line, sent = lax.optimization_barrier((mixed_line, sent))
+    mixed_sides = sides_of(mixed_line)
     grads_got = swap(sent)
+    mixed_all = gathered(mixed_sides)
     output = call(
         put_kernel, "put", [smem, smem] + [vmem] * 3, shaped((tok_rows, width), bf16),
         (own_id, counts, chosen, tokens_in, new_rows),
@@ -1041,10 +1108,11 @@
         ),
         (got, other, grads_got, kpos, qpos, qlow, turned, lse),
     )
+    moved = across(dkv_other, 1)
     dqkv, coef = call(
         keys_kernel, "keys", [vmem] * 4,
         (shaped((chips, HALF + SHARE, LANES), bf16), shaped((8, LANES), f32)),
-        (dq.reshape(chips, HALF, LANES), dkv_own, across(dkv_other, 1), coef),
+        (dq.reshape(chips, HALF, LANES), dkv_own, moved, coef),
     )
     got = swap(dqkv)
     sources = 4
@@ -1074,7 +1142,7 @@
                 pl.BlockSpec((width, hidden_cols), lambda i, o: (0, o[0] // 2)),
                 pl.BlockSpec((hidden_cols, width), lambda i, o: (o[0] // 2, 0)),
             ]
-            + [hbm] * (PIECES + 4),
+            + [hbm] * (PIECES + 5),
             out_specs=(
                 whole(hidden_cols // 2, width),
                 whole(hidden_cols // 2, width),
@@ -1091,10 +1159,11 @@
                 pltpu.VMEM((2 * HEAD_DIM, width), f32),
                 pltpu.VMEM((8, LANES), f32),
                 pltpu.SemaphoreType.DMA((2, 4)),
-                pltpu.SemaphoreType.DMA((2,)),
+                pltpu.SemaphoreType.DMA((2, 2)),
             ],
         ),
-        compiler_params=params,
+        compiler_params=params_of("units"),
+        cost_estimate=cost_of("units"),
         name="units",
     )(own_id, counts, grads_got, dqkv, total, coef, vectors, both, dweight, w_out, w_up, w_down, *both_all, *mixed_all)
     sent, grad_down = call(
@@ -1113,26 +1182,12 @@
     )
     block = shaped((out_rows, width), f32)
     row = shaped((1, out_rows), f32)
-    own_rows = pl.BlockSpec((out_rows, width), lambda i, o: (o[0], 0))
-    grad_up, grad_out, grad_query, grad_key, grad_value, grad_router, grad_gain_attn, grad_gain_mlp = pl.pallas_call(
-        finish_kernel,
-        out_shape=(shaped((out_rows, hidden_width), f32), block, block, block, block, row, row, row),
-        grid_spec=pltpu.PrefetchScalarGridSpec(
-            num_scalar_prefetch=1,
-            grid=(1,),
-            in_specs=[
-                whole(chips, GRAD_ROWS, LANES),
-                whole(3, out_rows),
-                pl.BlockSpec((out_rows, hidden_width), lambda i, o: (o[0], 0)),
-                own_rows,
-                own_rows,
-                own_rows,
-            ],
-            out_specs=(whole(out_rows, hidden_width),) + (whole(out_rows, width),) * 4 + (whole(1, out_rows),) * 3,
-        ),
-        compiler_params=params,
-        name="finish",
-    )(own_id, last, own_gains, w_up, w_query, w_key, w_value)
+    first_row = own * out_rows
+    grad_up, grad_out, grad_query, grad_key, grad_value, grad_router, grad_gain_attn, grad_gain_mlp = call(
+        finish_kernel, "finish", [vmem] * 6,
+        (shaped((out_rows, hidden_width), f32), block, block, block, block, row, row, row),
+        (last, own_gains, *(lax.dynamic_slice_in_dim(w, first_row, out_rows) for w in (w_up, w_query, w_key, w_value))),
+    )
     return (
         output,
         input_grad,

time: 196 us -> 173 us (0.88)
  waiting for transfers between devices: 55.4 us -> 15.4 us
  blocking collectives: 14.2 us -> 39 us
  Pallas kernels: 67.9 us -> 58.7 us
    all_to_all x1 -> x2, blocking collectives: 14.2 us -> 39 us  [swap(): lax.all_to_all(value, 'seq', split_axis=0, concat_axis=0, tiled=True, axi...]
    all_to_all x4 -> x3, waiting for transfers between devices: 31.7 us -> 11.6 us  [swap(): lax.all_to_all(value, 'seq', split_axis=0, concat_axis=0, tiled=True, axi...]
    ppermute x10 -> x11, waiting for transfers between devices: 23.7 us -> 3.86 us  [across(): return lax.ppermute(value, 'seq', [(s, s ^ bits) for s in range(devices)])]
    pallas_call x10 -> x12, Pallas kernels: 49.9 us -> 43 us  [call(): pl.pallas_call(kernel, out_shape=out_shape, in_specs=in_specs, out_specs=...]
    dynamic_slice x0 -> x3, local copies, waits for them, and re-layouts: none -> 2.7 us  [pairs(): lax.dynamic_slice_in_dim(w, first_row, out_rows)]
    pallas_call x1 -> x0, Pallas kernels: 2.32 us -> none  [pairs(): pl.pallas_call(finish_kernel, out_shape=(shaped((out_rows, hidden_width),...]
    reshape x5 -> x0, local copies, waits for them, and re-layouts: 2.19 us -> none  [the longest x4 1.51 us: query_order(): value.reshape(blocks, chips // blocks, 2, HALF).swapaxes(1, 2)]
    ppermute x10 -> x11, starting transfers between devices: 8.58 us -> 10.6 us  [across(): return lax.ppermute(value, 'seq', [(s, s ^ bits) for s in range(devices)])]
  transfers between devices with their start and end apart: 15 -> 15, of which waited for: 8 -> 6; matrix products, arithmetic and copies ran while one was open for 3% -> 3% of each run, Pallas kernels for 32% -> 32%
where the time goes in v1:
time: 173 us; the launch traced here: 172 us
  Pallas kernels  58.7 us (34%)
  blocking collectives  39 us (23%)
  starting transfers between devices  33.5 us (19%)
  waiting for transfers between devices  15.4 us (9%)
  between operations  14.3 us (8%)
  local copies, waits for them, and re-layouts  9.09 us (5%)
    pallas_call x12, Pallas kernels, call(): pl.pallas_call(kernel, out_shape=out_shape, in_specs=in_specs, out_specs=...  43 us
    all_to_all x2, blocking collectives, swap(): lax.all_to_all(value, 'seq', split_axis=0, concat_axis=0, tiled=True, axi...  39 us
    all_to_all x3, starting transfers between devices, swap(): lax.all_to_all(value, 'seq', split_axis=0, concat_axis=0, tiled=True, axi...  22.8 us
    pallas_call x1, Pallas kernels, pairs(): pl.pallas_call(units_kernel, out_shape=(shaped((hidden_cols // 2, width),...  15.7 us
    all_to_all x3, waiting for transfers between devices, swap(): lax.all_to_all(value, 'seq', split_axis=0, concat_axis=0, tiled=True, axi...  11.6 us
    ppermute x11, starting transfers between devices, across(): return lax.ppermute(value, 'seq', [(s, s ^ bits) for s in range(devices)])  10.6 us
    unnamed x36, local copies, waits for them, and re-layouts  4.22 us
    ppermute x11, waiting for transfers between devices, across(): return lax.ppermute(value, 'seq', [(s, s ^ bits) for s in range(devices)])  3.86 us
  transfers between devices with their start and end apart: 15, of which 6 were waited for; matrix products, arithmetic and copies ran while one was open for 3% of the time, Pallas kernels for 32%

profile of v1, /device:TPU:0, one launch (start us, length us, event | category | flops | bytes accessed | tf_op | source)
XLA Modules:
  0.0 171.6 jit_solution(15341733045787051283)
XLA Ops:
  7.3 1.4 reshape.46.chosen_ref
  8.6 2.8 %fetch.1.both_ref.rows_ref = bf16[1,128,1024]{2,1,0:T(8,128)(2,1)} custom-call(s32[1]{0:T(128)} %bitcast.own_ref, s32[32]{0:T(128)} %counts_ref.13, s32[32,64]{1,0:T(8,128)} %reshape.46.chosen_ref, bf16[512,1024]{1,0:T(8,128)(2,1)} %old_ref.2, bf16[512,1024]{1,0:T(8,128)(2,1)} %old_ref.3), custom_call_target="tpu_custom_call" | custom-call | bytes 9900000 | tf_op jit(solution)/shard_map/fetch/pallas_call | solution.py:979
  12.2 5.2 %prepare.1 = bf16[16,104,128]{2,1,0:T(8,128)(2,1)} custom-call(s32[1]{0:T(128)} %bitcast.own_ref, s32[32]{0:T(128)} %counts_ref.13, bf16[1,128,1024]{2,1,0:T(8,128)(2,1)} %fetch.1.both_ref.rows_ref, f32[3,1024]{1,0:T(4,128)} %maximum_convert_fusion.vectors_ref, bf16[1024,1024]{1,0:T(8,128)(2,1)} %wq_ref.3, bf16[1024,1024]{1,0:T(8,128)(2,1)} %wk_ref.3, ...), custom_call_target="tpu_custom_call" | custom-call | bytes 16500000 | tf_op jit(solution)/shard_map/prepare/pallas_call | solution.py:979
  17.4 25.2 %all_to_all.25.got_ref = bf16[16,104,128]{2,1,0:T(8,128)(2,1)S(1)} all-to-all(bf16[16,104,128]{2,1,0:T(8,128)(2,1)} %prepare.1), channel_id=1, replica_groups={{0,2,4,6,8,10,12,14,16,18,20,22,24,26,28,30},{1,3,5,7,9,11,13,15,17,19,..., dimensions={0} | all-to-all | bytes 851968 | tf_op jit(solution)/shard_map/all_to_all | solution.py:1023
  44.3 3.0 %attend.1 = (bf16[512,128]{1,0:T(8,128)(2,1)S(1)}, f32[512,128]{1,0:T(8,128)S(1)}, f32[4,256]{1,0:T(4,128)S(1)}, f32[8,128]{1,0:T(8,128)S(1)}) custom-call(bf16[16,104,128]{2,1,0:T(8,128)(2,1)S(1)} %all_to_all.25.got_ref, bf16[16,104,128]{2,1,0:T(8,128)(2,1)S(1)} %collective-permute-done.other_ref, f32[2,1024]{1,0:T(2,128)S(1)} %get-tuple-element.46.kpos_ref, ...), custom_call_target="tpu_custom_call" | custom-call | bytes 16500000 | tf_op jit(solution)/shard_map/attend/pallas_call | solution.py:979
  47.9 13.8 %all_to_all.26.got_ref = bf16[16,32,128]{2,1,0:T(8,128)(2,1)S(1)} all-to-all(bf16[16,32,128]{2,1,0:T(8,128)(2,1)S(1)} %bitcast.7), channel_id=1, replica_groups={{0,2,4,6,8,10,12,14,16,18,20,22,24,26,28,30},{1,3,5,7,9,11,13,15,17,19,..., dimensions={0} | all-to-all | bytes 262144 | tf_op jit(solution)/shard_map/all_to_all | solution.py:1023
  61.8 1.7 collective-permute-start.1
  64.5 1.7 %collective-permute-start.3 = (bf16[1,64,1024]{2,1,0:T(8,128)(2,1)S(1)}, bf16[1,64,1024]{2,1,0:T(8,128)(2,1)S(1)}, u32[]{:S(2)}, u32[]{:S(2)}) collective-permute-start(bf16[1,64,1024]{2,1,0:T(8,128)(2,1)S(1)} %unpack.1.mixed_ref), channel_id=1, source_target_pairs={{0,24},{1,25},{2,26},{3,27},{4,28},{5,29},{6,30},{7,31},{8,16},{9,... | collective-permute-start | bytes 393224 | tf_op jit(solution)/shard_map/ppermute | solution.py:1026
  66.3 14.4 %middle.1 = (bf16[16,72,128]{2,1,0:T(8,128)(2,1)}, bf16[64,1024]{1,0:T(8,128)(2,1)}, f32[64,1024]{1,0:T(8,128)}, f32[64,128]{1,0:T(8,128)}) custom-call(s32[1]{0:T(128)} %bitcast.own_ref, s32[32]{0:T(128)} %counts_ref.13, bf16[1,64,1024]{2,1,0:T(8,128)(2,1)} %copy-done.1, f32[8,128]{1,0:T(8,128)} %copy-done.5, bf16[1,128,1024]{2,1,0:T(8,128)(2,1)} %fetch.1.both_ref.rows_ref, ...), custom_call_target="tpu_custom_call" | custom-call | bytes 49500000 | tf_op jit(solution)/shard_map/middle/pallas_call | solution.py:979
  81.8 11.3 %all-to-all-start.2 = ((bf16[16,72,128]{2,1,0:T(8,128)(2,1)}), bf16[16,72,128]{2,1,0:T(8,128)(2,1)S(1)}, u32[]{:S(2)}, u32[]{:S(2)}) async-start(bf16[16,72,128]{2,1,0:T(8,128)(2,1)} %get-tuple-element.53), calls=%async_computation.2 | async-start | bytes 589824 | tf_op jit(solution)/shard_map/all_to_all | solution.py:1023
  93.2 1.9 %collective-permute-start.6 = (bf16[4,64,1024]{2,1,0:T(8,128)(2,1)S(1)}, bf16[4,64,1024]{2,1,0:T(8,128)(2,1)S(1)}, u32[]{:S(2)}, u32[]{:S(2)}) collective-permute-start(bf16[4,64,1024]{2,1,0:T(8,128)(2,1)S(1)} %pad_maximum_fusion.rest_1_), channel_id=1, source_target_pairs={{0,4},{1,5},{2,6},{3,7},{4,0},{5,1},{6,2},{7,3},{8,12},{9,13},{10,... | collective-permute-start | bytes 1572872 | tf_op jit(solution)/shard_map/ppermute | solution.py:1026
  95.1 1.5 collective-permute-start.5
  96.6 9.0 %all-to-all-done.2.grad_ref.got_ref = bf16[16,72,128]{2,1,0:T(8,128)(2,1)S(1)} async-done(((bf16[16,72,128]{2,1,0:T(8,128)(2,1)}), bf16[16,72,128]{2,1,0:T(8,128)(2,1)S(1)}, u32[]{:S(2)}, u32[]{:S(2)}) %all-to-all-start.2) | async-done | bytes 294944 | tf_op jit(solution)/shard_map/all_to_all | solution.py:1023
  105.6 3.7 %attend_back.1 = (bf16[512,128]{1,0:T(8,128)(2,1)S(1)}, f32[1024,128]{1,0:T(8,128)S(1)}, f32[1032,128]{1,0:T(8,128)S(1)}, f32[8,128]{1,0:T(8,128)S(1)}) custom-call(bf16[16,104,128]{2,1,0:T(8,128)(2,1)S(1)} %all_to_all.25.got_ref, bf16[16,104,128]{2,1,0:T(8,128)(2,1)S(1)} %collective-permute-done.other_ref, ...), custom_call_target="tpu_custom_call" | custom-call | bytes 19800000 | tf_op jit(solution)/shard_map/attend_back/pallas_call | solution.py:979
  110.4 1.2 collective-permute-start.8
  113.1 5.1 %all-to-all-start.3 = ((bf16[16,96,128]{2,1,0:T(8,128)(2,1)}), bf16[16,96,128]{2,1,0:T(8,128)(2,1)S(1)}, u32[]{:S(2)}, u32[]{:S(2)}) async-start(bf16[16,96,128]{2,1,0:T(8,128)(2,1)} %get-tuple-element.60.dqkv_ref), calls=%async_computation.3 | async-start | bytes 786432 | tf_op jit(solution)/shard_map/all_to_all | solution.py:1023
  119.6 15.7 %units.1 = (f32[128,1024]{1,0:T(8,128)}, bf16[128,1024]{1,0:T(8,128)(2,1)}, f32[16,136,128]{2,1,0:T(8,128)}, bf16[16,136,128]{2,1,0:T(8,128)(2,1)}) custom-call(s32[1]{0:T(128)} %bitcast.own_ref, s32[32]{0:T(128)} %counts_ref.13, bf16[16,72,128]{2,1,0:T(8,128)(2,1)} %copy-done, bf16[16,96,128]{2,1,0:T(8,128)(2,1)} %get-tuple-element.60.dqkv_ref, ...), custom_call_target="tpu_custom_call" | custom-call | bytes 52800000 | tf_op jit(solution)/shard_map/units/pallas_call | solution.py:1121
  135.9 2.0 %collective-permute-done.10.down_moved_ref = bf16[128,1024]{1,0:T(8,128)(2,1)S(1)} collective-permute-done((bf16[128,1024]{1,0:T(8,128)(2,1)}, bf16[128,1024]{1,0:T(8,128)(2,1)S(1)}, u32[]{:S(2)}, u32[]{:S(2)}) %collective-permute-start.10) | collective-permute-done | bytes 262176 | tf_op jit(solution)/shard_map/ppermute | solution.py:1026
  137.9 1.2 copy-done.2
  141.3 6.3 %all-to-all-start.4 = ((bf16[16,136,128]{2,1,0:T(8,128)(2,1)}), bf16[16,136,128]{2,1,0:T(8,128)(2,1)S(1)}, u32[]{:S(2)}, u32[]{:S(2)}) async-start(bf16[16,136,128]{2,1,0:T(8,128)(2,1)} %get-tuple-element.69), calls=%async_computation.4 | async-start | bytes 1114112 | tf_op jit(solution)/shard_map/all_to_all | solution.py:1023
  151.1 2.6 %put.1 = bf16[512,1024]{1,0:T(8,128)(2,1)} custom-call(s32[1]{0:T(128)} %bitcast.own_ref, s32[32]{0:T(128)} %counts_ref.13, s32[32,64]{1,0:T(8,128)} %reshape.46.chosen_ref, bf16[512,1024]{1,0:T(8,128)(2,1)} %old_ref.2, bf16[64,1024]{1,0:T(8,128)(2,1)} %get-tuple-element.51.new_ref), custom_call_target="tpu_custom_call" | custom-call | bytes 9900000 | tf_op jit(solution)/shard_map/put/pallas_call | solution.py:979
  153.7 7.3 %rows.1 = bf16[512,1024]{1,0:T(8,128)(2,1)} custom-call(s32[1]{0:T(128)} %bitcast.own_ref, s32[32]{0:T(128)} %counts_ref.13, s32[32,64]{1,0:T(8,128)} %reshape.46.chosen_ref, bf16[16,96,128]{2,1,0:T(8,128)(2,1)} %copy-done.9, bf16[1,128,1024]{2,1,0:T(8,128)(2,1)} %fetch.1.both_ref.rows_ref, f32[64,1024]{1,0:T(8,128)} %get-tuple-element.61.dmiddle_ref, ...), custom_call_target="tpu_custom_call" | custom-call | bytes 23100000 | tf_op jit(solution)/shard_map/rows/pallas_call | solution.py:979
  161.1 2.5 %all-to-all-done.4.got_ref = bf16[16,136,128]{2,1,0:T(8,128)(2,1)S(1)} async-done(((bf16[16,136,128]{2,1,0:T(8,128)(2,1)}), bf16[16,136,128]{2,1,0:T(8,128)(2,1)S(1)}, u32[]{:S(2)}, u32[]{:S(2)}) %all-to-all-start.4) | async-done | bytes 557088 | tf_op jit(solution)/shard_map/all_to_all | solution.py:1023
  163.6 1.2 finish.1
  (71 shorter events, 15.4 us)
Async XLA Ops:
  7.2 111.7 %all-gather.2.cloned.1.call-start = ((), (), s32[]{:S(2)}) async-start(), calls=%async_computation.5 | async-start | bytes 4456448 | tf_op jit(solution)/shard_map/all_gather | solution.py:1043
  12.1 30.4 %copy-start.17 = (s32[4]{0:T(128)S(1)}, s32[4]{0:T(128)}, u32[]{:S(2)}) copy-start(s32[4]{0:T(128)} %param.25) | copy-start | bytes 52
  12.1 30.4 %copy-start.4 = (s32[32,64]{1,0:T(8,128)S(1)}, s32[32,64]{1,0:T(8,128)}, u32[]{:S(2)}) copy-start(s32[32,64]{1,0:T(8,128)} %reshape.46.chosen_ref) | copy-start | bytes 24580
  12.2 30.4 %copy-start.6 = (s32[32]{0:T(128)S(1)}, s32[32]{0:T(128)}, u32[]{:S(2)}) copy-start(s32[32]{0:T(128)} %counts_ref.13) | copy-start | bytes 388
  42.5 1.8 %collective-permute-start = (bf16[16,104,128]{2,1,0:T(8,128)(2,1)S(1)}, bf16[16,104,128]{2,1,0:T(8,128)(2,1)S(1)}, u32[]{:S(2)}, u32[]{:S(2)}) collective-permute-start(bf16[16,104,128]{2,1,0:T(8,128)(2,1)S(1)} %all_to_all.25.got_ref), channel_id=1, source_target_pairs={{0,1},{1,0},{2,3},{3,2},{4,5},{5,4},{6,7},{7,6},{8,9},{9,8},{10,11... | collective-permute-start | bytes 1277960 | tf_op jit(solution)/shard_map/ppermute | solution.py:1026
  61.8 4.5 %copy-start.1 = (bf16[1,64,1024]{2,1,0:T(8,128)(2,1)}, bf16[1,64,1024]{2,1,0:T(8,128)(2,1)S(1)}, u32[]{:S(2)}) copy-start(bf16[1,64,1024]{2,1,0:T(8,128)(2,1)S(1)} %unpack.1.mixed_ref) | copy-start | bytes 393220
  61.8 18.8 %collective-permute-start.1 = (bf16[1,64,1024]{2,1,0:T(8,128)(2,1)S(1)}, bf16[1,64,1024]{2,1,0:T(8,128)(2,1)S(1)}, u32[]{:S(2)}, u32[]{:S(2)}) collective-permute-start(bf16[1,64,1024]{2,1,0:T(8,128)(2,1)S(1)} %unpack.1.mixed_ref), channel_id=1, source_target_pairs={{0,8},{1,9},{2,10},{3,11},{4,12},{5,13},{6,14},{7,15},{8,0},{9,1},... | collective-permute-start | bytes 393224 | tf_op jit(solution)/shard_map/ppermute | solution.py:1026
  63.5 17.3 %collective-permute-start.2 = (bf16[1,64,1024]{2,1,0:T(8,128)(2,1)S(1)}, bf16[1,64,1024]{2,1,0:T(8,128)(2,1)S(1)}, u32[]{:S(2)}, u32[]{:S(2)}) collective-permute-start(bf16[1,64,1024]{2,1,0:T(8,128)(2,1)S(1)} %unpack.1.mixed_ref), channel_id=1, source_target_pairs={{0,16},{1,17},{2,18},{3,19},{4,20},{5,21},{6,22},{7,23},{8,24},{9,... | collective-permute-start | bytes 393224 | tf_op jit(solution)/shard_map/ppermute | solution.py:1026
  64.5 16.3 %collective-permute-start.3 = (bf16[1,64,1024]{2,1,0:T(8,128)(2,1)S(1)}, bf16[1,64,1024]{2,1,0:T(8,128)(2,1)S(1)}, u32[]{:S(2)}, u32[]{:S(2)}) collective-permute-start(bf16[1,64,1024]{2,1,0:T(8,128)(2,1)S(1)} %unpack.1.mixed_ref), channel_id=1, source_target_pairs={{0,24},{1,25},{2,26},{3,27},{4,28},{5,29},{6,30},{7,31},{8,16},{9,... | collective-permute-start | bytes 393224 | tf_op jit(solution)/shard_map/ppermute | solution.py:1026
  81.8 30.7 %copy-start.8 = (bf16[4,64,1024]{2,1,0:T(8,128)(2,1)}, bf16[4,64,1024]{2,1,0:T(8,128)(2,1)S(1)}, u32[]{:S(2)}) copy-start(bf16[4,64,1024]{2,1,0:T(8,128)(2,1)S(1)} %pad_maximum_fusion.rest_1_) | copy-start | bytes 1572868
  81.8 23.8 %all-to-all-start.2 = ((bf16[16,72,128]{2,1,0:T(8,128)(2,1)}), bf16[16,72,128]{2,1,0:T(8,128)(2,1)S(1)}, u32[]{:S(2)}, u32[]{:S(2)}) async-start(bf16[16,72,128]{2,1,0:T(8,128)(2,1)} %get-tuple-element.53), calls=%async_computation.2 | async-start | bytes 589824 | tf_op jit(solution)/shard_map/all_to_all | solution.py:1023
  93.2 16.2 %collective-permute-start.6 = (bf16[4,64,1024]{2,1,0:T(8,128)(2,1)S(1)}, bf16[4,64,1024]{2,1,0:T(8,128)(2,1)S(1)}, u32[]{:S(2)}, u32[]{:S(2)}) collective-permute-start(bf16[4,64,1024]{2,1,0:T(8,128)(2,1)S(1)} %pad_maximum_fusion.rest_1_), channel_id=1, source_target_pairs={{0,4},{1,5},{2,6},{3,7},{4,0},{5,1},{6,2},{7,3},{8,12},{9,13},{10,... | collective-permute-start | bytes 1572872 | tf_op jit(solution)/shard_map/ppermute | solution.py:1026
  95.1 15.3 %collective-permute-start.5 = (bf16[4,64,1024]{2,1,0:T(8,128)(2,1)S(1)}, bf16[4,64,1024]{2,1,0:T(8,128)(2,1)S(1)}, u32[]{:S(2)}, u32[]{:S(2)}) collective-permute-start(bf16[4,64,1024]{2,1,0:T(8,128)(2,1)S(1)} %pad_maximum_fusion.rest_1_), channel_id=1, source_target_pairs={{0,2},{1,3},{2,0},{3,1},{4,6},{5,7},{6,4},{7,5},{8,10},{9,11},{10,... | collective-permute-start | bytes 1572872 | tf_op jit(solution)/shard_map/ppermute | solution.py:1026
  105.6 7.5 %copy-start = (bf16[16,72,128]{2,1,0:T(8,128)(2,1)}, bf16[16,72,128]{2,1,0:T(8,128)(2,1)S(1)}, u32[]{:S(2)}) copy-start(bf16[16,72,128]{2,1,0:T(8,128)(2,1)S(1)} %all-to-all-done.2.grad_ref.got_ref) | copy-start | bytes 884740
  109.3 2.3 %collective-permute-start.4 = (f32[1032,128]{1,0:T(8,128)S(1)}, f32[1032,128]{1,0:T(8,128)S(1)}, u32[]{:S(2)}, u32[]{:S(2)}) collective-permute-start(f32[1032,128]{1,0:T(8,128)S(1)} %get-tuple-element.58), channel_id=1, source_target_pairs={{0,1},{1,0},{2,3},{3,2},{4,5},{5,4},{6,7},{7,6},{8,9},{9,8},{10,11... | collective-permute-start | bytes 1585160 | tf_op jit(solution)/shard_map/ppermute | solution.py:1026
  109.4 9.5 %copy-start.10 = (bf16[4,64,1024]{2,1,0:T(8,128)(2,1)}, bf16[4,64,1024]{2,1,0:T(8,128)(2,1)S(1)}, u32[]{:S(2)}) copy-start(bf16[4,64,1024]{2,1,0:T(8,128)(2,1)S(1)} %collective-permute-done.6.rest_3_) | copy-start | bytes 1572868
  109.5 8.8 %collective-permute-start.7 = (bf16[2,64,1024]{2,1,0:T(8,128)(2,1)S(1)}, bf16[2,64,1024]{2,1,0:T(8,128)(2,1)S(1)}, u32[]{:S(2)}, u32[]{:S(2)}) collective-permute-start(bf16[2,64,1024]{2,1,0:T(8,128)(2,1)S(1)} %slice.8), channel_id=1, source_target_pairs={{0,2},{1,3},{2,0},{3,1},{4,6},{5,7},{6,4},{7,5},{8,10},{9,11},{10,... | collective-permute-start | bytes 786440 | tf_op jit(solution)/shard_map/ppermute | solution.py:1026
  110.4 8.5 %copy-start.11 = (bf16[4,64,1024]{2,1,0:T(8,128)(2,1)}, bf16[4,64,1024]{2,1,0:T(8,128)(2,1)S(1)}, u32[]{:S(2)}) copy-start(bf16[4,64,1024]{2,1,0:T(8,128)(2,1)S(1)} %collective-permute-done.5.rest_2_) | copy-start | bytes 1572868
  110.4 8.5 %collective-permute-start.8 = (bf16[2,64,1024]{2,1,0:T(8,128)(2,1)S(1)}, bf16[2,64,1024]{2,1,0:T(8,128)(2,1)S(1)}, u32[]{:S(2)}, u32[]{:S(2)}) collective-permute-start(bf16[2,64,1024]{2,1,0:T(8,128)(2,1)S(1)} %slice.9), channel_id=1, source_target_pairs={{0,4},{1,5},{2,6},{3,7},{4,0},{5,1},{6,2},{7,3},{8,12},{9,13},{10,... | collective-permute-start | bytes 786440 | tf_op jit(solution)/shard_map/ppermute | solution.py:1026
  113.1 28.2 %all-to-all-start.3 = ((bf16[16,96,128]{2,1,0:T(8,128)(2,1)}), bf16[16,96,128]{2,1,0:T(8,128)(2,1)S(1)}, u32[]{:S(2)}, u32[]{:S(2)}) async-start(bf16[16,96,128]{2,1,0:T(8,128)(2,1)} %get-tuple-element.60.dqkv_ref), calls=%async_computation.3 | async-start | bytes 786432 | tf_op jit(solution)/shard_map/all_to_all | solution.py:1023
  135.3 2.6 %collective-permute-start.9 = (bf16[16,136,128]{2,1,0:T(8,128)(2,1)}, bf16[16,136,128]{2,1,0:T(8,128)(2,1)S(1)}, u32[]{:S(2)}, u32[]{:S(2)}) collective-permute-start(bf16[16,136,128]{2,1,0:T(8,128)(2,1)} %get-tuple-element.66), channel_id=1, source_target_pairs={{0,1},{1,0},{2,3},{3,2},{4,5},{5,4},{6,7},{7,6},{8,9},{9,8},{10,11... | collective-permute-start | bytes 1671176 | tf_op jit(solution)/shard_map/ppermute | solution.py:1026
  135.4 2.5 %collective-permute-start.10 = (bf16[128,1024]{1,0:T(8,128)(2,1)}, bf16[128,1024]{1,0:T(8,128)(2,1)S(1)}, u32[]{:S(2)}, u32[]{:S(2)}) collective-permute-start(bf16[128,1024]{1,0:T(8,128)(2,1)} %get-tuple-element.68), channel_id=1, source_target_pairs={{0,1},{1,0},{2,3},{3,2},{4,5},{5,4},{6,7},{7,6},{8,9},{9,8},{10,11... | collective-permute-start | bytes 786440 | tf_op jit(solution)/shard_map/ppermute | solution.py:1026
  141.3 12.4 %copy-start.9 = (bf16[16,96,128]{2,1,0:T(8,128)(2,1)}, bf16[16,96,128]{2,1,0:T(8,128)(2,1)S(1)}, u32[]{:S(2)}) copy-start(bf16[16,96,128]{2,1,0:T(8,128)(2,1)S(1)} %all-to-all-done.3.got_ref) | copy-start | bytes 1179652
  141.3 22.3 %all-to-all-start.4 = ((bf16[16,136,128]{2,1,0:T(8,128)(2,1)}), bf16[16,136,128]{2,1,0:T(8,128)(2,1)S(1)}, u32[]{:S(2)}, u32[]{:S(2)}) async-start(bf16[16,136,128]{2,1,0:T(8,128)(2,1)} %get-tuple-element.69), calls=%async_computation.4 | async-start | bytes 1114112 | tf_op jit(solution)/shard_map/all_to_all | solution.py:1023
  (9 other events, 17.8 us)
Sparse Core Ops, SparseCore 0:
  11.6 91.3 all-gather.1

commit v2 on v1

--- a/solution.py
+++ b/solution.py
@@ -598,34 +598,47 @@
         qlow_ref[b : b + 1, :] = both[1:]
 
 
-def fetch_kernel(own_ref, counts_ref, chosen_ref, tokens_ref, grads_ref, both_ref):
+def fetch_kernel(own_ref, counts_ref, chosen_ref, tokens_ref, grads_ref, both_ref, rows_ref, upstream_ref):
     hot = one_hot(own_ref, counts_ref, chosen_ref, tokens_ref.shape[0], False)
     capacity = hot.shape[1]
     pick = jnp.transpose(jnp.concatenate([hot, jnp.zeros_like(hot)], axis=1))[:capacity].astype(bf16)
     live = live_column(own_ref, counts_ref, capacity)
-    both_ref[0, :capacity, :] = nn(pick, tokens_ref[...]).astype(bf16)
-    both_ref[0, capacity:, :] = jnp.where(live, nn(pick, grads_ref[...]), 0.0).astype(bf16)
-
-
-def prepare_kernel(own_ref, counts_ref, both_ref, vectors_ref, wq_ref, wk_ref, wv_ref, sent_ref, wq, wk, wv, sems):
-    copies = [
-        pltpu.make_async_copy(source, target, sems.at[i])
-        for i, (source, target) in enumerate(((wq_ref, wq), (wk_ref, wk), (wv_ref, wv)))
-    ]
-    for copy in copies:
-        copy.start()
-    capacity = both_ref.shape[1] // 2
-    rows = both_ref[0, :capacity, :].astype(f32)
-    live = live_column(own_ref, counts_ref, capacity)
-    gate_sum = jnp.sum(jnp.where(live, gate_of(rows, vectors_ref), 0.0), axis=0, keepdims=True)
-    write_note(sent_ref, HALF + SHARE, gate_sum)
-    normed = (rows * inverse_rms(rows) * vectors_ref[1:2, :]).astype(bf16)
-    copies[0].wait()
-    pack_rows(sent_ref, 0, nn(normed, wq[...]).astype(bf16))
-    copies[1].wait()
-    keys = nn(normed, wk[...]).astype(bf16)
-    copies[2].wait()
-    pack_pairs(sent_ref, HALF, keys, nn(normed, wv[...]).astype(bf16))
+    rows = nn(pick, tokens_ref[...]).astype(bf16)
+    upstream = jnp.where(live, nn(pick, grads_ref[...]), 0.0).astype(bf16)
+    both_ref[0, :capacity, :] = rows
+    both_ref[0, capacity:, :] = upstream
+    rows_ref[0] = rows
+    upstream_ref[0] = upstream
+
+
+def project_kernel(own_ref, counts_ref, vectors_ref, wq, wk, wv, *rest):
+    pieces, sent_ref = rest[:-1], rest[-1]
+    head = own_ref[0] // 2
+    core = own_ref[0] % 2
+    even = head % 2 == 0
+    k = 0
+    weights = None
+    for piece in pieces:
+        blocks, capacity, width = piece.shape
+        rows = piece[...].reshape(blocks * capacity, width).astype(f32)
+        gate = gate_of(rows, vectors_ref)
+        normed = (rows * inverse_rms(rows) * vectors_ref[1:2, :]).astype(bf16)
+        if weights is None:
+            w_pair = jnp.where(even, joined(wk[...], swapped(wv[...])), joined(swapped(wk[...]), wv[...]))
+            weights = jnp.concatenate([w_pair, jnp.where(even, wq[...], swapped(wq[...]))], axis=1)
+        product = nn(normed, weights)
+        for j in range(blocks):
+            chip = chip_of(own_ref, k)
+            block = product[j * capacity : (j + 1) * capacity]
+            query = block[:, LANES:]
+            sent_ref[chip, :HALF, :] = joined(query[:HALF], swapped(query[HALF:])).astype(bf16)
+            sent_ref[chip, HALF : HALF + SHARE, :] = block[:, :LANES].astype(bf16)
+            slot = lax.broadcasted_iota(jnp.int32, (capacity, 1), 0)
+            live = slot < counts_ref[2 * chip + core]
+            part = jnp.where(live, gate[j * capacity : (j + 1) * capacity], 0.0)
+            part = jnp.sum(part, axis=0, keepdims=True)
+            sent_ref[chip, HALF + SHARE :, :] = in_parts(jnp.broadcast_to(part, (NOTE, LANES)))
+            k += 1
 
 
 def unpack_kernel(got_ref, mixed_ref):
@@ -633,7 +646,7 @@
 
 
 CHUNKS = 4
-PIECES = 1
+PIECES = (5, 4, 5)
 
 
 def middle_kernel(
@@ -723,35 +736,30 @@
     own_ref, counts_ref, got_ref, dqkv_ref, total_ref, coef_ref, vectors_ref, rows_ref, dweight_ref,
     out_ref, up_ref, down_ref, *rest,
 ):
-    boths, mixeds, rest = rest[:PIECES], rest[PIECES : PIECES + 5], rest[PIECES + 5 :]
+    gathers = []
+    for count in PIECES:
+        gathers.append(rest[:count])
+        rest = rest[count:]
     down_keep_ref, down_give_ref, keep_ref, give_ref, rest = *rest[:4], rest[4:]
-    both, mixed_slots, grad_up, grad_down, grad_out, grad_q, grad_kv, ratio_ref, both_sems, mixed_sems = rest
+    *slots, grad_up, grad_down, grad_out, grad_q, grad_kv, ratio_ref, sems = rest
+    rows_slots, upstream_slots, mixed_slots = slots
     step = pl.program_id(0)
     steps = pl.num_programs(0)
-    _, sources, twice, width = both.shape
-    capacity = twice // 2
+    _, sources, capacity, width = mixed_slots.shape
     core = own_ref[0] % 2
     slot = step % 2
 
-    def both_copies(k, at):
-        if PIECES == 5:
-            return piece_copies(boths, both, both_sems, k)
-        return [
-            pltpu.make_async_copy(boths[0].at[chip_of(own_ref, 4 * k + j)], both.at[at, j], both_sems.at[at, j])
-            for j in range(4)
-        ]
-
-    def piece_copies(pieces, slots, sems, k):
+    def copies(k):
         at = k % 2
-        if k < 3:
-            return [pltpu.make_async_copy(pieces[k], slots.at[at], sems.at[at, 0])]
-        return [
-            pltpu.make_async_copy(pieces[k + half], slots.at[at, 2 * half : 2 * half + 2], sems.at[at, half])
-            for half in range(2)
-        ]
-
-    def copies(k):
-        return both_copies(k, k % 2) + piece_copies(mixeds, mixed_slots, mixed_sems, k)
+        result = []
+        for i, pieces in enumerate(gathers):
+            if k < 3 or len(pieces) == 4:
+                result.append(pltpu.make_async_copy(pieces[k], slots[i].at[at], sems.at[at, i, 0]))
+                continue
+            for half in range(2):
+                target = slots[i].at[at, 2 * half : 2 * half + 2]
+                result.append(pltpu.make_async_copy(pieces[k + half], target, sems.at[at, i, half]))
+        return result
 
     for k in range(4):
 
@@ -782,8 +790,8 @@
         value = value.reshape(sources, capacity, width)
         return value[:, :HALF, :].reshape(sources * HALF, width), value[:, HALF:, :].reshape(sources * HALF, width)
 
-    rows = both[slot, :, :capacity, :].reshape(sources * capacity, width).astype(f32)
-    upstream = both[slot, :, capacity:, :].reshape(sources * capacity, width).astype(f32)
+    rows = rows_slots[slot].reshape(sources * capacity, width).astype(f32)
+    upstream = upstream_slots[slot].reshape(sources * capacity, width).astype(f32)
     mixed = mixed_slots[slot].reshape(sources * capacity, width)
     normed_attn = (rows * inverse_rms(rows) * vectors_ref[1:2, :]).astype(bf16)
     low_query, high_query = halves(dqkv_ref, 0)
@@ -952,7 +960,7 @@
 smem = pl.BlockSpec(memory_space=pltpu.SMEM)
 hbm = pl.BlockSpec(memory_space=pl.ANY)
 megabytes = {
-    "places": 4, "fetch": 56, "prepare": 56, "attend": 20, "unpack": 4, "middle": 56, "put": 56, "attend_back": 24,
+    "places": 4, "fetch": 56, "project": 16, "attend": 20, "unpack": 4, "middle": 56, "put": 56, "attend_back": 24,
     "keys": 8, "units": 56, "merge": 10, "rows": 56, "finish": 12,
 }
 
@@ -966,7 +974,7 @@
 
 
 microseconds = {
-    "places": 1, "fetch": 3, "prepare": 5, "attend": 5, "unpack": 2, "middle": 15, "put": 3, "attend_back": 6, "keys": 2,
+    "places": 1, "fetch": 3, "project": 4, "attend": 5, "unpack": 2, "middle": 15, "put": 3, "attend_back": 6, "keys": 2,
     "units": 16, "merge": 3, "rows": 7, "finish": 2,
 }
 
@@ -1034,20 +1042,18 @@
     def gathered(sides):
         return sides + [across(sides[2][:2], 2), across(sides[1][2:], 4)]
 
+    def gathered_whole(sides):
+        return sides + [across(sides[2], 2)]
+
     blocks = chips * HALF // BLOCK
     square = pltpu.VMEM((width, width), bf16)
-    both = call(
-        fetch_kernel, "fetch", [smem, smem] + [vmem] * 3, shaped((1, 2 * capacity, width), bf16),
+    block = shaped((1, capacity, width), bf16)
+    both, own_rows, own_upstream = call(
+        fetch_kernel, "fetch", [smem, smem] + [vmem] * 3, (shaped((1, 2 * capacity, width), bf16), block, block),
         (own_id, counts, chosen, tokens_in, out_grad),
     )
-    both_all = [lax.all_gather(both[0], "seq", axis=0, axis_index_groups=cores)]
-    sent = call(
-        prepare_kernel, "prepare", [smem, smem] + [vmem] * 2 + [hbm] * 3,
-        shaped((chips, HALF + SHARE + NOTE, LANES), bf16),
-        (own_id, counts, both, vectors, w_query, w_key, w_value),
-        [square] * 3 + [pltpu.SemaphoreType.DMA((3,))],
-    )
-    chosen_after, _ = lax.optimization_barrier((chosen, sent))
+    rows_line = line_of(own_rows)
+    chosen_after, rows_line = lax.optimization_barrier((chosen, rows_line))
     kpos, qpos, qlow = call(
         places_kernel, "places", [smem] * 3 + [vmem],
         (
@@ -1057,8 +1063,19 @@
         ),
         (own_id, counts, jnp.append(lengths, tok_rows), chosen_after),
     )
-    got = swap(sent)
+    rows_all = gathered(sides_of(rows_line))
+    column = own // 4 * LANES
+    columns = [lax.dynamic_slice_in_dim(w, column, LANES, 1) for w in (w_query, w_key, w_value)]
+    upstream_line = line_of(own_upstream)
+    rows_all, upstream_line = lax.optimization_barrier((rows_all, upstream_line))
+    kpos, qpos, qlow, columns, rows_all = lax.optimization_barrier((kpos, qpos, qlow, columns, rows_all))
+    got = call(
+        project_kernel, "project", [smem, smem] + [vmem] * 9,
+        shaped((chips, HALF + SHARE + NOTE, LANES), bf16),
+        (own_id, counts, vectors, *columns, *rows_all),
+    )
     other = across(got, 1)
+    upstream_sides = sides_of(upstream_line)
     mixed_packed, turned, lse, total = call(
         functools.partial(pair_attend_kernel, factor), "attend", [vmem] * 5,
         (
@@ -1070,6 +1087,8 @@
         (got, other, kpos, qpos, qlow),
     )
     mixed_got = swap(mixed_packed.reshape(chips, HALF, LANES))
+    upstream_sides, mixed_got = lax.optimization_barrier((upstream_sides, mixed_got))
+    upstream_all = gathered_whole(upstream_sides)
     mixed = call(unpack_kernel, "unpack", [vmem], shaped((1, capacity, width), bf16), (mixed_got,))
     mixed_line = line_of(mixed)
     sent, new_rows, dmiddle, dweight = call(
@@ -1092,6 +1111,7 @@
     )
     mixed_line, sent = lax.optimization_barrier((mixed_line, sent))
     mixed_sides = sides_of(mixed_line)
+    upstream_all, sent = lax.optimization_barrier((upstream_all, sent))
     grads_got = swap(sent)
     mixed_all = gathered(mixed_sides)
     output = call(
@@ -1142,7 +1162,7 @@
                 pl.BlockSpec((width, hidden_cols), lambda i, o: (0, o[0] // 2)),
                 pl.BlockSpec((hidden_cols, width), lambda i, o: (o[0] // 2, 0)),
             ]
-            + [hbm] * (PIECES + 5),
+            + [hbm] * sum(PIECES),
             out_specs=(
                 whole(hidden_cols // 2, width),
                 whole(hidden_cols // 2, width),
@@ -1150,7 +1170,8 @@
                 whole(chips, GRAD_ROWS, LANES),
             ),
             scratch_shapes=[
-                pltpu.VMEM((2, sources, 2 * capacity, width), bf16),
+                pltpu.VMEM((2, sources, capacity, width), bf16),
+                pltpu.VMEM((2, sources, capacity, width), bf16),
                 pltpu.VMEM((2, sources, capacity, width), bf16),
                 pltpu.VMEM((hidden_cols, width), f32),
                 pltpu.VMEM((hidden_cols, width), f32),
@@ -1158,14 +1179,13 @@
                 pltpu.VMEM((HEAD_DIM, width), f32),
                 pltpu.VMEM((2 * HEAD_DIM, width), f32),
                 pltpu.VMEM((8, LANES), f32),
-                pltpu.SemaphoreType.DMA((2, 4)),
-                pltpu.SemaphoreType.DMA((2, 2)),
+                pltpu.SemaphoreType.DMA((2, 3, 2)),
             ],
         ),
         compiler_params=params_of("units"),
         cost_estimate=cost_of("units"),
         name="units",
-    )(own_id, counts, grads_got, dqkv, total, coef, vectors, both, dweight, w_out, w_up, w_down, *both_all, *mixed_all)
+    )(own_id, counts, grads_got, dqkv, total, coef, vectors, both, dweight, w_out, w_up, w_down, *rows_all, *upstream_all, *mixed_all)
     sent, grad_down = call(
         merge_kernel, "merge", [vmem] * 4,
         (shaped((chips, GRAD_ROWS, LANES), bf16), shaped((hidden_cols // 2, width), f32)),

time: 173 us -> 161 us (0.931)
  blocking collectives: 39 us -> 0 us
  waiting for transfers between devices: 15.4 us -> 39.1 us
  starting transfers between devices: 33.5 us -> 50 us
  between operations: 14.3 us -> 1.11 us
  Pallas kernels: 58.7 us -> 55.9 us
  local copies, waits for them, and re-layouts: 9.09 us -> 11.7 us
    all_to_all x2 -> x0, blocking collectives: 39 us -> none  [swap(): lax.all_to_all(value, 'seq', split_axis=0, concat_axis=0, tiled=True, axi...]
    ppermute x11 -> x24, waiting for transfers between devices: 3.86 us -> 28.4 us  [across(): return lax.ppermute(value, 'seq', [(s, s ^ bits) for s in range(devices)])]
    ppermute x11 -> x24, starting transfers between devices: 10.6 us -> 28.9 us  [across(): return lax.ppermute(value, 'seq', [(s, s ^ bits) for s in range(devices)])]
    pallas_call x12, Pallas kernels: 43 us -> 40.6 us  [call(): pl.pallas_call(kernel, out_shape=out_shape, in_specs=in_specs, out_specs=...]
    dynamic_slice x0 -> x2, local copies, waits for them, and re-layouts: none -> 2.05 us  [pairs(): lax.dynamic_slice_in_dim(w, column, LANES, 1)]
    all_to_all x3 -> x4, starting transfers between devices: 22.8 us -> 21.1 us  [swap(): lax.all_to_all(value, 'seq', split_axis=0, concat_axis=0, tiled=True, axi...]
    all_to_all x3 -> x4, waiting for transfers between devices: 11.6 us -> 10.7 us  [swap(): lax.all_to_all(value, 'seq', split_axis=0, concat_axis=0, tiled=True, axi...]
    unnamed x36 -> x54, local copies, waits for them, and re-layouts: 4.22 us -> 3.77 us
  transfers between devices with their start and end apart: 15 -> 28, of which waited for: 6 -> 14; matrix products, arithmetic and copies ran while one was open for 3% -> 5% of each run, Pallas kernels for 32% -> 31%
where the time goes in v2:
time: 161 us; the launch traced here: 160 us
  Pallas kernels  55.9 us (35%)
  starting transfers between devices  50 us (31%)
  waiting for transfers between devices  39.1 us (24%)
  local copies, waits for them, and re-layouts  11.7 us (7%)
  other arithmetic  2.11 us (1%)
    pallas_call x12, Pallas kernels, call(): pl.pallas_call(kernel, out_shape=out_shape, in_specs=in_specs, out_specs=...  40.6 us
    ppermute x24, starting transfers between devices, across(): return lax.ppermute(value, 'seq', [(s, s ^ bits) for s in range(devices)])  28.9 us
    ppermute x24, waiting for transfers between devices, across(): return lax.ppermute(value, 'seq', [(s, s ^ bits) for s in range(devices)])  28.4 us
    all_to_all x4, starting transfers between devices, swap(): lax.all_to_all(value, 'seq', split_axis=0, concat_axis=0, tiled=True, axi...  21.1 us
    pallas_call x1, Pallas kernels, pairs(): pl.pallas_call(units_kernel, out_shape=(shaped((hidden_cols // 2, width),...  15.2 us
    all_to_all x4, waiting for transfers between devices, swap(): lax.all_to_all(value, 'seq', split_axis=0, concat_axis=0, tiled=True, axi...  10.7 us
    unnamed x54, local copies, waits for them, and re-layouts  3.77 us
  transfers between devices with their start and end apart: 28, of which 14 were waited for; matrix products, arithmetic and copies ran while one was open for 5% of the time, Pallas kernels for 31%

profile of v2, /device:TPU:0, one launch (start us, length us, event | category | flops | bytes accessed | tf_op | source)
XLA Modules:
  0.0 159.9 jit_solution(16562022443266480647)
XLA Ops:
  2.1 2.8 %fetch.1 = (bf16[1,128,1024]{2,1,0:T(8,128)(2,1)}, bf16[1,64,1024]{2,1,0:T(8,128)(2,1)}, bf16[1,64,1024]{2,1,0:T(8,128)(2,1)}) custom-call(s32[1]{0:T(128)} %bitcast.own_ref, s32[32]{0:T(128)} %counts_ref.13, s32[32,64]{1,0:T(8,128)} %reshape.46.chosen_ref, bf16[512,1024]{1,0:T(8,128)(2,1)} %old_ref.2, bf16[512,1024]{1,0:T(8,128)(2,1)} %old_ref.3), custom_call_target="tpu_custom_call" | custom-call | bytes 9900000 | tf_op jit(solution)/shard_map/fetch/pallas_call | solution.py:987
  4.9 3.1 %collective-permute-start = (bf16[1,64,1024]{2,1,0:T(8,128)(2,1)}, bf16[1,64,1024]{2,1,0:T(8,128)(2,1)S(1)}, u32[]{:S(2)}, u32[]{:S(2)}) collective-permute-start(bf16[1,64,1024]{2,1,0:T(8,128)(2,1)} %get-tuple-element.75), channel_id=1, source_target_pairs={{0,8},{1,9},{2,10},{3,11},{4,12},{5,13},{6,14},{7,15},{8,0},{9,1},... | collective-permute-start | bytes 393224 | tf_op jit(solution)/shard_map/ppermute | solution.py:1034
  8.0 2.6 %collective-permute-start.1 = (bf16[1,64,1024]{2,1,0:T(8,128)(2,1)}, bf16[1,64,1024]{2,1,0:T(8,128)(2,1)S(1)}, u32[]{:S(2)}, u32[]{:S(2)}) collective-permute-start(bf16[1,64,1024]{2,1,0:T(8,128)(2,1)} %get-tuple-element.75), channel_id=1, source_target_pairs={{0,16},{1,17},{2,18},{3,19},{4,20},{5,21},{6,22},{7,23},{8,24},{9,... | collective-permute-start | bytes 393224 | tf_op jit(solution)/shard_map/ppermute | solution.py:1034
  10.6 2.6 %collective-permute-done = bf16[1,64,1024]{2,1,0:T(8,128)(2,1)S(1)} collective-permute-done((bf16[1,64,1024]{2,1,0:T(8,128)(2,1)}, bf16[1,64,1024]{2,1,0:T(8,128)(2,1)S(1)}, u32[]{:S(2)}, u32[]{:S(2)}) %collective-permute-start) | collective-permute-done | bytes 131104 | tf_op jit(solution)/shard_map/ppermute | solution.py:1034
  13.3 7.9 %collective-permute-done.1 = bf16[1,64,1024]{2,1,0:T(8,128)(2,1)S(1)} collective-permute-done((bf16[1,64,1024]{2,1,0:T(8,128)(2,1)}, bf16[1,64,1024]{2,1,0:T(8,128)(2,1)S(1)}, u32[]{:S(2)}, u32[]{:S(2)}) %collective-permute-start.1) | collective-permute-done | bytes 131104 | tf_op jit(solution)/shard_map/ppermute | solution.py:1034
  30.7 2.7 %collective-permute-done.4.rest_2_ = bf16[4,64,1024]{2,1,0:T(8,128)(2,1)S(1)} collective-permute-done((bf16[4,64,1024]{2,1,0:T(8,128)(2,1)S(1)}, bf16[4,64,1024]{2,1,0:T(8,128)(2,1)S(1)}, u32[]{:S(2)}, u32[]{:S(2)}) %collective-permute-start.4) | collective-permute-done | bytes 524320 | tf_op jit(solution)/shard_map/ppermute | solution.py:1034
  40.3 2.9 %collective-permute-done.6.rest_4_ = bf16[2,64,1024]{2,1,0:T(8,128)(2,1)S(1)} collective-permute-done((bf16[2,64,1024]{2,1,0:T(8,128)(2,1)S(1)}, bf16[2,64,1024]{2,1,0:T(8,128)(2,1)S(1)}, u32[]{:S(2)}, u32[]{:S(2)}) %collective-permute-start.6) | collective-permute-done | bytes 262176 | tf_op jit(solution)/shard_map/ppermute | solution.py:1034
  43.2 2.2 %project.1.got_ref = bf16[16,104,128]{2,1,0:T(8,128)(2,1)S(1)} custom-call(s32[1]{0:T(128)} %bitcast.own_ref, s32[32]{0:T(128)S(1)} %copy-done.12, f32[3,1024]{1,0:T(4,128)S(1)} %maximum_convert_fusion.vectors_ref, bf16[1024,128]{1,0:T(8,128)(2,1)S(1)} %constant_dynamic-slice_fusion.7.wq, bf16[1024,128]{1,0:T(8,128)(2,1)S(1)} %get-tuple-element.89.wk, ...), custom_call_target="tpu_custom_call" | custom-call | bytes 13200000 | tf_op jit(solution)/shard_map/project/pallas_call | solution.py:987
  47.2 3.7 %attend.1 = (bf16[512,128]{1,0:T(8,128)(2,1)}, f32[512,128]{1,0:T(8,128)S(1)}, f32[4,256]{1,0:T(4,128)S(1)}, f32[8,128]{1,0:T(8,128)S(1)}) custom-call(bf16[16,104,128]{2,1,0:T(8,128)(2,1)S(1)} %project.1.got_ref, bf16[16,104,128]{2,1,0:T(8,128)(2,1)S(1)} %collective-permute-done.12.other_ref, f32[2,1024]{1,0:T(2,128)S(1)} %get-tuple-element.96.kpos_ref, ...), custom_call_target="tpu_custom_call" | custom-call | bytes 16500000 | tf_op jit(solution)/shard_map/attend/pallas_call | solution.py:987
  50.9 5.6 %all-to-all-start = ((bf16[16,32,128]{2,1,0:T(8,128)(2,1)}), bf16[16,32,128]{2,1,0:T(8,128)(2,1)S(1)}, u32[]{:S(2)}, u32[]{:S(2)}) async-start(bf16[16,32,128]{2,1,0:T(8,128)(2,1)} %bitcast.1), calls=%async_computation | async-start | bytes 262144 | tf_op jit(solution)/shard_map/all_to_all | solution.py:1031
  56.6 3.4 %collective-permute-done.10.rest_6_ = bf16[4,64,1024]{2,1,0:T(8,128)(2,1)S(1)} collective-permute-done((bf16[4,64,1024]{2,1,0:T(8,128)(2,1)S(1)}, bf16[4,64,1024]{2,1,0:T(8,128)(2,1)S(1)}, u32[]{:S(2)}, u32[]{:S(2)}) %collective-permute-start.10) | collective-permute-done | bytes 524320 | tf_op jit(solution)/shard_map/ppermute | solution.py:1034
  61.6 2.7 %all-to-all-done.got_ref = bf16[16,32,128]{2,1,0:T(8,128)(2,1)S(1)} async-done(((bf16[16,32,128]{2,1,0:T(8,128)(2,1)}), bf16[16,32,128]{2,1,0:T(8,128)(2,1)S(1)}, u32[]{:S(2)}, u32[]{:S(2)}) %all-to-all-start) | async-done | bytes 131104 | tf_op jit(solution)/shard_map/all_to_all | solution.py:1031
  67.0 3.0 %collective-permute-start.16 = (bf16[1,64,1024]{2,1,0:T(8,128)(2,1)S(1)}, bf16[1,64,1024]{2,1,0:T(8,128)(2,1)S(1)}, u32[]{:S(2)}, u32[]{:S(2)}) collective-permute-start(bf16[1,64,1024]{2,1,0:T(8,128)(2,1)S(1)} %unpack.1.mixed_ref), channel_id=1, source_target_pairs={{0,24},{1,25},{2,26},{3,27},{4,28},{5,29},{6,30},{7,31},{8,16},{9,... | collective-permute-start | bytes 393224 | tf_op jit(solution)/shard_map/ppermute | solution.py:1034
  70.0 14.3 %middle.1 = (bf16[16,72,128]{2,1,0:T(8,128)(2,1)}, bf16[64,1024]{1,0:T(8,128)(2,1)}, f32[64,1024]{1,0:T(8,128)}, f32[64,128]{1,0:T(8,128)}) custom-call(s32[1]{0:T(128)} %bitcast.own_ref, s32[32]{0:T(128)} %counts_ref.13, bf16[1,64,1024]{2,1,0:T(8,128)(2,1)} %copy-done.4, f32[8,128]{1,0:T(8,128)} %copy-done.11, ...), custom_call_target="tpu_custom_call" | custom-call | bytes 49500000 | tf_op jit(solution)/shard_map/middle/pallas_call | solution.py:987
  85.3 3.5 %all-to-all-start.1 = ((bf16[16,72,128]{2,1,0:T(8,128)(2,1)}), bf16[16,72,128]{2,1,0:T(8,128)(2,1)S(1)}, u32[]{:S(2)}, u32[]{:S(2)}) async-start(bf16[16,72,128]{2,1,0:T(8,128)(2,1)} %get-tuple-element.109), calls=%async_computation.1 | async-start | bytes 589824 | tf_op jit(solution)/shard_map/all_to_all | solution.py:1031
  92.2 5.5 %all-to-all-done.1.grad_ref.got_ref = bf16[16,72,128]{2,1,0:T(8,128)(2,1)S(1)} async-done(((bf16[16,72,128]{2,1,0:T(8,128)(2,1)}), bf16[16,72,128]{2,1,0:T(8,128)(2,1)S(1)}, u32[]{:S(2)}, u32[]{:S(2)}) %all-to-all-start.1) | async-done | bytes 294944 | tf_op jit(solution)/shard_map/all_to_all | solution.py:1031
  97.7 3.8 %attend_back.1 = (bf16[512,128]{1,0:T(8,128)(2,1)S(1)}, f32[1024,128]{1,0:T(8,128)S(1)}, f32[1032,128]{1,0:T(8,128)S(1)}, f32[8,128]{1,0:T(8,128)S(1)}) custom-call(bf16[16,104,128]{2,1,0:T(8,128)(2,1)S(1)} %project.1.got_ref, bf16[16,104,128]{2,1,0:T(8,128)(2,1)S(1)} %collective-permute-done.12.other_ref, ...), custom_call_target="tpu_custom_call" | custom-call | bytes 19800000 | tf_op jit(solution)/shard_map/attend_back/pallas_call | solution.py:987
  108.7 5.0 %all-to-all-start.2 = ((bf16[16,96,128]{2,1,0:T(8,128)(2,1)}), bf16[16,96,128]{2,1,0:T(8,128)(2,1)S(1)}, u32[]{:S(2)}, u32[]{:S(2)}) async-start(bf16[16,96,128]{2,1,0:T(8,128)(2,1)} %get-tuple-element.116.dqkv_ref), calls=%async_computation.2 | async-start | bytes 786432 | tf_op jit(solution)/shard_map/all_to_all | solution.py:1031
  114.6 15.2 %units.1 = (f32[128,1024]{1,0:T(8,128)}, bf16[128,1024]{1,0:T(8,128)(2,1)}, f32[16,136,128]{2,1,0:T(8,128)}, bf16[16,136,128]{2,1,0:T(8,128)(2,1)}) custom-call(s32[1]{0:T(128)} %bitcast.own_ref, s32[32]{0:T(128)} %counts_ref.13, bf16[16,72,128]{2,1,0:T(8,128)(2,1)} %copy-done.3, bf16[16,96,128]{2,1,0:T(8,128)(2,1)} %get-tuple-element.116.dqkv_ref, ...), custom_call_target="tpu_custom_call" | custom-call | bytes 52800000 | tf_op jit(solution)/shard_map/units/pallas_call | solution.py:1141
  130.4 2.0 %collective-permute-done.23.down_moved_ref = bf16[128,1024]{1,0:T(8,128)(2,1)S(1)} collective-permute-done((bf16[128,1024]{1,0:T(8,128)(2,1)}, bf16[128,1024]{1,0:T(8,128)(2,1)S(1)}, u32[]{:S(2)}, u32[]{:S(2)}) %collective-permute-start.23) | collective-permute-done | bytes 262176 | tf_op jit(solution)/shard_map/ppermute | solution.py:1034
  135.8 6.9 %all-to-all-start.3 = ((bf16[16,136,128]{2,1,0:T(8,128)(2,1)}), bf16[16,136,128]{2,1,0:T(8,128)(2,1)S(1)}, u32[]{:S(2)}, u32[]{:S(2)}) async-start(bf16[16,136,128]{2,1,0:T(8,128)(2,1)} %get-tuple-element.129), calls=%async_computation.3 | async-start | bytes 1114112 | tf_op jit(solution)/shard_map/all_to_all | solution.py:1031
  146.2 2.6 %put.1 = bf16[512,1024]{1,0:T(8,128)(2,1)} custom-call(s32[1]{0:T(128)} %bitcast.own_ref, s32[32]{0:T(128)} %counts_ref.13, s32[32,64]{1,0:T(8,128)} %reshape.46.chosen_ref, bf16[512,1024]{1,0:T(8,128)(2,1)} %old_ref.2, bf16[64,1024]{1,0:T(8,128)(2,1)} %get-tuple-element.103.new_ref), custom_call_target="tpu_custom_call" | custom-call | bytes 9900000 | tf_op jit(solution)/shard_map/put/pallas_call | solution.py:987
  148.8 7.3 %rows.1 = bf16[512,1024]{1,0:T(8,128)(2,1)} custom-call(s32[1]{0:T(128)} %bitcast.own_ref, s32[32]{0:T(128)} %counts_ref.13, s32[32,64]{1,0:T(8,128)} %reshape.46.chosen_ref, bf16[16,96,128]{2,1,0:T(8,128)(2,1)} %copy-done.16, bf16[1,128,1024]{2,1,0:T(8,128)(2,1)} %get-tuple-element.102.both_ref.rows_ref, f32[64,1024]{1,0:T(8,128)} %get-tuple-element.117.dmiddle_ref, ...), custom_call_target="tpu_custom_call" | custom-call | bytes 23100000 | tf_op jit(solution)/shard_map/rows/pallas_call | solution.py:987
  156.2 2.5 %all-to-all-done.3.got_ref = bf16[16,136,128]{2,1,0:T(8,128)(2,1)S(1)} async-done(((bf16[16,136,128]{2,1,0:T(8,128)(2,1)}), bf16[16,136,128]{2,1,0:T(8,128)(2,1)S(1)}, u32[]{:S(2)}, u32[]{:S(2)}) %all-to-all-start.3) | async-done | bytes 557088 | tf_op jit(solution)/shard_map/all_to_all | solution.py:1031
  (118 shorter events, 44.6 us)
Async XLA Ops:
  4.9 8.3 %collective-permute-start = (bf16[1,64,1024]{2,1,0:T(8,128)(2,1)}, bf16[1,64,1024]{2,1,0:T(8,128)(2,1)S(1)}, u32[]{:S(2)}, u32[]{:S(2)}) collective-permute-start(bf16[1,64,1024]{2,1,0:T(8,128)(2,1)} %get-tuple-element.75), channel_id=1, source_target_pairs={{0,8},{1,9},{2,10},{3,11},{4,12},{5,13},{6,14},{7,15},{8,0},{9,1},... | collective-permute-start | bytes 393224 | tf_op jit(solution)/shard_map/ppermute | solution.py:1034
  8.0 13.2 %collective-permute-start.1 = (bf16[1,64,1024]{2,1,0:T(8,128)(2,1)}, bf16[1,64,1024]{2,1,0:T(8,128)(2,1)S(1)}, u32[]{:S(2)}, u32[]{:S(2)}) collective-permute-start(bf16[1,64,1024]{2,1,0:T(8,128)(2,1)} %get-tuple-element.75), channel_id=1, source_target_pairs={{0,16},{1,17},{2,18},{3,19},{4,20},{5,21},{6,22},{7,23},{8,24},{9,... | collective-permute-start | bytes 393224 | tf_op jit(solution)/shard_map/ppermute | solution.py:1034
  10.6 10.6 %collective-permute-start.2 = (bf16[1,64,1024]{2,1,0:T(8,128)(2,1)}, bf16[1,64,1024]{2,1,0:T(8,128)(2,1)S(1)}, u32[]{:S(2)}, u32[]{:S(2)}) collective-permute-start(bf16[1,64,1024]{2,1,0:T(8,128)(2,1)} %get-tuple-element.75), channel_id=1, source_target_pairs={{0,24},{1,25},{2,26},{3,27},{4,28},{5,29},{6,30},{7,31},{8,16},{9,... | collective-permute-start | bytes 393224 | tf_op jit(solution)/shard_map/ppermute | solution.py:1034
  22.2 11.3 %collective-permute-start.4 = (bf16[4,64,1024]{2,1,0:T(8,128)(2,1)S(1)}, bf16[4,64,1024]{2,1,0:T(8,128)(2,1)S(1)}, u32[]{:S(2)}, u32[]{:S(2)}) collective-permute-start(bf16[4,64,1024]{2,1,0:T(8,128)(2,1)S(1)} %pad_maximum_fusion.rest_0_), channel_id=1, source_target_pairs={{0,4},{1,5},{2,6},{3,7},{4,0},{5,1},{6,2},{7,3},{8,12},{9,13},{10,... | collective-permute-start | bytes 1572872 | tf_op jit(solution)/shard_map/ppermute | solution.py:1034
  23.7 13.0 %collective-permute-start.3 = (bf16[4,64,1024]{2,1,0:T(8,128)(2,1)S(1)}, bf16[4,64,1024]{2,1,0:T(8,128)(2,1)S(1)}, u32[]{:S(2)}, u32[]{:S(2)}) collective-permute-start(bf16[4,64,1024]{2,1,0:T(8,128)(2,1)S(1)} %pad_maximum_fusion.rest_0_), channel_id=1, source_target_pairs={{0,2},{1,3},{2,0},{3,1},{4,6},{5,7},{6,4},{7,5},{8,10},{9,11},{10,... | collective-permute-start | bytes 1572872 | tf_op jit(solution)/shard_map/ppermute | solution.py:1034
  25.2 13.7 %collective-permute-start.7 = (bf16[1,64,1024]{2,1,0:T(8,128)(2,1)}, bf16[1,64,1024]{2,1,0:T(8,128)(2,1)S(1)}, u32[]{:S(2)}, u32[]{:S(2)}) collective-permute-start(bf16[1,64,1024]{2,1,0:T(8,128)(2,1)} %get-tuple-element.77), channel_id=1, source_target_pairs={{0,8},{1,9},{2,10},{3,11},{4,12},{5,13},{6,14},{7,15},{8,0},{9,1},... | collective-permute-start | bytes 393224 | tf_op jit(solution)/shard_map/ppermute | solution.py:1034
  27.2 11.7 %collective-permute-start.8 = (bf16[1,64,1024]{2,1,0:T(8,128)(2,1)}, bf16[1,64,1024]{2,1,0:T(8,128)(2,1)S(1)}, u32[]{:S(2)}, u32[]{:S(2)}) collective-permute-start(bf16[1,64,1024]{2,1,0:T(8,128)(2,1)} %get-tuple-element.77), channel_id=1, source_target_pairs={{0,16},{1,17},{2,18},{3,19},{4,20},{5,21},{6,22},{7,23},{8,24},{9,... | collective-permute-start | bytes 393224 | tf_op jit(solution)/shard_map/ppermute | solution.py:1034
  28.2 10.8 %collective-permute-start.9 = (bf16[1,64,1024]{2,1,0:T(8,128)(2,1)}, bf16[1,64,1024]{2,1,0:T(8,128)(2,1)S(1)}, u32[]{:S(2)}, u32[]{:S(2)}) collective-permute-start(bf16[1,64,1024]{2,1,0:T(8,128)(2,1)} %get-tuple-element.77), channel_id=1, source_target_pairs={{0,24},{1,25},{2,26},{3,27},{4,28},{5,29},{6,30},{7,31},{8,16},{9,... | collective-permute-start | bytes 393224 | tf_op jit(solution)/shard_map/ppermute | solution.py:1034
  33.4 6.8 %collective-permute-start.5 = (bf16[2,64,1024]{2,1,0:T(8,128)(2,1)S(1)}, bf16[2,64,1024]{2,1,0:T(8,128)(2,1)S(1)}, u32[]{:S(2)}, u32[]{:S(2)}) collective-permute-start(bf16[2,64,1024]{2,1,0:T(8,128)(2,1)S(1)} %slice.16), channel_id=1, source_target_pairs={{0,2},{1,3},{2,0},{3,1},{4,6},{5,7},{6,4},{7,5},{8,10},{9,11},{10,... | collective-permute-start | bytes 786440 | tf_op jit(solution)/shard_map/ppermute | solution.py:1034
  36.7 6.4 %collective-permute-start.6 = (bf16[2,64,1024]{2,1,0:T(8,128)(2,1)S(1)}, bf16[2,64,1024]{2,1,0:T(8,128)(2,1)S(1)}, u32[]{:S(2)}, u32[]{:S(2)}) collective-permute-start(bf16[2,64,1024]{2,1,0:T(8,128)(2,1)S(1)} %slice.17), channel_id=1, source_target_pairs={{0,4},{1,5},{2,6},{3,7},{4,0},{5,1},{6,2},{7,3},{8,12},{9,13},{10,... | collective-permute-start | bytes 786440 | tf_op jit(solution)/shard_map/ppermute | solution.py:1034
  45.5 14.5 %collective-permute-start.10 = (bf16[4,64,1024]{2,1,0:T(8,128)(2,1)S(1)}, bf16[4,64,1024]{2,1,0:T(8,128)(2,1)S(1)}, u32[]{:S(2)}, u32[]{:S(2)}) collective-permute-start(bf16[4,64,1024]{2,1,0:T(8,128)(2,1)S(1)} %pad_maximum_fusion.1.rest_5_), channel_id=1, source_target_pairs={{0,2},{1,3},{2,0},{3,1},{4,6},{5,7},{6,4},{7,5},{8,10},{9,11},{10,... | collective-permute-start | bytes 1572872 | tf_op jit(solution)/shard_map/ppermute | solution.py:1034
  47.0 14.6 %collective-permute-start.11 = (bf16[4,64,1024]{2,1,0:T(8,128)(2,1)S(1)}, bf16[4,64,1024]{2,1,0:T(8,128)(2,1)S(1)}, u32[]{:S(2)}, u32[]{:S(2)}) collective-permute-start(bf16[4,64,1024]{2,1,0:T(8,128)(2,1)S(1)} %pad_maximum_fusion.1.rest_5_), channel_id=1, source_target_pairs={{0,4},{1,5},{2,6},{3,7},{4,0},{5,1},{6,2},{7,3},{8,12},{9,13},{10,... | collective-permute-start | bytes 1572872 | tf_op jit(solution)/shard_map/ppermute | solution.py:1034
  50.9 13.4 %all-to-all-start = ((bf16[16,32,128]{2,1,0:T(8,128)(2,1)}), bf16[16,32,128]{2,1,0:T(8,128)(2,1)S(1)}, u32[]{:S(2)}, u32[]{:S(2)}) async-start(bf16[16,32,128]{2,1,0:T(8,128)(2,1)} %bitcast.1), calls=%async_computation | async-start | bytes 262144 | tf_op jit(solution)/shard_map/all_to_all | solution.py:1031
  64.4 21.0 %collective-permute-start.13 = (bf16[4,64,1024]{2,1,0:T(8,128)(2,1)S(1)}, bf16[4,64,1024]{2,1,0:T(8,128)(2,1)}, u32[]{:S(2)}, u32[]{:S(2)}) collective-permute-start(bf16[4,64,1024]{2,1,0:T(8,128)(2,1)S(1)} %collective-permute-done.11.rest_7_), channel_id=1, source_target_pairs={{0,2},{1,3},{2,0},{3,1},{4,6},{5,7},{6,4},{7,5},{8,10},{9,11},{10,... | collective-permute-start | bytes 1572872 | tf_op jit(solution)/shard_map/ppermute | solution.py:1034
  65.6 18.7 %collective-permute-start.14 = (bf16[1,64,1024]{2,1,0:T(8,128)(2,1)S(1)}, bf16[1,64,1024]{2,1,0:T(8,128)(2,1)S(1)}, u32[]{:S(2)}, u32[]{:S(2)}) collective-permute-start(bf16[1,64,1024]{2,1,0:T(8,128)(2,1)S(1)} %unpack.1.mixed_ref), channel_id=1, source_target_pairs={{0,8},{1,9},{2,10},{3,11},{4,12},{5,13},{6,14},{7,15},{8,0},{9,1},... | collective-permute-start | bytes 393224 | tf_op jit(solution)/shard_map/ppermute | solution.py:1034
  65.9 18.5 %collective-permute-start.15 = (bf16[1,64,1024]{2,1,0:T(8,128)(2,1)S(1)}, bf16[1,64,1024]{2,1,0:T(8,128)(2,1)S(1)}, u32[]{:S(2)}, u32[]{:S(2)}) collective-permute-start(bf16[1,64,1024]{2,1,0:T(8,128)(2,1)S(1)} %unpack.1.mixed_ref), channel_id=1, source_target_pairs={{0,16},{1,17},{2,18},{3,19},{4,20},{5,21},{6,22},{7,23},{8,24},{9,... | collective-permute-start | bytes 393224 | tf_op jit(solution)/shard_map/ppermute | solution.py:1034
  67.0 17.4 %collective-permute-start.16 = (bf16[1,64,1024]{2,1,0:T(8,128)(2,1)S(1)}, bf16[1,64,1024]{2,1,0:T(8,128)(2,1)S(1)}, u32[]{:S(2)}, u32[]{:S(2)}) collective-permute-start(bf16[1,64,1024]{2,1,0:T(8,128)(2,1)S(1)} %unpack.1.mixed_ref), channel_id=1, source_target_pairs={{0,24},{1,25},{2,26},{3,27},{4,28},{5,29},{6,30},{7,31},{8,16},{9,... | collective-permute-start | bytes 393224 | tf_op jit(solution)/shard_map/ppermute | solution.py:1034
  85.3 12.3 %all-to-all-start.1 = ((bf16[16,72,128]{2,1,0:T(8,128)(2,1)}), bf16[16,72,128]{2,1,0:T(8,128)(2,1)S(1)}, u32[]{:S(2)}, u32[]{:S(2)}) async-start(bf16[16,72,128]{2,1,0:T(8,128)(2,1)} %get-tuple-element.109), calls=%async_computation.1 | async-start | bytes 589824 | tf_op jit(solution)/shard_map/all_to_all | solution.py:1031
  88.9 14.6 %collective-permute-start.19 = (bf16[4,64,1024]{2,1,0:T(8,128)(2,1)S(1)}, bf16[4,64,1024]{2,1,0:T(8,128)(2,1)S(1)}, u32[]{:S(2)}, u32[]{:S(2)}) collective-permute-start(bf16[4,64,1024]{2,1,0:T(8,128)(2,1)S(1)} %pad_maximum_fusion.2.rest_9_), channel_id=1, source_target_pairs={{0,4},{1,5},{2,6},{3,7},{4,0},{5,1},{6,2},{7,3},{8,12},{9,13},{10,... | collective-permute-start | bytes 1572872 | tf_op jit(solution)/shard_map/ppermute | solution.py:1034
  90.7 14.4 %collective-permute-start.18 = (bf16[4,64,1024]{2,1,0:T(8,128)(2,1)S(1)}, bf16[4,64,1024]{2,1,0:T(8,128)(2,1)}, u32[]{:S(2)}, u32[]{:S(2)}) collective-permute-start(bf16[4,64,1024]{2,1,0:T(8,128)(2,1)S(1)} %pad_maximum_fusion.2.rest_9_), channel_id=1, source_target_pairs={{0,2},{1,3},{2,0},{3,1},{4,6},{5,7},{6,4},{7,5},{8,10},{9,11},{10,... | collective-permute-start | bytes 1572872 | tf_op jit(solution)/shard_map/ppermute | solution.py:1034
  103.5 10.2 %collective-permute-start.20 = (bf16[2,64,1024]{2,1,0:T(8,128)(2,1)S(1)}, bf16[2,64,1024]{2,1,0:T(8,128)(2,1)S(1)}, u32[]{:S(2)}, u32[]{:S(2)}) collective-permute-start(bf16[2,64,1024]{2,1,0:T(8,128)(2,1)S(1)} %slice.18), channel_id=1, source_target_pairs={{0,2},{1,3},{2,0},{3,1},{4,6},{5,7},{6,4},{7,5},{8,10},{9,11},{10,... | collective-permute-start | bytes 786440 | tf_op jit(solution)/shard_map/ppermute | solution.py:1034
  106.1 7.7 %collective-permute-start.21 = (bf16[2,64,1024]{2,1,0:T(8,128)(2,1)S(1)}, bf16[2,64,1024]{2,1,0:T(8,128)(2,1)S(1)}, u32[]{:S(2)}, u32[]{:S(2)}) collective-permute-start(bf16[2,64,1024]{2,1,0:T(8,128)(2,1)S(1)} %slice.19), channel_id=1, source_target_pairs={{0,4},{1,5},{2,6},{3,7},{4,0},{5,1},{6,2},{7,3},{8,12},{9,13},{10,... | collective-permute-start | bytes 786440 | tf_op jit(solution)/shard_map/ppermute | solution.py:1034
  108.7 27.2 %all-to-all-start.2 = ((bf16[16,96,128]{2,1,0:T(8,128)(2,1)}), bf16[16,96,128]{2,1,0:T(8,128)(2,1)S(1)}, u32[]{:S(2)}, u32[]{:S(2)}) async-start(bf16[16,96,128]{2,1,0:T(8,128)(2,1)} %get-tuple-element.116.dqkv_ref), calls=%async_computation.2 | async-start | bytes 786432 | tf_op jit(solution)/shard_map/all_to_all | solution.py:1031
  135.8 22.9 %all-to-all-start.3 = ((bf16[16,136,128]{2,1,0:T(8,128)(2,1)}), bf16[16,136,128]{2,1,0:T(8,128)(2,1)S(1)}, u32[]{:S(2)}, u32[]{:S(2)}) async-start(bf16[16,136,128]{2,1,0:T(8,128)(2,1)} %get-tuple-element.129), calls=%async_computation.3 | async-start | bytes 1114112 | tf_op jit(solution)/shard_map/all_to_all | solution.py:1031
  (31 other events, 451.7 us)

commit v3 on v2

--- a/solution.py
+++ b/solution.py
@@ -513,8 +513,13 @@
     return jnp.sum(jnp.sum(rows, axis=0), axis=0, keepdims=True)[:, :1]
 
 
+def slots_of(chosen_ref, device):
+    row = chosen_ref[pl.ds(device // 2, 1), :]
+    return jnp.where(device % 2 == 0, row[:, :SHARE], row[:, SHARE:])
+
+
 def one_hot(own_ref, counts_ref, chosen_ref, tok_rows, live_only):
-    offsets = chosen_ref[pl.ds(own_ref[0], 1), :]
+    offsets = slots_of(chosen_ref, own_ref[0])
     capacity = offsets.shape[1]
     rows = lax.broadcasted_iota(jnp.int32, (tok_rows, capacity), 0)
     hot = rows == offsets
@@ -561,7 +566,7 @@
 
 def places_kernel(own_ref, counts_ref, lengths_ref, chosen_ref, kpos_ref, qpos_ref, qlow_ref):
     core = own_ref[0] % 2
-    devices, capacity = chosen_ref.shape
+    devices, capacity = 2 * chosen_ref.shape[0], SHARE
     tok_rows = lengths_ref[lengths_ref.shape[0] - 1]
     slot = lax.broadcasted_iota(jnp.int32, (1, capacity), 1)
     ends = []
@@ -569,7 +574,7 @@
         ends.append(lengths_ref[k] + (ends[-1] if ends else 0))
 
     def place(device):
-        value = device * tok_rows + chosen_ref[pl.ds(device, 1), :]
+        value = device * tok_rows + slots_of(chosen_ref, device)
         return value, slot < counts_ref[device]
 
     def key_row(device):
@@ -651,7 +656,7 @@
 
 def middle_kernel(
     own_ref, counts_ref, mixed_ref, total_ref, both_ref, vectors_ref, out_ref, up_ref, down_ref,
-    sent_ref, new_ref, dmiddle_ref, dweight_ref, w_out, w_up, w_down, hidden_ref, active_ref, sems,
+    sent_ref, active_ref, attn_ref, dmiddle_ref, dweight_ref, w_out, w_up, w_down, hidden_ref, sems,
 ):
     width, total_cols = up_ref.shape
     cols = total_cols // CHUNKS
@@ -673,9 +678,11 @@
     scaling = gate * ratio
     gain = vectors_ref[2:3, :]
     dbranch = scaling * upstream
-    dmlp = dbranch.astype(bf16)
+    upstream_low = both_ref[0, capacity:, :]
     copies[0].wait()
     attn_out = nn(mixed_ref[0], w_out[...])
+    attn_ref[...] = attn_out
+    dweight = jnp.sum(upstream * attn_out, axis=1, keepdims=True)
     middle = rows + attn_out
     scale = inverse_rms(middle)
     normed = (middle * scale * gain).astype(bf16)
@@ -688,12 +695,12 @@
         copies[1 + CHUNKS + c].wait()
         hidden = hidden_ref[:, part]
         value, slope = gelu_pair(hidden)
-        active_ref[:, part] = value.astype(bf16)
-        dhidden = (nt(dmlp, w_down[part, :]) * slope).astype(bf16)
+        active = value.astype(bf16)
+        active_ref[:, part] = active
+        product = nt(upstream_low, w_down[part, :])
+        dweight = dweight + jnp.sum(active.astype(f32) * product, axis=1, keepdims=True)
+        dhidden = (scaling * product * slope).astype(bf16)
         dnormed = dnormed + nt(dhidden, w_up[:, part])
-    branch = attn_out + nn(active_ref[...], w_down[...])
-    new_ref[...] = (rows + scaling * branch).astype(bf16)
-    dweight = jnp.sum(upstream * branch, axis=1, keepdims=True)
     dweight_ref[...] = jnp.broadcast_to(dweight, dweight_ref.shape)
     scaled = gain * dnormed
     dmiddle = scale * scaled - middle * (scale * scale * scale) * jnp.mean(scaled * middle, axis=-1, keepdims=True)
@@ -704,8 +711,24 @@
     write_note(sent_ref, 2 * HALF, jnp.sum(jnp.where(live, dweight * gate, 0.0), axis=0, keepdims=True))
 
 
-def put_kernel(own_ref, counts_ref, chosen_ref, old_ref, new_ref, result_ref):
-    put_rows(own_ref, counts_ref, chosen_ref, old_ref, new_ref[...], result_ref)
+def put_kernel(
+    own_ref, counts_ref, chosen_ref, total_ref, both_ref, vectors_ref, active_ref, attn_ref, old_ref, down_ref,
+    result_ref, w_down, sems,
+):
+    rows_of_chunk = down_ref.shape[0] // CHUNKS
+    parts = [pl.ds(c * rows_of_chunk, rows_of_chunk) for c in range(CHUNKS)]
+    copies = [pltpu.make_async_copy(down_ref.at[p, :], w_down.at[p, :], sems.at[c]) for c, p in enumerate(parts)]
+    for copy in copies:
+        copy.start()
+    rows = both_ref[0, : both_ref.shape[1] // 2, :].astype(f32)
+    scaling = gate_of(rows, vectors_ref) * (total_count(counts_ref) / total_ref[:1, :1])
+    mlp_out = jnp.zeros_like(rows)
+    for c, copy in enumerate(copies):
+        part = slice(c * rows_of_chunk, (c + 1) * rows_of_chunk)
+        copy.wait()
+        mlp_out = mlp_out + nn(active_ref[:, part], w_down[part, :])
+    new = (rows + scaling * (attn_ref[...] + mlp_out)).astype(bf16)
+    put_rows(own_ref, counts_ref, chosen_ref, old_ref, new, result_ref)
 
 
 def put_rows(own_ref, counts_ref, chosen_ref, old_ref, new, result_ref):
@@ -821,7 +844,7 @@
             return jnp.where(core == 0, even, odd), jnp.where(core == 0, odd, even)
 
         def store(first, kept, given):
-            keep_ref[:, first : first + kept.shape[1], :] = kept
+            keep_ref[:, first : first + kept.shape[1], :] = kept.astype(bf16)
             give_ref[:, first : first + kept.shape[1], :] = given.astype(bf16)
 
         for t in range(TILES):
@@ -845,7 +868,7 @@
             if shift:
                 tile = jnp.concatenate([tile[:, shift:], tile[:, :shift]], axis=1)
             after = jnp.concatenate([tile[:, OUT_ROWS:], tile[:, :OUT_ROWS]], axis=1)
-            keep_ref[c, AT_NOTE:, :] = jnp.where(core == 0, tile, after)
+            keep_ref[c, AT_NOTE:, :] = in_parts(jnp.where(core == 0, tile, after))
             give_ref[c, AT_NOTE:, :] = in_parts(jnp.where(core == 0, after, tile))
         down = grad_down[...]
         half = down.shape[0] // 2
@@ -853,11 +876,11 @@
         down_give_ref[...] = jnp.where(core == 0, down[half:], down[:half]).astype(bf16)
 
 
-def merge_kernel(keep_ref, moved_ref, down_keep_ref, down_moved_ref, sent_ref, down_ref):
-    sent_ref[:, :AT_NOTE, :] = (keep_ref[:, :AT_NOTE, :] + moved_ref[:, :AT_NOTE, :].astype(f32)).astype(bf16)
-    note = keep_ref[:, AT_NOTE:, :] + jnp.sum(moved_ref[:, AT_NOTE:, :].astype(f32), axis=1, keepdims=True)
-    sent_ref[:, AT_NOTE:, :] = in_parts(note)
-    down_ref[...] = down_keep_ref[...] + down_moved_ref[...].astype(f32)
+def merge_kernel(keep_ref, moved_ref, sent_ref):
+    total = keep_ref[...].astype(f32) + moved_ref[...].astype(f32)
+    sent_ref[:, :AT_NOTE, :] = total[:, :AT_NOTE].astype(bf16)
+    note = jnp.sum(total[:, AT_NOTE:], axis=1, keepdims=True)
+    sent_ref[:, AT_NOTE:, :] = in_parts(jnp.broadcast_to(note, (note.shape[0], NOTE, LANES)))
 
 
 def rows_kernel(
@@ -974,7 +997,7 @@
 
 
 microseconds = {
-    "places": 1, "fetch": 3, "project": 4, "attend": 5, "unpack": 2, "middle": 15, "put": 3, "attend_back": 6, "keys": 2,
+    "places": 1, "fetch": 3, "project": 4, "attend": 5, "unpack": 2, "middle": 15, "put": 6, "attend_back": 6, "keys": 2,
     "units": 16, "merge": 3, "rows": 7, "finish": 2,
 }
 
@@ -1022,7 +1045,7 @@
     factor = HEAD_DIM ** (-0.5)
     core = own % 2
     own_id = own.astype(jnp.int32).reshape(1)
-    chosen = chosen.reshape(devices, capacity)
+    chosen = chosen.reshape(chips, 2 * capacity)
     vectors = jnp.stack([w_router, gain_attn, gain_mlp]).astype(f32)
     own_gains = lax.dynamic_slice_in_dim(vectors, own * out_rows, out_rows, 1)
     cores = [[2 * c + k for c in range(chips)] for k in range(2)]
@@ -1091,11 +1114,12 @@
     upstream_all = gathered_whole(upstream_sides)
     mixed = call(unpack_kernel, "unpack", [vmem], shaped((1, capacity, width), bf16), (mixed_got,))
     mixed_line = line_of(mixed)
-    sent, new_rows, dmiddle, dweight = call(
+    sent, active, attn_out, dmiddle, dweight = call(
         middle_kernel, "middle", [smem, smem] + [vmem] * 4 + [hbm] * 3,
         (
             shaped((chips, 2 * HALF + NOTE, LANES), bf16),
-            shaped((capacity, width), bf16),
+            shaped((capacity, hidden_width), bf16),
+            shaped((capacity, width), f32),
             shaped((capacity, width), f32),
             shaped((capacity, LANES), f32),
         ),
@@ -1105,7 +1129,6 @@
             pltpu.VMEM((width, hidden_width), bf16),
             pltpu.VMEM((hidden_width, width), bf16),
             pltpu.VMEM((capacity, hidden_width), f32),
-            pltpu.VMEM((capacity, hidden_width), bf16),
             pltpu.SemaphoreType.DMA((1 + 2 * CHUNKS,)),
         ],
     )
@@ -1113,11 +1136,13 @@
     mixed_sides = sides_of(mixed_line)
     upstream_all, sent = lax.optimization_barrier((upstream_all, sent))
     grads_got = swap(sent)
+    output = call(
+        put_kernel, "put", [smem, smem] + [vmem] * 7 + [hbm], shaped((tok_rows, width), bf16),
+        (own_id, counts, chosen, total, both, vectors, active, attn_out, tokens_in, w_down),
+        [pltpu.VMEM((hidden_width, width), bf16), pltpu.SemaphoreType.DMA((CHUNKS,))],
+    )
     mixed_all = gathered(mixed_sides)
-    output = call(
-        put_kernel, "put", [smem, smem] + [vmem] * 3, shaped((tok_rows, width), bf16),
-        (own_id, counts, chosen, tokens_in, new_rows),
-    )
+    output, grads_got = lax.optimization_barrier((output, grads_got))
     dq, dkv_own, dkv_other, coef = call(
         functools.partial(pair_attend_back_kernel, factor), "attend_back", [vmem] * 8,
         (
@@ -1143,7 +1168,7 @@
         out_shape=(
             shaped((hidden_cols // 2, width), f32),
             shaped((hidden_cols // 2, width), bf16),
-            shaped((chips, GRAD_ROWS, LANES), f32),
+            shaped((chips, GRAD_ROWS, LANES), bf16),
             shaped((chips, GRAD_ROWS, LANES), bf16),
         ),
         grid_spec=pltpu.PrefetchScalarGridSpec(
@@ -1186,11 +1211,10 @@
         cost_estimate=cost_of("units"),
         name="units",
     )(own_id, counts, grads_got, dqkv, total, coef, vectors, both, dweight, w_out, w_up, w_down, *rows_all, *upstream_all, *mixed_all)
-    sent, grad_down = call(
-        merge_kernel, "merge", [vmem] * 4,
-        (shaped((chips, GRAD_ROWS, LANES), bf16), shaped((hidden_cols // 2, width), f32)),
-        (keep, across(give, 1), down_keep, across(down_give, 1)),
-    )
+    sent = call(
+        merge_kernel, "merge", [vmem] * 2, shaped((chips, GRAD_ROWS, LANES), bf16), (keep, across(give, 1))
+    )
+    grad_down = down_keep + across(down_give, 1).astype(f32)
     last = swap(sent)
     input_grad = call(
         rows_kernel, "rows", [smem, smem] + [vmem] * 9 + [hbm] * 3, shaped((tok_rows, width), bf16),

time: 161 us -> 156 us (0.969)
  waiting for transfers between devices: 39.1 us -> 33.8 us
  Pallas kernels: 55.9 us -> 58.7 us
  local copies, waits for them, and re-layouts: 11.7 us -> 9.1 us
    all_to_all x4, waiting for transfers between devices: 10.7 us -> 6.88 us  [swap(): lax.all_to_all(value, 'seq', split_axis=0, concat_axis=0, tiled=True, axi...]
    pallas_call x12, Pallas kernels: 40.6 us -> 43.8 us  [call(): pl.pallas_call(kernel, out_shape=out_shape, in_specs=in_specs, out_specs=...]
    unnamed x54 -> x56, local copies, waits for them, and re-layouts: 3.77 us -> 2.56 us
  transfers between devices with their start and end apart: 28 -> 28, of which waited for: 14 -> 13; matrix products, arithmetic and copies ran while one was open for 5% -> 5% of each run, Pallas kernels for 31% -> 34%
where the time goes in v3:
time: 156 us; the launch traced here: 155 us
  Pallas kernels  58.7 us (38%)
  starting transfers between devices  49.6 us (32%)
  waiting for transfers between devices  33.8 us (22%)
  local copies, waits for them, and re-layouts  9.1 us (6%)
  other arithmetic  2.96 us (2%)
    pallas_call x12, Pallas kernels, call(): pl.pallas_call(kernel, out_shape=out_shape, in_specs=in_specs, out_specs=...  43.8 us
    ppermute x24, starting transfers between devices, across(): return lax.ppermute(value, 'seq', [(s, s ^ bits) for s in range(devices)])  28.3 us
    ppermute x24, waiting for transfers between devices, across(): return lax.ppermute(value, 'seq', [(s, s ^ bits) for s in range(devices)])  27 us
    all_to_all x4, starting transfers between devices, swap(): lax.all_to_all(value, 'seq', split_axis=0, concat_axis=0, tiled=True, axi...  21.3 us
    pallas_call x1, Pallas kernels, pairs(): pl.pallas_call(units_kernel, out_shape=(shaped((hidden_cols // 2, width),...  14.9 us
    all_to_all x4, waiting for transfers between devices, swap(): lax.all_to_all(value, 'seq', split_axis=0, concat_axis=0, tiled=True, axi...  6.88 us
  transfers between devices with their start and end apart: 28, of which 13 were waited for; matrix products, arithmetic and copies ran while one was open for 5% of the time, Pallas kernels for 34%

profile of v3, /device:TPU:0, one launch (start us, length us, event | category | flops | bytes accessed | tf_op | source)
XLA Modules:
  0.0 155.3 jit_solution(1232617598713155565)
XLA Ops:
  0.7 2.9 %fetch.1 = (bf16[1,128,1024]{2,1,0:T(8,128)(2,1)}, bf16[1,64,1024]{2,1,0:T(8,128)(2,1)}, bf16[1,64,1024]{2,1,0:T(8,128)(2,1)}) custom-call(s32[1]{0:T(128)} %bitcast.own_ref, s32[32]{0:T(128)} %counts_ref.13, s32[16,128]{1,0:T(8,128)} %bitcast.7, bf16[512,1024]{1,0:T(8,128)(2,1)} %old_ref.2, bf16[512,1024]{1,0:T(8,128)(2,1)} %old_ref.3), custom_call_target="tpu_custom_call" | custom-call | bytes 9900000 | tf_op jit(solution)/shard_map/fetch/pallas_call | solution.py:1010
  3.6 3.1 %collective-permute-start = (bf16[1,64,1024]{2,1,0:T(8,128)(2,1)}, bf16[1,64,1024]{2,1,0:T(8,128)(2,1)S(1)}, u32[]{:S(2)}, u32[]{:S(2)}) collective-permute-start(bf16[1,64,1024]{2,1,0:T(8,128)(2,1)} %get-tuple-element.76), channel_id=1, source_target_pairs={{0,8},{1,9},{2,10},{3,11},{4,12},{5,13},{6,14},{7,15},{8,0},{9,1},... | collective-permute-start | bytes 393224 | tf_op jit(solution)/shard_map/ppermute | solution.py:1057
  6.7 2.6 %collective-permute-start.1 = (bf16[1,64,1024]{2,1,0:T(8,128)(2,1)}, bf16[1,64,1024]{2,1,0:T(8,128)(2,1)S(1)}, u32[]{:S(2)}, u32[]{:S(2)}) collective-permute-start(bf16[1,64,1024]{2,1,0:T(8,128)(2,1)} %get-tuple-element.76), channel_id=1, source_target_pairs={{0,16},{1,17},{2,18},{3,19},{4,20},{5,21},{6,22},{7,23},{8,24},{9,... | collective-permute-start | bytes 393224 | tf_op jit(solution)/shard_map/ppermute | solution.py:1057
  9.3 2.6 %collective-permute-done = bf16[1,64,1024]{2,1,0:T(8,128)(2,1)S(1)} collective-permute-done((bf16[1,64,1024]{2,1,0:T(8,128)(2,1)}, bf16[1,64,1024]{2,1,0:T(8,128)(2,1)S(1)}, u32[]{:S(2)}, u32[]{:S(2)}) %collective-permute-start) | collective-permute-done | bytes 131104 | tf_op jit(solution)/shard_map/ppermute | solution.py:1057
  12.0 7.9 %collective-permute-done.1 = bf16[1,64,1024]{2,1,0:T(8,128)(2,1)S(1)} collective-permute-done((bf16[1,64,1024]{2,1,0:T(8,128)(2,1)}, bf16[1,64,1024]{2,1,0:T(8,128)(2,1)S(1)}, u32[]{:S(2)}, u32[]{:S(2)}) %collective-permute-start.1) | collective-permute-done | bytes 131104 | tf_op jit(solution)/shard_map/ppermute | solution.py:1057
  23.9 2.0 %collective-permute-start.7 = (bf16[1,64,1024]{2,1,0:T(8,128)(2,1)}, bf16[1,64,1024]{2,1,0:T(8,128)(2,1)S(1)}, u32[]{:S(2)}, u32[]{:S(2)}) collective-permute-start(bf16[1,64,1024]{2,1,0:T(8,128)(2,1)} %get-tuple-element.82), channel_id=1, source_target_pairs={{0,8},{1,9},{2,10},{3,11},{4,12},{5,13},{6,14},{7,15},{8,0},{9,1},... | collective-permute-start | bytes 393224 | tf_op jit(solution)/shard_map/ppermute | solution.py:1057
  29.4 2.7 %collective-permute-done.4.rest_2_ = bf16[4,64,1024]{2,1,0:T(8,128)(2,1)S(1)} collective-permute-done((bf16[4,64,1024]{2,1,0:T(8,128)(2,1)S(1)}, bf16[4,64,1024]{2,1,0:T(8,128)(2,1)S(1)}, u32[]{:S(2)}, u32[]{:S(2)}) %collective-permute-start.4) | collective-permute-done | bytes 524320 | tf_op jit(solution)/shard_map/ppermute | solution.py:1057
  39.0 2.9 %collective-permute-done.6.rest_4_ = bf16[2,64,1024]{2,1,0:T(8,128)(2,1)S(1)} collective-permute-done((bf16[2,64,1024]{2,1,0:T(8,128)(2,1)S(1)}, bf16[2,64,1024]{2,1,0:T(8,128)(2,1)S(1)}, u32[]{:S(2)}, u32[]{:S(2)}) %collective-permute-start.6) | collective-permute-done | bytes 262176 | tf_op jit(solution)/shard_map/ppermute | solution.py:1057
  41.9 2.2 %project.1.got_ref = bf16[16,104,128]{2,1,0:T(8,128)(2,1)S(1)} custom-call(s32[1]{0:T(128)} %bitcast.own_ref, s32[32]{0:T(128)S(1)} %copy-done.11, f32[3,1024]{1,0:T(4,128)S(1)} %maximum_convert_fusion.vectors_ref, bf16[1024,128]{1,0:T(8,128)(2,1)S(1)} %constant_dynamic-slice_fusion.7.wq, bf16[1024,128]{1,0:T(8,128)(2,1)S(1)} %get-tuple-element.89.wk, ...), custom_call_target="tpu_custom_call" | custom-call | bytes 13200000 | tf_op jit(solution)/shard_map/project/pallas_call | solution.py:1010
  45.9 3.7 %attend.1 = (bf16[512,128]{1,0:T(8,128)(2,1)}, f32[512,128]{1,0:T(8,128)S(1)}, f32[4,256]{1,0:T(4,128)S(1)}, f32[8,128]{1,0:T(8,128)S(1)}) custom-call(bf16[16,104,128]{2,1,0:T(8,128)(2,1)S(1)} %project.1.got_ref, bf16[16,104,128]{2,1,0:T(8,128)(2,1)S(1)} %collective-permute-done.10.other_ref, f32[2,1024]{1,0:T(2,128)S(1)} %get-tuple-element.96.kpos_ref, ...), custom_call_target="tpu_custom_call" | custom-call | bytes 16500000 | tf_op jit(solution)/shard_map/attend/pallas_call | solution.py:1010
  49.6 5.6 %all-to-all-start = ((bf16[16,32,128]{2,1,0:T(8,128)(2,1)}), bf16[16,32,128]{2,1,0:T(8,128)(2,1)S(1)}, u32[]{:S(2)}, u32[]{:S(2)}) async-start(bf16[16,32,128]{2,1,0:T(8,128)(2,1)} %bitcast.2), calls=%async_computation | async-start | bytes 262144 | tf_op jit(solution)/shard_map/all_to_all | solution.py:1054
  55.3 3.4 %collective-permute-done.11.rest_6_ = bf16[4,64,1024]{2,1,0:T(8,128)(2,1)S(1)} collective-permute-done((bf16[4,64,1024]{2,1,0:T(8,128)(2,1)S(1)}, bf16[4,64,1024]{2,1,0:T(8,128)(2,1)S(1)}, u32[]{:S(2)}, u32[]{:S(2)}) %collective-permute-start.11) | collective-permute-done | bytes 524320 | tf_op jit(solution)/shard_map/ppermute | solution.py:1057
  60.3 2.7 %all-to-all-done.got_ref = bf16[16,32,128]{2,1,0:T(8,128)(2,1)S(1)} async-done(((bf16[16,32,128]{2,1,0:T(8,128)(2,1)}), bf16[16,32,128]{2,1,0:T(8,128)(2,1)S(1)}, u32[]{:S(2)}, u32[]{:S(2)}) %all-to-all-start) | async-done | bytes 131104 | tf_op jit(solution)/shard_map/all_to_all | solution.py:1054
  65.7 3.0 %collective-permute-start.16 = (bf16[1,64,1024]{2,1,0:T(8,128)(2,1)S(1)}, bf16[1,64,1024]{2,1,0:T(8,128)(2,1)S(1)}, u32[]{:S(2)}, u32[]{:S(2)}) collective-permute-start(bf16[1,64,1024]{2,1,0:T(8,128)(2,1)S(1)} %unpack.1.mixed_ref), channel_id=1, source_target_pairs={{0,24},{1,25},{2,26},{3,27},{4,28},{5,29},{6,30},{7,31},{8,16},{9,... | collective-permute-start | bytes 393224 | tf_op jit(solution)/shard_map/ppermute | solution.py:1057
  68.7 13.0 %middle.1 = (bf16[16,72,128]{2,1,0:T(8,128)(2,1)}, bf16[64,4096]{1,0:T(8,128)(2,1)}, f32[64,1024]{1,0:T(8,128)}, f32[64,1024]{1,0:T(8,128)}, f32[64,128]{1,0:T(8,128)}) custom-call(s32[1]{0:T(128)} %bitcast.own_ref, s32[32]{0:T(128)} %counts_ref.13, bf16[1,64,1024]{2,1,0:T(8,128)(2,1)} %copy-done.4, f32[8,128]{1,0:T(8,128)} %copy-done.10, ...), custom_call_target="tpu_custom_call" | custom-call | bytes 49500000 | tf_op jit(solution)/shard_map/middle/pallas_call | solution.py:1010
  82.8 3.8 %all-to-all-start.1 = ((bf16[16,72,128]{2,1,0:T(8,128)(2,1)}), bf16[16,72,128]{2,1,0:T(8,128)(2,1)S(1)}, u32[]{:S(2)}, u32[]{:S(2)}) async-start(bf16[16,72,128]{2,1,0:T(8,128)(2,1)} %get-tuple-element.111), calls=%async_computation.1 | async-start | bytes 589824 | tf_op jit(solution)/shard_map/all_to_all | solution.py:1054
  89.7 6.8 %put.1 = bf16[512,1024]{1,0:T(8,128)(2,1)} custom-call(s32[1]{0:T(128)} %bitcast.own_ref, s32[32]{0:T(128)} %counts_ref.13, s32[16,128]{1,0:T(8,128)} %bitcast.8, f32[8,128]{1,0:T(8,128)} %copy-done.10, bf16[1,128,1024]{2,1,0:T(8,128)(2,1)} %get-tuple-element.100.both_ref.rows_ref, f32[3,1024]{1,0:T(4,128)} %copy-done.7, ...), custom_call_target="tpu_custom_call" | custom-call | bytes 19800000 | tf_op jit(solution)/shard_map/put/pallas_call | solution.py:1010
  96.6 3.8 %attend_back.1 = (bf16[512,128]{1,0:T(8,128)(2,1)S(1)}, f32[1024,128]{1,0:T(8,128)S(1)}, f32[1032,128]{1,0:T(8,128)S(1)}, f32[8,128]{1,0:T(8,128)S(1)}) custom-call(bf16[16,104,128]{2,1,0:T(8,128)(2,1)S(1)} %project.1.got_ref, bf16[16,104,128]{2,1,0:T(8,128)(2,1)S(1)} %collective-permute-done.10.other_ref, ...), custom_call_target="tpu_custom_call" | custom-call | bytes 19800000 | tf_op jit(solution)/shard_map/attend_back/pallas_call | solution.py:1010
  106.2 5.0 %all-to-all-start.2 = ((bf16[16,96,128]{2,1,0:T(8,128)(2,1)}), bf16[16,96,128]{2,1,0:T(8,128)(2,1)S(1)}, u32[]{:S(2)}, u32[]{:S(2)}) async-start(bf16[16,96,128]{2,1,0:T(8,128)(2,1)} %get-tuple-element.120.dqkv_ref), calls=%async_computation.2 | async-start | bytes 786432 | tf_op jit(solution)/shard_map/all_to_all | solution.py:1054
  112.1 14.9 %units.1 = (f32[128,1024]{1,0:T(8,128)}, bf16[128,1024]{1,0:T(8,128)(2,1)}, bf16[16,136,128]{2,1,0:T(8,128)(2,1)}, bf16[16,136,128]{2,1,0:T(8,128)(2,1)}) custom-call(s32[1]{0:T(128)} %bitcast.own_ref, s32[32]{0:T(128)} %counts_ref.13, bf16[16,72,128]{2,1,0:T(8,128)(2,1)} %copy-done.3, bf16[16,96,128]{2,1,0:T(8,128)(2,1)} %get-tuple-element.120.dqkv_ref, ...), custom_call_target="tpu_custom_call" | custom-call | bytes 52800000 | tf_op jit(solution)/shard_map/units/pallas_call | solution.py:1166
  127.1 2.2 %collective-permute-done.22.moved_ref = bf16[16,136,128]{2,1,0:T(8,128)(2,1)S(1)} collective-permute-done((bf16[16,136,128]{2,1,0:T(8,128)(2,1)}, bf16[16,136,128]{2,1,0:T(8,128)(2,1)S(1)}, u32[]{:S(2)}, u32[]{:S(2)}) %collective-permute-start.22) | collective-permute-done | bytes 557088 | tf_op jit(solution)/shard_map/ppermute | solution.py:1057
  131.3 6.9 %all-to-all-start.3 = ((bf16[16,136,128]{2,1,0:T(8,128)(2,1)}), bf16[16,136,128]{2,1,0:T(8,128)(2,1)S(1)}, u32[]{:S(2)}, u32[]{:S(2)}) async-start(bf16[16,136,128]{2,1,0:T(8,128)(2,1)} %merge.1), calls=%async_computation.3 | async-start | bytes 1114112 | tf_op jit(solution)/shard_map/all_to_all | solution.py:1054
  142.6 7.4 %rows.1 = bf16[512,1024]{1,0:T(8,128)(2,1)} custom-call(s32[1]{0:T(128)} %bitcast.own_ref, s32[32]{0:T(128)} %counts_ref.13, s32[16,128]{1,0:T(8,128)} %bitcast.9, bf16[16,96,128]{2,1,0:T(8,128)(2,1)} %copy-done.15, bf16[1,128,1024]{2,1,0:T(8,128)(2,1)} %get-tuple-element.100.both_ref.rows_ref, f32[64,1024]{1,0:T(8,128)} %get-tuple-element.121.dmiddle_ref, ...), custom_call_target="tpu_custom_call" | custom-call | bytes 23100000 | tf_op jit(solution)/shard_map/rows/pallas_call | solution.py:1010
  150.0 4.1 %all-to-all-done.3.got_ref = bf16[16,136,128]{2,1,0:T(8,128)(2,1)S(1)} async-done(((bf16[16,136,128]{2,1,0:T(8,128)(2,1)}), bf16[16,136,128]{2,1,0:T(8,128)(2,1)S(1)}, u32[]{:S(2)}, u32[]{:S(2)}) %all-to-all-start.3) | async-done | bytes 557088 | tf_op jit(solution)/shard_map/all_to_all | solution.py:1054
  (120 shorter events, 38.9 us)
Async XLA Ops:
  3.6 8.3 %collective-permute-start = (bf16[1,64,1024]{2,1,0:T(8,128)(2,1)}, bf16[1,64,1024]{2,1,0:T(8,128)(2,1)S(1)}, u32[]{:S(2)}, u32[]{:S(2)}) collective-permute-start(bf16[1,64,1024]{2,1,0:T(8,128)(2,1)} %get-tuple-element.76), channel_id=1, source_target_pairs={{0,8},{1,9},{2,10},{3,11},{4,12},{5,13},{6,14},{7,15},{8,0},{9,1},... | collective-permute-start | bytes 393224 | tf_op jit(solution)/shard_map/ppermute | solution.py:1057
  6.7 13.2 %collective-permute-start.1 = (bf16[1,64,1024]{2,1,0:T(8,128)(2,1)}, bf16[1,64,1024]{2,1,0:T(8,128)(2,1)S(1)}, u32[]{:S(2)}, u32[]{:S(2)}) collective-permute-start(bf16[1,64,1024]{2,1,0:T(8,128)(2,1)} %get-tuple-element.76), channel_id=1, source_target_pairs={{0,16},{1,17},{2,18},{3,19},{4,20},{5,21},{6,22},{7,23},{8,24},{9,... | collective-permute-start | bytes 393224 | tf_op jit(solution)/shard_map/ppermute | solution.py:1057
  9.3 10.6 %collective-permute-start.2 = (bf16[1,64,1024]{2,1,0:T(8,128)(2,1)}, bf16[1,64,1024]{2,1,0:T(8,128)(2,1)S(1)}, u32[]{:S(2)}, u32[]{:S(2)}) collective-permute-start(bf16[1,64,1024]{2,1,0:T(8,128)(2,1)} %get-tuple-element.76), channel_id=1, source_target_pairs={{0,24},{1,25},{2,26},{3,27},{4,28},{5,29},{6,30},{7,31},{8,16},{9,... | collective-permute-start | bytes 393224 | tf_op jit(solution)/shard_map/ppermute | solution.py:1057
  20.9 11.3 %collective-permute-start.4 = (bf16[4,64,1024]{2,1,0:T(8,128)(2,1)S(1)}, bf16[4,64,1024]{2,1,0:T(8,128)(2,1)S(1)}, u32[]{:S(2)}, u32[]{:S(2)}) collective-permute-start(bf16[4,64,1024]{2,1,0:T(8,128)(2,1)S(1)} %pad_maximum_fusion.rest_0_), channel_id=1, source_target_pairs={{0,4},{1,5},{2,6},{3,7},{4,0},{5,1},{6,2},{7,3},{8,12},{9,13},{10,... | collective-permute-start | bytes 1572872 | tf_op jit(solution)/shard_map/ppermute | solution.py:1057
  22.4 13.0 %collective-permute-start.3 = (bf16[4,64,1024]{2,1,0:T(8,128)(2,1)S(1)}, bf16[4,64,1024]{2,1,0:T(8,128)(2,1)S(1)}, u32[]{:S(2)}, u32[]{:S(2)}) collective-permute-start(bf16[4,64,1024]{2,1,0:T(8,128)(2,1)S(1)} %pad_maximum_fusion.rest_0_), channel_id=1, source_target_pairs={{0,2},{1,3},{2,0},{3,1},{4,6},{5,7},{6,4},{7,5},{8,10},{9,11},{10,... | collective-permute-start | bytes 1572872 | tf_op jit(solution)/shard_map/ppermute | solution.py:1057
  23.9 13.9 %collective-permute-start.7 = (bf16[1,64,1024]{2,1,0:T(8,128)(2,1)}, bf16[1,64,1024]{2,1,0:T(8,128)(2,1)S(1)}, u32[]{:S(2)}, u32[]{:S(2)}) collective-permute-start(bf16[1,64,1024]{2,1,0:T(8,128)(2,1)} %get-tuple-element.82), channel_id=1, source_target_pairs={{0,8},{1,9},{2,10},{3,11},{4,12},{5,13},{6,14},{7,15},{8,0},{9,1},... | collective-permute-start | bytes 393224 | tf_op jit(solution)/shard_map/ppermute | solution.py:1057
  25.9 11.9 %collective-permute-start.8 = (bf16[1,64,1024]{2,1,0:T(8,128)(2,1)}, bf16[1,64,1024]{2,1,0:T(8,128)(2,1)S(1)}, u32[]{:S(2)}, u32[]{:S(2)}) collective-permute-start(bf16[1,64,1024]{2,1,0:T(8,128)(2,1)} %get-tuple-element.82), channel_id=1, source_target_pairs={{0,16},{1,17},{2,18},{3,19},{4,20},{5,21},{6,22},{7,23},{8,24},{9,... | collective-permute-start | bytes 393224 | tf_op jit(solution)/shard_map/ppermute | solution.py:1057
  26.9 10.9 %collective-permute-start.9 = (bf16[1,64,1024]{2,1,0:T(8,128)(2,1)}, bf16[1,64,1024]{2,1,0:T(8,128)(2,1)S(1)}, u32[]{:S(2)}, u32[]{:S(2)}) collective-permute-start(bf16[1,64,1024]{2,1,0:T(8,128)(2,1)} %get-tuple-element.82), channel_id=1, source_target_pairs={{0,24},{1,25},{2,26},{3,27},{4,28},{5,29},{6,30},{7,31},{8,16},{9,... | collective-permute-start | bytes 393224 | tf_op jit(solution)/shard_map/ppermute | solution.py:1057
  32.1 6.8 %collective-permute-start.5 = (bf16[2,64,1024]{2,1,0:T(8,128)(2,1)S(1)}, bf16[2,64,1024]{2,1,0:T(8,128)(2,1)S(1)}, u32[]{:S(2)}, u32[]{:S(2)}) collective-permute-start(bf16[2,64,1024]{2,1,0:T(8,128)(2,1)S(1)} %slice.16), channel_id=1, source_target_pairs={{0,2},{1,3},{2,0},{3,1},{4,6},{5,7},{6,4},{7,5},{8,10},{9,11},{10,... | collective-permute-start | bytes 786440 | tf_op jit(solution)/shard_map/ppermute | solution.py:1057
  35.4 6.4 %collective-permute-start.6 = (bf16[2,64,1024]{2,1,0:T(8,128)(2,1)S(1)}, bf16[2,64,1024]{2,1,0:T(8,128)(2,1)S(1)}, u32[]{:S(2)}, u32[]{:S(2)}) collective-permute-start(bf16[2,64,1024]{2,1,0:T(8,128)(2,1)S(1)} %slice.17), channel_id=1, source_target_pairs={{0,4},{1,5},{2,6},{3,7},{4,0},{5,1},{6,2},{7,3},{8,12},{9,13},{10,... | collective-permute-start | bytes 786440 | tf_op jit(solution)/shard_map/ppermute | solution.py:1057
  44.2 14.5 %collective-permute-start.11 = (bf16[4,64,1024]{2,1,0:T(8,128)(2,1)S(1)}, bf16[4,64,1024]{2,1,0:T(8,128)(2,1)S(1)}, u32[]{:S(2)}, u32[]{:S(2)}) collective-permute-start(bf16[4,64,1024]{2,1,0:T(8,128)(2,1)S(1)} %pad_maximum_fusion.1.rest_5_), channel_id=1, source_target_pairs={{0,2},{1,3},{2,0},{3,1},{4,6},{5,7},{6,4},{7,5},{8,10},{9,11},{10,... | collective-permute-start | bytes 1572872 | tf_op jit(solution)/shard_map/ppermute | solution.py:1057
  45.7 14.6 %collective-permute-start.12 = (bf16[4,64,1024]{2,1,0:T(8,128)(2,1)S(1)}, bf16[4,64,1024]{2,1,0:T(8,128)(2,1)S(1)}, u32[]{:S(2)}, u32[]{:S(2)}) collective-permute-start(bf16[4,64,1024]{2,1,0:T(8,128)(2,1)S(1)} %pad_maximum_fusion.1.rest_5_), channel_id=1, source_target_pairs={{0,4},{1,5},{2,6},{3,7},{4,0},{5,1},{6,2},{7,3},{8,12},{9,13},{10,... | collective-permute-start | bytes 1572872 | tf_op jit(solution)/shard_map/ppermute | solution.py:1057
  49.6 13.4 %all-to-all-start = ((bf16[16,32,128]{2,1,0:T(8,128)(2,1)}), bf16[16,32,128]{2,1,0:T(8,128)(2,1)S(1)}, u32[]{:S(2)}, u32[]{:S(2)}) async-start(bf16[16,32,128]{2,1,0:T(8,128)(2,1)} %bitcast.2), calls=%async_computation | async-start | bytes 262144 | tf_op jit(solution)/shard_map/all_to_all | solution.py:1054
  63.1 19.7 %collective-permute-start.13 = (bf16[4,64,1024]{2,1,0:T(8,128)(2,1)S(1)}, bf16[4,64,1024]{2,1,0:T(8,128)(2,1)}, u32[]{:S(2)}, u32[]{:S(2)}) collective-permute-start(bf16[4,64,1024]{2,1,0:T(8,128)(2,1)S(1)} %collective-permute-done.12.rest_7_), channel_id=1, source_target_pairs={{0,2},{1,3},{2,0},{3,1},{4,6},{5,7},{6,4},{7,5},{8,10},{9,11},{10,... | collective-permute-start | bytes 1572872 | tf_op jit(solution)/shard_map/ppermute | solution.py:1057
  64.3 17.5 %collective-permute-start.14 = (bf16[1,64,1024]{2,1,0:T(8,128)(2,1)S(1)}, bf16[1,64,1024]{2,1,0:T(8,128)(2,1)S(1)}, u32[]{:S(2)}, u32[]{:S(2)}) collective-permute-start(bf16[1,64,1024]{2,1,0:T(8,128)(2,1)S(1)} %unpack.1.mixed_ref), channel_id=1, source_target_pairs={{0,8},{1,9},{2,10},{3,11},{4,12},{5,13},{6,14},{7,15},{8,0},{9,1},... | collective-permute-start | bytes 393224 | tf_op jit(solution)/shard_map/ppermute | solution.py:1057
  64.6 17.2 %collective-permute-start.15 = (bf16[1,64,1024]{2,1,0:T(8,128)(2,1)S(1)}, bf16[1,64,1024]{2,1,0:T(8,128)(2,1)S(1)}, u32[]{:S(2)}, u32[]{:S(2)}) collective-permute-start(bf16[1,64,1024]{2,1,0:T(8,128)(2,1)S(1)} %unpack.1.mixed_ref), channel_id=1, source_target_pairs={{0,16},{1,17},{2,18},{3,19},{4,20},{5,21},{6,22},{7,23},{8,24},{9,... | collective-permute-start | bytes 393224 | tf_op jit(solution)/shard_map/ppermute | solution.py:1057
  65.7 16.1 %collective-permute-start.16 = (bf16[1,64,1024]{2,1,0:T(8,128)(2,1)S(1)}, bf16[1,64,1024]{2,1,0:T(8,128)(2,1)S(1)}, u32[]{:S(2)}, u32[]{:S(2)}) collective-permute-start(bf16[1,64,1024]{2,1,0:T(8,128)(2,1)S(1)} %unpack.1.mixed_ref), channel_id=1, source_target_pairs={{0,24},{1,25},{2,26},{3,27},{4,28},{5,29},{6,30},{7,31},{8,16},{9,... | collective-permute-start | bytes 393224 | tf_op jit(solution)/shard_map/ppermute | solution.py:1057
  82.8 13.8 %all-to-all-start.1 = ((bf16[16,72,128]{2,1,0:T(8,128)(2,1)}), bf16[16,72,128]{2,1,0:T(8,128)(2,1)S(1)}, u32[]{:S(2)}, u32[]{:S(2)}) async-start(bf16[16,72,128]{2,1,0:T(8,128)(2,1)} %get-tuple-element.111), calls=%async_computation.1 | async-start | bytes 589824 | tf_op jit(solution)/shard_map/all_to_all | solution.py:1054
  86.6 14.5 %collective-permute-start.19 = (bf16[4,64,1024]{2,1,0:T(8,128)(2,1)S(1)}, bf16[4,64,1024]{2,1,0:T(8,128)(2,1)S(1)}, u32[]{:S(2)}, u32[]{:S(2)}) collective-permute-start(bf16[4,64,1024]{2,1,0:T(8,128)(2,1)S(1)} %pad_maximum_fusion.2.rest_9_), channel_id=1, source_target_pairs={{0,4},{1,5},{2,6},{3,7},{4,0},{5,1},{6,2},{7,3},{8,12},{9,13},{10,... | collective-permute-start | bytes 1572872 | tf_op jit(solution)/shard_map/ppermute | solution.py:1057
  88.2 14.3 %collective-permute-start.18 = (bf16[4,64,1024]{2,1,0:T(8,128)(2,1)S(1)}, bf16[4,64,1024]{2,1,0:T(8,128)(2,1)}, u32[]{:S(2)}, u32[]{:S(2)}) collective-permute-start(bf16[4,64,1024]{2,1,0:T(8,128)(2,1)S(1)} %pad_maximum_fusion.2.rest_9_), channel_id=1, source_target_pairs={{0,2},{1,3},{2,0},{3,1},{4,6},{5,7},{6,4},{7,5},{8,10},{9,11},{10,... | collective-permute-start | bytes 1572872 | tf_op jit(solution)/shard_map/ppermute | solution.py:1057
  101.1 10.1 %collective-permute-start.20 = (bf16[2,64,1024]{2,1,0:T(8,128)(2,1)S(1)}, bf16[2,64,1024]{2,1,0:T(8,128)(2,1)S(1)}, u32[]{:S(2)}, u32[]{:S(2)}) collective-permute-start(bf16[2,64,1024]{2,1,0:T(8,128)(2,1)S(1)} %slice.18), channel_id=1, source_target_pairs={{0,2},{1,3},{2,0},{3,1},{4,6},{5,7},{6,4},{7,5},{8,10},{9,11},{10,... | collective-permute-start | bytes 786440 | tf_op jit(solution)/shard_map/ppermute | solution.py:1057
  103.5 7.7 %collective-permute-start.21 = (bf16[2,64,1024]{2,1,0:T(8,128)(2,1)S(1)}, bf16[2,64,1024]{2,1,0:T(8,128)(2,1)S(1)}, u32[]{:S(2)}, u32[]{:S(2)}) collective-permute-start(bf16[2,64,1024]{2,1,0:T(8,128)(2,1)S(1)} %slice.19), channel_id=1, source_target_pairs={{0,4},{1,5},{2,6},{3,7},{4,0},{5,1},{6,2},{7,3},{8,12},{9,13},{10,... | collective-permute-start | bytes 786440 | tf_op jit(solution)/shard_map/ppermute | solution.py:1057
  106.2 25.0 %all-to-all-start.2 = ((bf16[16,96,128]{2,1,0:T(8,128)(2,1)}), bf16[16,96,128]{2,1,0:T(8,128)(2,1)S(1)}, u32[]{:S(2)}, u32[]{:S(2)}) async-start(bf16[16,96,128]{2,1,0:T(8,128)(2,1)} %get-tuple-element.120.dqkv_ref), calls=%async_computation.2 | async-start | bytes 786432 | tf_op jit(solution)/shard_map/all_to_all | solution.py:1054
  131.3 22.9 %all-to-all-start.3 = ((bf16[16,136,128]{2,1,0:T(8,128)(2,1)}), bf16[16,136,128]{2,1,0:T(8,128)(2,1)S(1)}, u32[]{:S(2)}, u32[]{:S(2)}) async-start(bf16[16,136,128]{2,1,0:T(8,128)(2,1)} %merge.1), calls=%async_computation.3 | async-start | bytes 1114112 | tf_op jit(solution)/shard_map/all_to_all | solution.py:1054
  (32 other events, 450.7 us)

commit v4 on v3

--- a/solution.py
+++ b/solution.py
@@ -654,9 +654,22 @@
 PIECES = (5, 4, 5)
 
 
+def early_kernel(both_ref, down_ref, product_ref, w_down, sems):
+    cols = down_ref.shape[0] // CHUNKS
+    parts = [pl.ds(c * cols, cols) for c in range(CHUNKS)]
+    copies = [pltpu.make_async_copy(down_ref.at[p, :], w_down.at[p, :], sems.at[c]) for c, p in enumerate(parts)]
+    for copy in copies:
+        copy.start()
+    upstream = both_ref[0, both_ref.shape[1] // 2 :, :]
+    for c, copy in enumerate(copies):
+        copy.wait()
+        part = slice(c * cols, (c + 1) * cols)
+        product_ref[:, part] = nt(upstream, w_down[part, :])
+
+
 def middle_kernel(
-    own_ref, counts_ref, mixed_ref, total_ref, both_ref, vectors_ref, out_ref, up_ref, down_ref,
-    sent_ref, active_ref, attn_ref, dmiddle_ref, dweight_ref, w_out, w_up, w_down, hidden_ref, sems,
+    own_ref, counts_ref, mixed_ref, total_ref, both_ref, vectors_ref, product_ref, out_ref, up_ref,
+    sent_ref, active_ref, attn_ref, dmiddle_ref, dweight_ref, w_out, w_up, sems,
 ):
     width, total_cols = up_ref.shape
     cols = total_cols // CHUNKS
@@ -664,9 +677,6 @@
     for c in range(CHUNKS):
         part = pl.ds(c * cols, cols)
         copies.append(pltpu.make_async_copy(up_ref.at[:, part], w_up.at[:, part], sems.at[1 + c]))
-    for c in range(CHUNKS):
-        part = pl.ds(c * cols, cols)
-        copies.append(pltpu.make_async_copy(down_ref.at[part, :], w_down.at[part, :], sems.at[1 + CHUNKS + c]))
     for copy in copies:
         copy.start()
     capacity = mixed_ref.shape[1]
@@ -678,7 +688,6 @@
     scaling = gate * ratio
     gain = vectors_ref[2:3, :]
     dbranch = scaling * upstream
-    upstream_low = both_ref[0, capacity:, :]
     copies[0].wait()
     attn_out = nn(mixed_ref[0], w_out[...])
     attn_ref[...] = attn_out
@@ -686,21 +695,16 @@
     middle = rows + attn_out
     scale = inverse_rms(middle)
     normed = (middle * scale * gain).astype(bf16)
-    for c in range(CHUNKS):
-        copies[1 + c].wait()
-        hidden_ref[:, c * cols : (c + 1) * cols] = nn(normed, w_up[:, c * cols : (c + 1) * cols])
     dnormed = jnp.zeros((capacity, width), f32)
     for c in range(CHUNKS):
         part = slice(c * cols, (c + 1) * cols)
-        copies[1 + CHUNKS + c].wait()
-        hidden = hidden_ref[:, part]
-        value, slope = gelu_pair(hidden)
+        copies[1 + c].wait()
+        value, slope = gelu_pair(nn(normed, w_up[:, part]))
         active = value.astype(bf16)
         active_ref[:, part] = active
-        product = nt(upstream_low, w_down[part, :])
+        product = product_ref[:, part]
         dweight = dweight + jnp.sum(active.astype(f32) * product, axis=1, keepdims=True)
-        dhidden = (scaling * product * slope).astype(bf16)
-        dnormed = dnormed + nt(dhidden, w_up[:, part])
+        dnormed = dnormed + nt((scaling * product * slope).astype(bf16), w_up[:, part])
     dweight_ref[...] = jnp.broadcast_to(dweight, dweight_ref.shape)
     scaled = gain * dnormed
     dmiddle = scale * scaled - middle * (scale * scale * scale) * jnp.mean(scaled * middle, axis=-1, keepdims=True)
@@ -983,7 +987,7 @@
 smem = pl.BlockSpec(memory_space=pltpu.SMEM)
 hbm = pl.BlockSpec(memory_space=pl.ANY)
 megabytes = {
-    "places": 4, "fetch": 56, "project": 16, "attend": 20, "unpack": 4, "middle": 56, "put": 56, "attend_back": 24,
+    "places": 4, "early": 56, "fetch": 56, "project": 16, "attend": 20, "unpack": 4, "middle": 56, "put": 56, "attend_back": 24,
     "keys": 8, "units": 56, "merge": 10, "rows": 56, "finish": 12,
 }
 
@@ -997,7 +1001,7 @@
 
 
 microseconds = {
-    "places": 1, "fetch": 3, "project": 4, "attend": 5, "unpack": 2, "middle": 15, "put": 6, "attend_back": 6, "keys": 2,
+    "places": 1, "early": 5, "fetch": 3, "project": 4, "attend": 5, "unpack": 2, "middle": 11, "put": 6, "attend_back": 6, "keys": 2,
     "units": 16, "merge": 3, "rows": 7, "finish": 2,
 }
 
@@ -1076,7 +1080,11 @@
         (own_id, counts, chosen, tokens_in, out_grad),
     )
     rows_line = line_of(own_rows)
-    chosen_after, rows_line = lax.optimization_barrier((chosen, rows_line))
+    product = call(
+        early_kernel, "early", [vmem, hbm], shaped((capacity, hidden_width), f32), (both, w_down),
+        [pltpu.VMEM((hidden_width, width), bf16), pltpu.SemaphoreType.DMA((CHUNKS,))],
+    )
+    chosen_after, product, rows_line = lax.optimization_barrier((chosen, product, rows_line))
     kpos, qpos, qlow = call(
         places_kernel, "places", [smem] * 3 + [vmem],
         (
@@ -1115,7 +1123,7 @@
     mixed = call(unpack_kernel, "unpack", [vmem], shaped((1, capacity, width), bf16), (mixed_got,))
     mixed_line = line_of(mixed)
     sent, active, attn_out, dmiddle, dweight = call(
-        middle_kernel, "middle", [smem, smem] + [vmem] * 4 + [hbm] * 3,
+        middle_kernel, "middle", [smem, smem] + [vmem] * 5 + [hbm] * 2,
         (
             shaped((chips, 2 * HALF + NOTE, LANES), bf16),
             shaped((capacity, hidden_width), bf16),
@@ -1123,13 +1131,11 @@
             shaped((capacity, width), f32),
             shaped((capacity, LANES), f32),
         ),
-        (own_id, counts, mixed, total, both, vectors, w_out, w_up, w_down),
+        (own_id, counts, mixed, total, both, vectors, product, w_out, w_up),
         [
             square,
             pltpu.VMEM((width, hidden_width), bf16),
-            pltpu.VMEM((hidden_width, width), bf16),
-            pltpu.VMEM((capacity, hidden_width), f32),
-            pltpu.SemaphoreType.DMA((1 + 2 * CHUNKS,)),
+            pltpu.SemaphoreType.DMA((1 + CHUNKS,)),
         ],
     )
     mixed_line, sent = lax.optimization_barrier((mixed_line, sent))

time: 156 us -> 152 us (0.974)
  waiting for transfers between devices: 33.8 us -> 27.2 us
  Pallas kernels: 58.7 us -> 62.4 us
    ppermute x24, waiting for transfers between devices: 27 us -> 20.3 us  [across(): return lax.ppermute(value, 'seq', [(s, s ^ bits) for s in range(devices)])]
    pallas_call x12 -> x13, Pallas kernels: 43.8 us -> 47.6 us  [call(): pl.pallas_call(kernel, out_shape=out_shape, in_specs=in_specs, out_specs=...]
  transfers between devices with their start and end apart: 28 -> 28, of which waited for: 13 -> 12; matrix products, arithmetic and copies ran while one was open for 5% -> 6% of each run, Pallas kernels for 34% -> 37%
where the time goes in v4:
time: 152 us; the launch traced here: 151 us
  Pallas kernels  62.4 us (41%)
  starting transfers between devices  49.5 us (33%)
  waiting for transfers between devices  27.2 us (18%)
  local copies, waits for them, and re-layouts  9.11 us (6%)
  other arithmetic  2.06 us (1%)
    pallas_call x13, Pallas kernels, call(): pl.pallas_call(kernel, out_shape=out_shape, in_specs=in_specs, out_specs=...  47.6 us
    ppermute x24, starting transfers between devices, across(): return lax.ppermute(value, 'seq', [(s, s ^ bits) for s in range(devices)])  28.4 us
    all_to_all x4, starting transfers between devices, swap(): lax.all_to_all(value, 'seq', split_axis=0, concat_axis=0, tiled=True, axi...  21.1 us
    ppermute x24, waiting for transfers between devices, across(): return lax.ppermute(value, 'seq', [(s, s ^ bits) for s in range(devices)])  20.3 us
    pallas_call x1, Pallas kernels, pairs(): pl.pallas_call(units_kernel, out_shape=(shaped((hidden_cols // 2, width),...  14.9 us
    all_to_all x4, waiting for transfers between devices, swap(): lax.all_to_all(value, 'seq', split_axis=0, concat_axis=0, tiled=True, axi...  6.91 us
  transfers between devices with their start and end apart: 28, of which 12 were waited for; matrix products, arithmetic and copies ran while one was open for 6% of the time, Pallas kernels for 37%

profile of v4, /device:TPU:0, one launch (start us, length us, event | category | flops | bytes accessed | tf_op | source)
XLA Modules:
  0.0 151.4 jit_solution(9532936953959292260)
XLA Ops:
  0.6 2.9 %fetch.1 = (bf16[1,128,1024]{2,1,0:T(8,128)(2,1)}, bf16[1,64,1024]{2,1,0:T(8,128)(2,1)}, bf16[1,64,1024]{2,1,0:T(8,128)(2,1)}) custom-call(s32[1]{0:T(128)} %bitcast.own_ref, s32[32]{0:T(128)} %counts_ref.13, s32[16,128]{1,0:T(8,128)} %bitcast.7, bf16[512,1024]{1,0:T(8,128)(2,1)} %old_ref.2, bf16[512,1024]{1,0:T(8,128)(2,1)} %old_ref.3), custom_call_target="tpu_custom_call" | custom-call | bytes 9900000 | tf_op jit(solution)/shard_map/fetch/pallas_call | solution.py:1014
  3.6 3.0 %collective-permute-start = (bf16[1,64,1024]{2,1,0:T(8,128)(2,1)}, bf16[1,64,1024]{2,1,0:T(8,128)(2,1)S(1)}, u32[]{:S(2)}, u32[]{:S(2)}) collective-permute-start(bf16[1,64,1024]{2,1,0:T(8,128)(2,1)} %get-tuple-element.78), channel_id=1, source_target_pairs={{0,8},{1,9},{2,10},{3,11},{4,12},{5,13},{6,14},{7,15},{8,0},{9,1},... | collective-permute-start | bytes 393224 | tf_op jit(solution)/shard_map/ppermute | solution.py:1061
  6.6 2.6 %collective-permute-start.1 = (bf16[1,64,1024]{2,1,0:T(8,128)(2,1)}, bf16[1,64,1024]{2,1,0:T(8,128)(2,1)S(1)}, u32[]{:S(2)}, u32[]{:S(2)}) collective-permute-start(bf16[1,64,1024]{2,1,0:T(8,128)(2,1)} %get-tuple-element.78), channel_id=1, source_target_pairs={{0,16},{1,17},{2,18},{3,19},{4,20},{5,21},{6,22},{7,23},{8,24},{9,... | collective-permute-start | bytes 393224 | tf_op jit(solution)/shard_map/ppermute | solution.py:1061
  9.2 6.6 %early.1.product_ref = f32[64,4096]{1,0:T(8,128)} custom-call(bf16[1,128,1024]{2,1,0:T(8,128)(2,1)} %get-tuple-element.77.both_ref.rows_ref, bf16[4096,1024]{1,0:T(8,128)(2,1)} %down_ref.5), custom_call_target="tpu_custom_call" | custom-call | bytes 16500000 | tf_op jit(solution)/shard_map/early/pallas_call | solution.py:1014
  15.9 3.9 %collective-permute-done.1 = bf16[1,64,1024]{2,1,0:T(8,128)(2,1)S(1)} collective-permute-done((bf16[1,64,1024]{2,1,0:T(8,128)(2,1)}, bf16[1,64,1024]{2,1,0:T(8,128)(2,1)S(1)}, u32[]{:S(2)}, u32[]{:S(2)}) %collective-permute-start.1) | collective-permute-done | bytes 131104 | tf_op jit(solution)/shard_map/ppermute | solution.py:1061
  22.9 2.0 %collective-permute-start.7 = (bf16[1,64,1024]{2,1,0:T(8,128)(2,1)S(1)}, bf16[1,64,1024]{2,1,0:T(8,128)(2,1)S(1)}, u32[]{:S(2)}, u32[]{:S(2)}) collective-permute-start(bf16[1,64,1024]{2,1,0:T(8,128)(2,1)S(1)} %copy-done.22), channel_id=1, source_target_pairs={{0,8},{1,9},{2,10},{3,11},{4,12},{5,13},{6,14},{7,15},{8,0},{9,1},... | collective-permute-start | bytes 393224 | tf_op jit(solution)/shard_map/ppermute | solution.py:1061
  28.4 2.7 %collective-permute-done.4.rest_2_ = bf16[4,64,1024]{2,1,0:T(8,128)(2,1)S(1)} collective-permute-done((bf16[4,64,1024]{2,1,0:T(8,128)(2,1)S(1)}, bf16[4,64,1024]{2,1,0:T(8,128)(2,1)S(1)}, u32[]{:S(2)}, u32[]{:S(2)}) %collective-permute-start.4) | collective-permute-done | bytes 524320 | tf_op jit(solution)/shard_map/ppermute | solution.py:1061
  37.9 2.9 %collective-permute-done.6.rest_4_ = bf16[2,64,1024]{2,1,0:T(8,128)(2,1)S(1)} collective-permute-done((bf16[2,64,1024]{2,1,0:T(8,128)(2,1)S(1)}, bf16[2,64,1024]{2,1,0:T(8,128)(2,1)S(1)}, u32[]{:S(2)}, u32[]{:S(2)}) %collective-permute-start.6) | collective-permute-done | bytes 262176 | tf_op jit(solution)/shard_map/ppermute | solution.py:1061
  40.8 2.2 %project.1.got_ref = bf16[16,104,128]{2,1,0:T(8,128)(2,1)S(1)} custom-call(s32[1]{0:T(128)} %bitcast.own_ref, s32[32]{0:T(128)S(1)} %copy-done.11, f32[3,1024]{1,0:T(4,128)S(1)} %maximum_convert_fusion.vectors_ref, bf16[1024,128]{1,0:T(8,128)(2,1)S(1)} %constant_dynamic-slice_fusion.7.wq, bf16[1024,128]{1,0:T(8,128)(2,1)S(1)} %get-tuple-element.91.wk, ...), custom_call_target="tpu_custom_call" | custom-call | bytes 13200000 | tf_op jit(solution)/shard_map/project/pallas_call | solution.py:1014
  44.9 3.7 %attend.1 = (bf16[512,128]{1,0:T(8,128)(2,1)}, f32[512,128]{1,0:T(8,128)S(1)}, f32[4,256]{1,0:T(4,128)S(1)}, f32[8,128]{1,0:T(8,128)S(1)}) custom-call(bf16[16,104,128]{2,1,0:T(8,128)(2,1)S(1)} %project.1.got_ref, bf16[16,104,128]{2,1,0:T(8,128)(2,1)S(1)} %collective-permute-done.10.other_ref, f32[2,1024]{1,0:T(2,128)S(1)} %get-tuple-element.98.kpos_ref, ...), custom_call_target="tpu_custom_call" | custom-call | bytes 16500000 | tf_op jit(solution)/shard_map/attend/pallas_call | solution.py:1014
  48.6 5.6 %all-to-all-start = ((bf16[16,32,128]{2,1,0:T(8,128)(2,1)}), bf16[16,32,128]{2,1,0:T(8,128)(2,1)S(1)}, u32[]{:S(2)}, u32[]{:S(2)}) async-start(bf16[16,32,128]{2,1,0:T(8,128)(2,1)} %bitcast.2), calls=%async_computation | async-start | bytes 262144 | tf_op jit(solution)/shard_map/all_to_all | solution.py:1058
  54.2 3.4 %collective-permute-done.11.rest_6_ = bf16[4,64,1024]{2,1,0:T(8,128)(2,1)S(1)} collective-permute-done((bf16[4,64,1024]{2,1,0:T(8,128)(2,1)S(1)}, bf16[4,64,1024]{2,1,0:T(8,128)(2,1)S(1)}, u32[]{:S(2)}, u32[]{:S(2)}) %collective-permute-start.11) | collective-permute-done | bytes 524320 | tf_op jit(solution)/shard_map/ppermute | solution.py:1061
  59.3 2.7 %all-to-all-done.got_ref = bf16[16,32,128]{2,1,0:T(8,128)(2,1)S(1)} async-done(((bf16[16,32,128]{2,1,0:T(8,128)(2,1)}), bf16[16,32,128]{2,1,0:T(8,128)(2,1)S(1)}, u32[]{:S(2)}, u32[]{:S(2)}) %all-to-all-start) | async-done | bytes 131104 | tf_op jit(solution)/shard_map/all_to_all | solution.py:1058
  64.6 3.0 %collective-permute-start.16 = (bf16[1,64,1024]{2,1,0:T(8,128)(2,1)S(1)}, bf16[1,64,1024]{2,1,0:T(8,128)(2,1)S(1)}, u32[]{:S(2)}, u32[]{:S(2)}) collective-permute-start(bf16[1,64,1024]{2,1,0:T(8,128)(2,1)S(1)} %unpack.1.mixed_ref), channel_id=1, source_target_pairs={{0,24},{1,25},{2,26},{3,27},{4,28},{5,29},{6,30},{7,31},{8,16},{9,... | collective-permute-start | bytes 393224 | tf_op jit(solution)/shard_map/ppermute | solution.py:1061
  67.7 10.3 %middle.1 = (bf16[16,72,128]{2,1,0:T(8,128)(2,1)}, bf16[64,4096]{1,0:T(8,128)(2,1)}, f32[64,1024]{1,0:T(8,128)}, f32[64,1024]{1,0:T(8,128)}, f32[64,128]{1,0:T(8,128)}) custom-call(s32[1]{0:T(128)} %bitcast.own_ref, s32[32]{0:T(128)} %counts_ref.13, bf16[1,64,1024]{2,1,0:T(8,128)(2,1)} %copy-done.4, f32[8,128]{1,0:T(8,128)} %copy-done.10, ...), custom_call_target="tpu_custom_call" | custom-call | bytes 36300000 | tf_op jit(solution)/shard_map/middle/pallas_call | solution.py:1014
  79.0 3.5 %all-to-all-start.1 = ((bf16[16,72,128]{2,1,0:T(8,128)(2,1)}), bf16[16,72,128]{2,1,0:T(8,128)(2,1)S(1)}, u32[]{:S(2)}, u32[]{:S(2)}) async-start(bf16[16,72,128]{2,1,0:T(8,128)(2,1)} %get-tuple-element.113), calls=%async_computation.1 | async-start | bytes 589824 | tf_op jit(solution)/shard_map/all_to_all | solution.py:1058
  85.9 6.8 %put.1 = bf16[512,1024]{1,0:T(8,128)(2,1)} custom-call(s32[1]{0:T(128)} %bitcast.own_ref, s32[32]{0:T(128)} %counts_ref.13, s32[16,128]{1,0:T(8,128)} %bitcast.8, f32[8,128]{1,0:T(8,128)} %copy-done.10, bf16[1,128,1024]{2,1,0:T(8,128)(2,1)} %get-tuple-element.77.both_ref.rows_ref, f32[3,1024]{1,0:T(4,128)} %copy-done.7, ...), custom_call_target="tpu_custom_call" | custom-call | bytes 19800000 | tf_op jit(solution)/shard_map/put/pallas_call | solution.py:1014
  92.7 3.8 %attend_back.1 = (bf16[512,128]{1,0:T(8,128)(2,1)S(1)}, f32[1024,128]{1,0:T(8,128)S(1)}, f32[1032,128]{1,0:T(8,128)S(1)}, f32[8,128]{1,0:T(8,128)S(1)}) custom-call(bf16[16,104,128]{2,1,0:T(8,128)(2,1)S(1)} %project.1.got_ref, bf16[16,104,128]{2,1,0:T(8,128)(2,1)S(1)} %collective-permute-done.10.other_ref, ...), custom_call_target="tpu_custom_call" | custom-call | bytes 19800000 | tf_op jit(solution)/shard_map/attend_back/pallas_call | solution.py:1014
  102.3 5.0 %all-to-all-start.2 = ((bf16[16,96,128]{2,1,0:T(8,128)(2,1)}), bf16[16,96,128]{2,1,0:T(8,128)(2,1)S(1)}, u32[]{:S(2)}, u32[]{:S(2)}) async-start(bf16[16,96,128]{2,1,0:T(8,128)(2,1)} %get-tuple-element.122.dqkv_ref), calls=%async_computation.2 | async-start | bytes 786432 | tf_op jit(solution)/shard_map/all_to_all | solution.py:1058
  108.2 14.9 %units.1 = (f32[128,1024]{1,0:T(8,128)}, bf16[128,1024]{1,0:T(8,128)(2,1)}, bf16[16,136,128]{2,1,0:T(8,128)(2,1)}, bf16[16,136,128]{2,1,0:T(8,128)(2,1)}) custom-call(s32[1]{0:T(128)} %bitcast.own_ref, s32[32]{0:T(128)} %counts_ref.13, bf16[16,72,128]{2,1,0:T(8,128)(2,1)} %copy-done.3, bf16[16,96,128]{2,1,0:T(8,128)(2,1)} %get-tuple-element.122.dqkv_ref, ...), custom_call_target="tpu_custom_call" | custom-call | bytes 52800000 | tf_op jit(solution)/shard_map/units/pallas_call | solution.py:1172
  123.2 2.2 %collective-permute-done.22.moved_ref = bf16[16,136,128]{2,1,0:T(8,128)(2,1)S(1)} collective-permute-done((bf16[16,136,128]{2,1,0:T(8,128)(2,1)}, bf16[16,136,128]{2,1,0:T(8,128)(2,1)S(1)}, u32[]{:S(2)}, u32[]{:S(2)}) %collective-permute-start.22) | collective-permute-done | bytes 557088 | tf_op jit(solution)/shard_map/ppermute | solution.py:1061
  127.4 6.9 %all-to-all-start.3 = ((bf16[16,136,128]{2,1,0:T(8,128)(2,1)}), bf16[16,136,128]{2,1,0:T(8,128)(2,1)S(1)}, u32[]{:S(2)}, u32[]{:S(2)}) async-start(bf16[16,136,128]{2,1,0:T(8,128)(2,1)} %merge.1), calls=%async_computation.3 | async-start | bytes 1114112 | tf_op jit(solution)/shard_map/all_to_all | solution.py:1058
  138.7 7.4 %rows.1 = bf16[512,1024]{1,0:T(8,128)(2,1)} custom-call(s32[1]{0:T(128)} %bitcast.own_ref, s32[32]{0:T(128)} %counts_ref.13, s32[16,128]{1,0:T(8,128)} %bitcast.9, bf16[16,96,128]{2,1,0:T(8,128)(2,1)} %copy-done.15, bf16[1,128,1024]{2,1,0:T(8,128)(2,1)} %get-tuple-element.77.both_ref.rows_ref, f32[64,1024]{1,0:T(8,128)} %get-tuple-element.123.dmiddle_ref, ...), custom_call_target="tpu_custom_call" | custom-call | bytes 23100000 | tf_op jit(solution)/shard_map/rows/pallas_call | solution.py:1014
  146.1 4.2 %all-to-all-done.3.got_ref = bf16[16,136,128]{2,1,0:T(8,128)(2,1)S(1)} async-done(((bf16[16,136,128]{2,1,0:T(8,128)(2,1)}), bf16[16,136,128]{2,1,0:T(8,128)(2,1)S(1)}, u32[]{:S(2)}, u32[]{:S(2)}) %all-to-all-start.3) | async-done | bytes 557088 | tf_op jit(solution)/shard_map/all_to_all | solution.py:1058
  (123 shorter events, 38.1 us)
Async XLA Ops:
  3.6 12.3 %collective-permute-start = (bf16[1,64,1024]{2,1,0:T(8,128)(2,1)}, bf16[1,64,1024]{2,1,0:T(8,128)(2,1)S(1)}, u32[]{:S(2)}, u32[]{:S(2)}) collective-permute-start(bf16[1,64,1024]{2,1,0:T(8,128)(2,1)} %get-tuple-element.78), channel_id=1, source_target_pairs={{0,8},{1,9},{2,10},{3,11},{4,12},{5,13},{6,14},{7,15},{8,0},{9,1},... | collective-permute-start | bytes 393224 | tf_op jit(solution)/shard_map/ppermute | solution.py:1061
  6.6 13.2 %collective-permute-start.1 = (bf16[1,64,1024]{2,1,0:T(8,128)(2,1)}, bf16[1,64,1024]{2,1,0:T(8,128)(2,1)S(1)}, u32[]{:S(2)}, u32[]{:S(2)}) collective-permute-start(bf16[1,64,1024]{2,1,0:T(8,128)(2,1)} %get-tuple-element.78), channel_id=1, source_target_pairs={{0,16},{1,17},{2,18},{3,19},{4,20},{5,21},{6,22},{7,23},{8,24},{9,... | collective-permute-start | bytes 393224 | tf_op jit(solution)/shard_map/ppermute | solution.py:1061
  9.2 10.6 %collective-permute-start.2 = (bf16[1,64,1024]{2,1,0:T(8,128)(2,1)}, bf16[1,64,1024]{2,1,0:T(8,128)(2,1)S(1)}, u32[]{:S(2)}, u32[]{:S(2)}) collective-permute-start(bf16[1,64,1024]{2,1,0:T(8,128)(2,1)} %get-tuple-element.78), channel_id=1, source_target_pairs={{0,24},{1,25},{2,26},{3,27},{4,28},{5,29},{6,30},{7,31},{8,16},{9,... | collective-permute-start | bytes 393224 | tf_op jit(solution)/shard_map/ppermute | solution.py:1061
  19.8 11.3 %collective-permute-start.4 = (bf16[4,64,1024]{2,1,0:T(8,128)(2,1)S(1)}, bf16[4,64,1024]{2,1,0:T(8,128)(2,1)S(1)}, u32[]{:S(2)}, u32[]{:S(2)}) collective-permute-start(bf16[4,64,1024]{2,1,0:T(8,128)(2,1)S(1)} %pad_maximum_fusion.rest_0_), channel_id=1, source_target_pairs={{0,4},{1,5},{2,6},{3,7},{4,0},{5,1},{6,2},{7,3},{8,12},{9,13},{10,... | collective-permute-start | bytes 1572872 | tf_op jit(solution)/shard_map/ppermute | solution.py:1061
  21.4 13.0 %collective-permute-start.3 = (bf16[4,64,1024]{2,1,0:T(8,128)(2,1)S(1)}, bf16[4,64,1024]{2,1,0:T(8,128)(2,1)S(1)}, u32[]{:S(2)}, u32[]{:S(2)}) collective-permute-start(bf16[4,64,1024]{2,1,0:T(8,128)(2,1)S(1)} %pad_maximum_fusion.rest_0_), channel_id=1, source_target_pairs={{0,2},{1,3},{2,0},{3,1},{4,6},{5,7},{6,4},{7,5},{8,10},{9,11},{10,... | collective-permute-start | bytes 1572872 | tf_op jit(solution)/shard_map/ppermute | solution.py:1061
  22.9 13.8 %collective-permute-start.7 = (bf16[1,64,1024]{2,1,0:T(8,128)(2,1)S(1)}, bf16[1,64,1024]{2,1,0:T(8,128)(2,1)S(1)}, u32[]{:S(2)}, u32[]{:S(2)}) collective-permute-start(bf16[1,64,1024]{2,1,0:T(8,128)(2,1)S(1)} %copy-done.22), channel_id=1, source_target_pairs={{0,8},{1,9},{2,10},{3,11},{4,12},{5,13},{6,14},{7,15},{8,0},{9,1},... | collective-permute-start | bytes 393224 | tf_op jit(solution)/shard_map/ppermute | solution.py:1061
  24.9 11.9 %collective-permute-start.8 = (bf16[1,64,1024]{2,1,0:T(8,128)(2,1)S(1)}, bf16[1,64,1024]{2,1,0:T(8,128)(2,1)S(1)}, u32[]{:S(2)}, u32[]{:S(2)}) collective-permute-start(bf16[1,64,1024]{2,1,0:T(8,128)(2,1)S(1)} %copy-done.22), channel_id=1, source_target_pairs={{0,16},{1,17},{2,18},{3,19},{4,20},{5,21},{6,22},{7,23},{8,24},{9,... | collective-permute-start | bytes 393224 | tf_op jit(solution)/shard_map/ppermute | solution.py:1061
  25.9 10.9 %collective-permute-start.9 = (bf16[1,64,1024]{2,1,0:T(8,128)(2,1)S(1)}, bf16[1,64,1024]{2,1,0:T(8,128)(2,1)S(1)}, u32[]{:S(2)}, u32[]{:S(2)}) collective-permute-start(bf16[1,64,1024]{2,1,0:T(8,128)(2,1)S(1)} %copy-done.22), channel_id=1, source_target_pairs={{0,24},{1,25},{2,26},{3,27},{4,28},{5,29},{6,30},{7,31},{8,16},{9,... | collective-permute-start | bytes 393224 | tf_op jit(solution)/shard_map/ppermute | solution.py:1061
  31.1 6.8 %collective-permute-start.5 = (bf16[2,64,1024]{2,1,0:T(8,128)(2,1)S(1)}, bf16[2,64,1024]{2,1,0:T(8,128)(2,1)S(1)}, u32[]{:S(2)}, u32[]{:S(2)}) collective-permute-start(bf16[2,64,1024]{2,1,0:T(8,128)(2,1)S(1)} %slice.16), channel_id=1, source_target_pairs={{0,2},{1,3},{2,0},{3,1},{4,6},{5,7},{6,4},{7,5},{8,10},{9,11},{10,... | collective-permute-start | bytes 786440 | tf_op jit(solution)/shard_map/ppermute | solution.py:1061
  34.4 6.4 %collective-permute-start.6 = (bf16[2,64,1024]{2,1,0:T(8,128)(2,1)S(1)}, bf16[2,64,1024]{2,1,0:T(8,128)(2,1)S(1)}, u32[]{:S(2)}, u32[]{:S(2)}) collective-permute-start(bf16[2,64,1024]{2,1,0:T(8,128)(2,1)S(1)} %slice.17), channel_id=1, source_target_pairs={{0,4},{1,5},{2,6},{3,7},{4,0},{5,1},{6,2},{7,3},{8,12},{9,13},{10,... | collective-permute-start | bytes 786440 | tf_op jit(solution)/shard_map/ppermute | solution.py:1061
  43.1 14.5 %collective-permute-start.11 = (bf16[4,64,1024]{2,1,0:T(8,128)(2,1)S(1)}, bf16[4,64,1024]{2,1,0:T(8,128)(2,1)S(1)}, u32[]{:S(2)}, u32[]{:S(2)}) collective-permute-start(bf16[4,64,1024]{2,1,0:T(8,128)(2,1)S(1)} %pad_maximum_fusion.1.rest_5_), channel_id=1, source_target_pairs={{0,2},{1,3},{2,0},{3,1},{4,6},{5,7},{6,4},{7,5},{8,10},{9,11},{10,... | collective-permute-start | bytes 1572872 | tf_op jit(solution)/shard_map/ppermute | solution.py:1061
  44.7 14.6 %collective-permute-start.12 = (bf16[4,64,1024]{2,1,0:T(8,128)(2,1)S(1)}, bf16[4,64,1024]{2,1,0:T(8,128)(2,1)S(1)}, u32[]{:S(2)}, u32[]{:S(2)}) collective-permute-start(bf16[4,64,1024]{2,1,0:T(8,128)(2,1)S(1)} %pad_maximum_fusion.1.rest_5_), channel_id=1, source_target_pairs={{0,4},{1,5},{2,6},{3,7},{4,0},{5,1},{6,2},{7,3},{8,12},{9,13},{10,... | collective-permute-start | bytes 1572872 | tf_op jit(solution)/shard_map/ppermute | solution.py:1061
  48.6 13.4 %all-to-all-start = ((bf16[16,32,128]{2,1,0:T(8,128)(2,1)}), bf16[16,32,128]{2,1,0:T(8,128)(2,1)S(1)}, u32[]{:S(2)}, u32[]{:S(2)}) async-start(bf16[16,32,128]{2,1,0:T(8,128)(2,1)} %bitcast.2), calls=%async_computation | async-start | bytes 262144 | tf_op jit(solution)/shard_map/all_to_all | solution.py:1058
  62.0 17.0 %collective-permute-start.13 = (bf16[4,64,1024]{2,1,0:T(8,128)(2,1)S(1)}, bf16[4,64,1024]{2,1,0:T(8,128)(2,1)}, u32[]{:S(2)}, u32[]{:S(2)}) collective-permute-start(bf16[4,64,1024]{2,1,0:T(8,128)(2,1)S(1)} %collective-permute-done.12.rest_7_), channel_id=1, source_target_pairs={{0,2},{1,3},{2,0},{3,1},{4,6},{5,7},{6,4},{7,5},{8,10},{9,11},{10,... | collective-permute-start | bytes 1572872 | tf_op jit(solution)/shard_map/ppermute | solution.py:1061
  63.2 14.7 %collective-permute-start.14 = (bf16[1,64,1024]{2,1,0:T(8,128)(2,1)S(1)}, bf16[1,64,1024]{2,1,0:T(8,128)(2,1)S(1)}, u32[]{:S(2)}, u32[]{:S(2)}) collective-permute-start(bf16[1,64,1024]{2,1,0:T(8,128)(2,1)S(1)} %unpack.1.mixed_ref), channel_id=1, source_target_pairs={{0,8},{1,9},{2,10},{3,11},{4,12},{5,13},{6,14},{7,15},{8,0},{9,1},... | collective-permute-start | bytes 393224 | tf_op jit(solution)/shard_map/ppermute | solution.py:1061
  63.5 14.5 %collective-permute-start.15 = (bf16[1,64,1024]{2,1,0:T(8,128)(2,1)S(1)}, bf16[1,64,1024]{2,1,0:T(8,128)(2,1)S(1)}, u32[]{:S(2)}, u32[]{:S(2)}) collective-permute-start(bf16[1,64,1024]{2,1,0:T(8,128)(2,1)S(1)} %unpack.1.mixed_ref), channel_id=1, source_target_pairs={{0,16},{1,17},{2,18},{3,19},{4,20},{5,21},{6,22},{7,23},{8,24},{9,... | collective-permute-start | bytes 393224 | tf_op jit(solution)/shard_map/ppermute | solution.py:1061
  64.6 13.3 %collective-permute-start.16 = (bf16[1,64,1024]{2,1,0:T(8,128)(2,1)S(1)}, bf16[1,64,1024]{2,1,0:T(8,128)(2,1)S(1)}, u32[]{:S(2)}, u32[]{:S(2)}) collective-permute-start(bf16[1,64,1024]{2,1,0:T(8,128)(2,1)S(1)} %unpack.1.mixed_ref), channel_id=1, source_target_pairs={{0,24},{1,25},{2,26},{3,27},{4,28},{5,29},{6,30},{7,31},{8,16},{9,... | collective-permute-start | bytes 393224 | tf_op jit(solution)/shard_map/ppermute | solution.py:1061
  79.0 13.7 %all-to-all-start.1 = ((bf16[16,72,128]{2,1,0:T(8,128)(2,1)}), bf16[16,72,128]{2,1,0:T(8,128)(2,1)S(1)}, u32[]{:S(2)}, u32[]{:S(2)}) async-start(bf16[16,72,128]{2,1,0:T(8,128)(2,1)} %get-tuple-element.113), calls=%async_computation.1 | async-start | bytes 589824 | tf_op jit(solution)/shard_map/all_to_all | solution.py:1058
  82.6 14.6 %collective-permute-start.19 = (bf16[4,64,1024]{2,1,0:T(8,128)(2,1)S(1)}, bf16[4,64,1024]{2,1,0:T(8,128)(2,1)S(1)}, u32[]{:S(2)}, u32[]{:S(2)}) collective-permute-start(bf16[4,64,1024]{2,1,0:T(8,128)(2,1)S(1)} %pad_maximum_fusion.2.rest_9_), channel_id=1, source_target_pairs={{0,4},{1,5},{2,6},{3,7},{4,0},{5,1},{6,2},{7,3},{8,12},{9,13},{10,... | collective-permute-start | bytes 1572872 | tf_op jit(solution)/shard_map/ppermute | solution.py:1061
  84.4 14.4 %collective-permute-start.18 = (bf16[4,64,1024]{2,1,0:T(8,128)(2,1)S(1)}, bf16[4,64,1024]{2,1,0:T(8,128)(2,1)}, u32[]{:S(2)}, u32[]{:S(2)}) collective-permute-start(bf16[4,64,1024]{2,1,0:T(8,128)(2,1)S(1)} %pad_maximum_fusion.2.rest_9_), channel_id=1, source_target_pairs={{0,2},{1,3},{2,0},{3,1},{4,6},{5,7},{6,4},{7,5},{8,10},{9,11},{10,... | collective-permute-start | bytes 1572872 | tf_op jit(solution)/shard_map/ppermute | solution.py:1061
  97.2 10.2 %collective-permute-start.20 = (bf16[2,64,1024]{2,1,0:T(8,128)(2,1)S(1)}, bf16[2,64,1024]{2,1,0:T(8,128)(2,1)S(1)}, u32[]{:S(2)}, u32[]{:S(2)}) collective-permute-start(bf16[2,64,1024]{2,1,0:T(8,128)(2,1)S(1)} %slice.18), channel_id=1, source_target_pairs={{0,2},{1,3},{2,0},{3,1},{4,6},{5,7},{6,4},{7,5},{8,10},{9,11},{10,... | collective-permute-start | bytes 786440 | tf_op jit(solution)/shard_map/ppermute | solution.py:1061
  99.7 7.7 %collective-permute-start.21 = (bf16[2,64,1024]{2,1,0:T(8,128)(2,1)S(1)}, bf16[2,64,1024]{2,1,0:T(8,128)(2,1)S(1)}, u32[]{:S(2)}, u32[]{:S(2)}) collective-permute-start(bf16[2,64,1024]{2,1,0:T(8,128)(2,1)S(1)} %slice.19), channel_id=1, source_target_pairs={{0,4},{1,5},{2,6},{3,7},{4,0},{5,1},{6,2},{7,3},{8,12},{9,13},{10,... | collective-permute-start | bytes 786440 | tf_op jit(solution)/shard_map/ppermute | solution.py:1061
  102.3 25.1 %all-to-all-start.2 = ((bf16[16,96,128]{2,1,0:T(8,128)(2,1)}), bf16[16,96,128]{2,1,0:T(8,128)(2,1)S(1)}, u32[]{:S(2)}, u32[]{:S(2)}) async-start(bf16[16,96,128]{2,1,0:T(8,128)(2,1)} %get-tuple-element.122.dqkv_ref), calls=%async_computation.2 | async-start | bytes 786432 | tf_op jit(solution)/shard_map/all_to_all | solution.py:1058
  127.4 22.9 %all-to-all-start.3 = ((bf16[16,136,128]{2,1,0:T(8,128)(2,1)}), bf16[16,136,128]{2,1,0:T(8,128)(2,1)S(1)}, u32[]{:S(2)}, u32[]{:S(2)}) async-start(bf16[16,136,128]{2,1,0:T(8,128)(2,1)} %merge.1), calls=%async_computation.3 | async-start | bytes 1114112 | tf_op jit(solution)/shard_map/all_to_all | solution.py:1058
  (33 other events, 365.8 us)

commit v5 on v4

--- a/solution.py
+++ b/solution.py
@@ -777,21 +777,23 @@
     slot = step % 2
 
     def copies(k):
-        at = k % 2
         result = []
         for i, pieces in enumerate(gathers):
-            if k < 3 or len(pieces) == 4:
-                result.append(pltpu.make_async_copy(pieces[k], slots[i].at[at], sems.at[at, i, 0]))
-                continue
-            for half in range(2):
-                target = slots[i].at[at, 2 * half : 2 * half + 2]
-                result.append(pltpu.make_async_copy(pieces[k + half], target, sems.at[at, i, half]))
+            for side in range(2):
+                piece = 2 * k + side
+                if piece < 3 or len(pieces) == 4:
+                    target = slots[i].at[k, 4 * side : 4 * side + 4]
+                    result.append(pltpu.make_async_copy(pieces[piece], target, sems.at[k, i, side, 0]))
+                    continue
+                for half in range(2):
+                    first = 4 * side + 2 * half
+                    target = slots[i].at[k, first : first + 2]
+                    result.append(pltpu.make_async_copy(pieces[piece + half], target, sems.at[k, i, side, half]))
         return result
 
-    for k in range(4):
-
-        @pl.when(step == max(k - 1, 0))
-        def _(k=k):
+    @pl.when(step == 0)
+    def _():
+        for k in range(2):
             for copy in copies(k):
                 copy.start()
 
@@ -801,7 +803,7 @@
             ref[...] = jnp.zeros_like(ref)
         ratio_ref[...] = jnp.broadcast_to(total_count(counts_ref) / total_ref[:1, :1], ratio_ref.shape)
 
-    for k in range(4):
+    for k in range(2):
 
         @pl.when(step == k)
         def _(k=k):
@@ -809,7 +811,7 @@
                 copy.wait()
 
     def halves(ref, first):
-        blocks = [ref[chip_of(own_ref, 4 * step + j), first : first + HALF, :] for j in range(sources)]
+        blocks = [ref[chip_of(own_ref, sources * step + j), first : first + HALF, :] for j in range(sources)]
         turned = jnp.transpose(jnp.concatenate(blocks, axis=0).astype(f32)).astype(bf16)
         return turned[:HEAD_DIM], turned[HEAD_DIM:]
 
@@ -824,7 +826,7 @@
     low_query, high_query = halves(dqkv_ref, 0)
     low_rows, high_rows = low_high(normed_attn)
     grad_q[...] += nn(low_query, low_rows) + nn(high_query, high_rows)
-    blocks = [dqkv_ref[chip_of(own_ref, 4 * step + j), HALF:, :] for j in range(sources)]
+    blocks = [dqkv_ref[chip_of(own_ref, sources * step + j), HALF:, :] for j in range(sources)]
     pairs_turned = jnp.transpose(jnp.concatenate(blocks, axis=0).astype(f32)).astype(bf16)
     grad_kv[...] += nn(pairs_turned, normed_attn)
     low_attn, high_attn = halves(got_ref, HALF)
@@ -1166,7 +1168,7 @@
         (dq.reshape(chips, HALF, LANES), dkv_own, moved, coef),
     )
     got = swap(dqkv)
-    sources = 4
+    sources = 8
     hidden_cols = hidden_width // chips
     whole = lambda *shape: pl.BlockSpec(shape, lambda i, o: (0,) * len(shape))
     down_keep, down_give, keep, give = pl.pallas_call(
@@ -1210,7 +1212,7 @@
                 pltpu.VMEM((HEAD_DIM, width), f32),
                 pltpu.VMEM((2 * HEAD_DIM, width), f32),
                 pltpu.VMEM((8, LANES), f32),
-                pltpu.SemaphoreType.DMA((2, 3, 2)),
+                pltpu.SemaphoreType.DMA((2, 3, 2, 2)),
             ],
         ),
         compiler_params=params_of("units"),

time: 152 us -> 152 us (level)
  no operation moved by 1% of the time
where the time goes in v5:
time: 152 us; the launch traced here: 151 us
  Pallas kernels  61.6 us (41%)
  starting transfers between devices  49.5 us (33%)
  waiting for transfers between devices  27.2 us (18%)
  local copies, waits for them, and re-layouts  9.11 us (6%)
  other arithmetic  2.06 us (1%)
    pallas_call x13, Pallas kernels, call(): pl.pallas_call(kernel, out_shape=out_shape, in_specs=in_specs, out_specs=...  47.6 us
    ppermute x24, starting transfers between devices, across(): return lax.ppermute(value, 'seq', [(s, s ^ bits) for s in range(devices)])  28.4 us
    all_to_all x4, starting transfers between devices, swap(): lax.all_to_all(value, 'seq', split_axis=0, concat_axis=0, tiled=True, axi...  21.1 us
    ppermute x24, waiting for transfers between devices, across(): return lax.ppermute(value, 'seq', [(s, s ^ bits) for s in range(devices)])  20.3 us
    pallas_call x1, Pallas kernels, pairs(): pl.pallas_call(units_kernel, out_shape=(shaped((hidden_cols // 2, width),...  14.1 us
    all_to_all x4, waiting for transfers between devices, swap(): lax.all_to_all(value, 'seq', split_axis=0, concat_axis=0, tiled=True, axi...  6.91 us
  transfers between devices with their start and end apart: 28, of which 12 were waited for; matrix products, arithmetic and copies ran while one was open for 6% of the time, Pallas kernels for 37%

profile of v5, /device:TPU:0, one launch (start us, length us, event | category | flops | bytes accessed | tf_op | source)
XLA Modules:
  0.0 150.7 jit_solution(80188882672516136)
XLA Ops:
  0.6 2.9 %fetch.1 = (bf16[1,128,1024]{2,1,0:T(8,128)(2,1)}, bf16[1,64,1024]{2,1,0:T(8,128)(2,1)}, bf16[1,64,1024]{2,1,0:T(8,128)(2,1)}) custom-call(s32[1]{0:T(128)} %bitcast.own_ref, s32[32]{0:T(128)} %counts_ref.13, s32[16,128]{1,0:T(8,128)} %bitcast.7, bf16[512,1024]{1,0:T(8,128)(2,1)} %old_ref.2, bf16[512,1024]{1,0:T(8,128)(2,1)} %old_ref.3), custom_call_target="tpu_custom_call" | custom-call | bytes 9900000 | tf_op jit(solution)/shard_map/fetch/pallas_call | solution.py:1016
  3.6 3.0 %collective-permute-start = (bf16[1,64,1024]{2,1,0:T(8,128)(2,1)}, bf16[1,64,1024]{2,1,0:T(8,128)(2,1)S(1)}, u32[]{:S(2)}, u32[]{:S(2)}) collective-permute-start(bf16[1,64,1024]{2,1,0:T(8,128)(2,1)} %get-tuple-element.78), channel_id=1, source_target_pairs={{0,8},{1,9},{2,10},{3,11},{4,12},{5,13},{6,14},{7,15},{8,0},{9,1},... | collective-permute-start | bytes 393224 | tf_op jit(solution)/shard_map/ppermute | solution.py:1063
  6.6 2.6 %collective-permute-start.1 = (bf16[1,64,1024]{2,1,0:T(8,128)(2,1)}, bf16[1,64,1024]{2,1,0:T(8,128)(2,1)S(1)}, u32[]{:S(2)}, u32[]{:S(2)}) collective-permute-start(bf16[1,64,1024]{2,1,0:T(8,128)(2,1)} %get-tuple-element.78), channel_id=1, source_target_pairs={{0,16},{1,17},{2,18},{3,19},{4,20},{5,21},{6,22},{7,23},{8,24},{9,... | collective-permute-start | bytes 393224 | tf_op jit(solution)/shard_map/ppermute | solution.py:1063
  9.2 6.6 %early.1.product_ref = f32[64,4096]{1,0:T(8,128)} custom-call(bf16[1,128,1024]{2,1,0:T(8,128)(2,1)} %get-tuple-element.77.both_ref.rows_ref, bf16[4096,1024]{1,0:T(8,128)(2,1)} %down_ref.5), custom_call_target="tpu_custom_call" | custom-call | bytes 16500000 | tf_op jit(solution)/shard_map/early/pallas_call | solution.py:1016
  15.9 3.9 %collective-permute-done.1 = bf16[1,64,1024]{2,1,0:T(8,128)(2,1)S(1)} collective-permute-done((bf16[1,64,1024]{2,1,0:T(8,128)(2,1)}, bf16[1,64,1024]{2,1,0:T(8,128)(2,1)S(1)}, u32[]{:S(2)}, u32[]{:S(2)}) %collective-permute-start.1) | collective-permute-done | bytes 131104 | tf_op jit(solution)/shard_map/ppermute | solution.py:1063
  22.9 2.0 %collective-permute-start.7 = (bf16[1,64,1024]{2,1,0:T(8,128)(2,1)S(1)}, bf16[1,64,1024]{2,1,0:T(8,128)(2,1)S(1)}, u32[]{:S(2)}, u32[]{:S(2)}) collective-permute-start(bf16[1,64,1024]{2,1,0:T(8,128)(2,1)S(1)} %copy-done.22), channel_id=1, source_target_pairs={{0,8},{1,9},{2,10},{3,11},{4,12},{5,13},{6,14},{7,15},{8,0},{9,1},... | collective-permute-start | bytes 393224 | tf_op jit(solution)/shard_map/ppermute | solution.py:1063
  28.4 2.7 %collective-permute-done.4.rest_2_ = bf16[4,64,1024]{2,1,0:T(8,128)(2,1)S(1)} collective-permute-done((bf16[4,64,1024]{2,1,0:T(8,128)(2,1)S(1)}, bf16[4,64,1024]{2,1,0:T(8,128)(2,1)S(1)}, u32[]{:S(2)}, u32[]{:S(2)}) %collective-permute-start.4) | collective-permute-done | bytes 524320 | tf_op jit(solution)/shard_map/ppermute | solution.py:1063
  37.9 2.9 %collective-permute-done.6.rest_4_ = bf16[2,64,1024]{2,1,0:T(8,128)(2,1)S(1)} collective-permute-done((bf16[2,64,1024]{2,1,0:T(8,128)(2,1)S(1)}, bf16[2,64,1024]{2,1,0:T(8,128)(2,1)S(1)}, u32[]{:S(2)}, u32[]{:S(2)}) %collective-permute-start.6) | collective-permute-done | bytes 262176 | tf_op jit(solution)/shard_map/ppermute | solution.py:1063
  40.8 2.2 %project.1.got_ref = bf16[16,104,128]{2,1,0:T(8,128)(2,1)S(1)} custom-call(s32[1]{0:T(128)} %bitcast.own_ref, s32[32]{0:T(128)S(1)} %copy-done.11, f32[3,1024]{1,0:T(4,128)S(1)} %maximum_convert_fusion.vectors_ref, bf16[1024,128]{1,0:T(8,128)(2,1)S(1)} %constant_dynamic-slice_fusion.7.wq, bf16[1024,128]{1,0:T(8,128)(2,1)S(1)} %get-tuple-element.91.wk, ...), custom_call_target="tpu_custom_call" | custom-call | bytes 13200000 | tf_op jit(solution)/shard_map/project/pallas_call | solution.py:1016
  44.9 3.7 %attend.1 = (bf16[512,128]{1,0:T(8,128)(2,1)}, f32[512,128]{1,0:T(8,128)S(1)}, f32[4,256]{1,0:T(4,128)S(1)}, f32[8,128]{1,0:T(8,128)S(1)}) custom-call(bf16[16,104,128]{2,1,0:T(8,128)(2,1)S(1)} %project.1.got_ref, bf16[16,104,128]{2,1,0:T(8,128)(2,1)S(1)} %collective-permute-done.10.other_ref, f32[2,1024]{1,0:T(2,128)S(1)} %get-tuple-element.98.kpos_ref, ...), custom_call_target="tpu_custom_call" | custom-call | bytes 16500000 | tf_op jit(solution)/shard_map/attend/pallas_call | solution.py:1016
  48.6 5.6 %all-to-all-start = ((bf16[16,32,128]{2,1,0:T(8,128)(2,1)}), bf16[16,32,128]{2,1,0:T(8,128)(2,1)S(1)}, u32[]{:S(2)}, u32[]{:S(2)}) async-start(bf16[16,32,128]{2,1,0:T(8,128)(2,1)} %bitcast.2), calls=%async_computation | async-start | bytes 262144 | tf_op jit(solution)/shard_map/all_to_all | solution.py:1060
  54.2 3.4 %collective-permute-done.11.rest_6_ = bf16[4,64,1024]{2,1,0:T(8,128)(2,1)S(1)} collective-permute-done((bf16[4,64,1024]{2,1,0:T(8,128)(2,1)S(1)}, bf16[4,64,1024]{2,1,0:T(8,128)(2,1)S(1)}, u32[]{:S(2)}, u32[]{:S(2)}) %collective-permute-start.11) | collective-permute-done | bytes 524320 | tf_op jit(solution)/shard_map/ppermute | solution.py:1063
  59.3 2.7 %all-to-all-done.got_ref = bf16[16,32,128]{2,1,0:T(8,128)(2,1)S(1)} async-done(((bf16[16,32,128]{2,1,0:T(8,128)(2,1)}), bf16[16,32,128]{2,1,0:T(8,128)(2,1)S(1)}, u32[]{:S(2)}, u32[]{:S(2)}) %all-to-all-start) | async-done | bytes 131104 | tf_op jit(solution)/shard_map/all_to_all | solution.py:1060
  64.6 3.0 %collective-permute-start.16 = (bf16[1,64,1024]{2,1,0:T(8,128)(2,1)S(1)}, bf16[1,64,1024]{2,1,0:T(8,128)(2,1)S(1)}, u32[]{:S(2)}, u32[]{:S(2)}) collective-permute-start(bf16[1,64,1024]{2,1,0:T(8,128)(2,1)S(1)} %unpack.1.mixed_ref), channel_id=1, source_target_pairs={{0,24},{1,25},{2,26},{3,27},{4,28},{5,29},{6,30},{7,31},{8,16},{9,... | collective-permute-start | bytes 393224 | tf_op jit(solution)/shard_map/ppermute | solution.py:1063
  67.7 10.3 %middle.1 = (bf16[16,72,128]{2,1,0:T(8,128)(2,1)}, bf16[64,4096]{1,0:T(8,128)(2,1)}, f32[64,1024]{1,0:T(8,128)}, f32[64,1024]{1,0:T(8,128)}, f32[64,128]{1,0:T(8,128)}) custom-call(s32[1]{0:T(128)} %bitcast.own_ref, s32[32]{0:T(128)} %counts_ref.13, bf16[1,64,1024]{2,1,0:T(8,128)(2,1)} %copy-done.4, f32[8,128]{1,0:T(8,128)} %copy-done.10, ...), custom_call_target="tpu_custom_call" | custom-call | bytes 36300000 | tf_op jit(solution)/shard_map/middle/pallas_call | solution.py:1016
  79.0 3.5 %all-to-all-start.1 = ((bf16[16,72,128]{2,1,0:T(8,128)(2,1)}), bf16[16,72,128]{2,1,0:T(8,128)(2,1)S(1)}, u32[]{:S(2)}, u32[]{:S(2)}) async-start(bf16[16,72,128]{2,1,0:T(8,128)(2,1)} %get-tuple-element.113), calls=%async_computation.1 | async-start | bytes 589824 | tf_op jit(solution)/shard_map/all_to_all | solution.py:1060
  85.9 6.8 %put.1 = bf16[512,1024]{1,0:T(8,128)(2,1)} custom-call(s32[1]{0:T(128)} %bitcast.own_ref, s32[32]{0:T(128)} %counts_ref.13, s32[16,128]{1,0:T(8,128)} %bitcast.8, f32[8,128]{1,0:T(8,128)} %copy-done.10, bf16[1,128,1024]{2,1,0:T(8,128)(2,1)} %get-tuple-element.77.both_ref.rows_ref, f32[3,1024]{1,0:T(4,128)} %copy-done.7, ...), custom_call_target="tpu_custom_call" | custom-call | bytes 19800000 | tf_op jit(solution)/shard_map/put/pallas_call | solution.py:1016
  92.7 3.8 %attend_back.1 = (bf16[512,128]{1,0:T(8,128)(2,1)S(1)}, f32[1024,128]{1,0:T(8,128)S(1)}, f32[1032,128]{1,0:T(8,128)S(1)}, f32[8,128]{1,0:T(8,128)S(1)}) custom-call(bf16[16,104,128]{2,1,0:T(8,128)(2,1)S(1)} %project.1.got_ref, bf16[16,104,128]{2,1,0:T(8,128)(2,1)S(1)} %collective-permute-done.10.other_ref, ...), custom_call_target="tpu_custom_call" | custom-call | bytes 19800000 | tf_op jit(solution)/shard_map/attend_back/pallas_call | solution.py:1016
  102.3 5.0 %all-to-all-start.2 = ((bf16[16,96,128]{2,1,0:T(8,128)(2,1)}), bf16[16,96,128]{2,1,0:T(8,128)(2,1)S(1)}, u32[]{:S(2)}, u32[]{:S(2)}) async-start(bf16[16,96,128]{2,1,0:T(8,128)(2,1)} %get-tuple-element.122.dqkv_ref), calls=%async_computation.2 | async-start | bytes 786432 | tf_op jit(solution)/shard_map/all_to_all | solution.py:1060
  108.2 14.1 %units.1 = (f32[128,1024]{1,0:T(8,128)}, bf16[128,1024]{1,0:T(8,128)(2,1)}, bf16[16,136,128]{2,1,0:T(8,128)(2,1)}, bf16[16,136,128]{2,1,0:T(8,128)(2,1)}) custom-call(s32[1]{0:T(128)} %bitcast.own_ref, s32[32]{0:T(128)} %counts_ref.13, bf16[16,72,128]{2,1,0:T(8,128)(2,1)} %copy-done.3, bf16[16,96,128]{2,1,0:T(8,128)(2,1)} %get-tuple-element.122.dqkv_ref, ...), custom_call_target="tpu_custom_call" | custom-call | bytes 52800000 | tf_op jit(solution)/shard_map/units/pallas_call | solution.py:1174
  122.4 2.2 %collective-permute-done.22.moved_ref = bf16[16,136,128]{2,1,0:T(8,128)(2,1)S(1)} collective-permute-done((bf16[16,136,128]{2,1,0:T(8,128)(2,1)}, bf16[16,136,128]{2,1,0:T(8,128)(2,1)S(1)}, u32[]{:S(2)}, u32[]{:S(2)}) %collective-permute-start.22) | collective-permute-done | bytes 557088 | tf_op jit(solution)/shard_map/ppermute | solution.py:1063
  126.6 6.9 %all-to-all-start.3 = ((bf16[16,136,128]{2,1,0:T(8,128)(2,1)}), bf16[16,136,128]{2,1,0:T(8,128)(2,1)S(1)}, u32[]{:S(2)}, u32[]{:S(2)}) async-start(bf16[16,136,128]{2,1,0:T(8,128)(2,1)} %merge.1), calls=%async_computation.3 | async-start | bytes 1114112 | tf_op jit(solution)/shard_map/all_to_all | solution.py:1060
  138.0 7.4 %rows.1 = bf16[512,1024]{1,0:T(8,128)(2,1)} custom-call(s32[1]{0:T(128)} %bitcast.own_ref, s32[32]{0:T(128)} %counts_ref.13, s32[16,128]{1,0:T(8,128)} %bitcast.9, bf16[16,96,128]{2,1,0:T(8,128)(2,1)} %copy-done.15, bf16[1,128,1024]{2,1,0:T(8,128)(2,1)} %get-tuple-element.77.both_ref.rows_ref, f32[64,1024]{1,0:T(8,128)} %get-tuple-element.123.dmiddle_ref, ...), custom_call_target="tpu_custom_call" | custom-call | bytes 23100000 | tf_op jit(solution)/shard_map/rows/pallas_call | solution.py:1016
  145.3 4.2 %all-to-all-done.3.got_ref = bf16[16,136,128]{2,1,0:T(8,128)(2,1)S(1)} async-done(((bf16[16,136,128]{2,1,0:T(8,128)(2,1)}), bf16[16,136,128]{2,1,0:T(8,128)(2,1)S(1)}, u32[]{:S(2)}, u32[]{:S(2)}) %all-to-all-start.3) | async-done | bytes 557088 | tf_op jit(solution)/shard_map/all_to_all | solution.py:1060
  (123 shorter events, 38.1 us)
Async XLA Ops:
  3.6 12.3 %collective-permute-start = (bf16[1,64,1024]{2,1,0:T(8,128)(2,1)}, bf16[1,64,1024]{2,1,0:T(8,128)(2,1)S(1)}, u32[]{:S(2)}, u32[]{:S(2)}) collective-permute-start(bf16[1,64,1024]{2,1,0:T(8,128)(2,1)} %get-tuple-element.78), channel_id=1, source_target_pairs={{0,8},{1,9},{2,10},{3,11},{4,12},{5,13},{6,14},{7,15},{8,0},{9,1},... | collective-permute-start | bytes 393224 | tf_op jit(solution)/shard_map/ppermute | solution.py:1063
  6.6 13.2 %collective-permute-start.1 = (bf16[1,64,1024]{2,1,0:T(8,128)(2,1)}, bf16[1,64,1024]{2,1,0:T(8,128)(2,1)S(1)}, u32[]{:S(2)}, u32[]{:S(2)}) collective-permute-start(bf16[1,64,1024]{2,1,0:T(8,128)(2,1)} %get-tuple-element.78), channel_id=1, source_target_pairs={{0,16},{1,17},{2,18},{3,19},{4,20},{5,21},{6,22},{7,23},{8,24},{9,... | collective-permute-start | bytes 393224 | tf_op jit(solution)/shard_map/ppermute | solution.py:1063
  9.2 10.6 %collective-permute-start.2 = (bf16[1,64,1024]{2,1,0:T(8,128)(2,1)}, bf16[1,64,1024]{2,1,0:T(8,128)(2,1)S(1)}, u32[]{:S(2)}, u32[]{:S(2)}) collective-permute-start(bf16[1,64,1024]{2,1,0:T(8,128)(2,1)} %get-tuple-element.78), channel_id=1, source_target_pairs={{0,24},{1,25},{2,26},{3,27},{4,28},{5,29},{6,30},{7,31},{8,16},{9,... | collective-permute-start | bytes 393224 | tf_op jit(solution)/shard_map/ppermute | solution.py:1063
  19.8 11.3 %collective-permute-start.4 = (bf16[4,64,1024]{2,1,0:T(8,128)(2,1)S(1)}, bf16[4,64,1024]{2,1,0:T(8,128)(2,1)S(1)}, u32[]{:S(2)}, u32[]{:S(2)}) collective-permute-start(bf16[4,64,1024]{2,1,0:T(8,128)(2,1)S(1)} %pad_maximum_fusion.rest_0_), channel_id=1, source_target_pairs={{0,4},{1,5},{2,6},{3,7},{4,0},{5,1},{6,2},{7,3},{8,12},{9,13},{10,... | collective-permute-start | bytes 1572872 | tf_op jit(solution)/shard_map/ppermute | solution.py:1063
  21.4 13.0 %collective-permute-start.3 = (bf16[4,64,1024]{2,1,0:T(8,128)(2,1)S(1)}, bf16[4,64,1024]{2,1,0:T(8,128)(2,1)S(1)}, u32[]{:S(2)}, u32[]{:S(2)}) collective-permute-start(bf16[4,64,1024]{2,1,0:T(8,128)(2,1)S(1)} %pad_maximum_fusion.rest_0_), channel_id=1, source_target_pairs={{0,2},{1,3},{2,0},{3,1},{4,6},{5,7},{6,4},{7,5},{8,10},{9,11},{10,... | collective-permute-start | bytes 1572872 | tf_op jit(solution)/shard_map/ppermute | solution.py:1063
  22.9 13.8 %collective-permute-start.7 = (bf16[1,64,1024]{2,1,0:T(8,128)(2,1)S(1)}, bf16[1,64,1024]{2,1,0:T(8,128)(2,1)S(1)}, u32[]{:S(2)}, u32[]{:S(2)}) collective-permute-start(bf16[1,64,1024]{2,1,0:T(8,128)(2,1)S(1)} %copy-done.22), channel_id=1, source_target_pairs={{0,8},{1,9},{2,10},{3,11},{4,12},{5,13},{6,14},{7,15},{8,0},{9,1},... | collective-permute-start | bytes 393224 | tf_op jit(solution)/shard_map/ppermute | solution.py:1063
  24.9 11.9 %collective-permute-start.8 = (bf16[1,64,1024]{2,1,0:T(8,128)(2,1)S(1)}, bf16[1,64,1024]{2,1,0:T(8,128)(2,1)S(1)}, u32[]{:S(2)}, u32[]{:S(2)}) collective-permute-start(bf16[1,64,1024]{2,1,0:T(8,128)(2,1)S(1)} %copy-done.22), channel_id=1, source_target_pairs={{0,16},{1,17},{2,18},{3,19},{4,20},{5,21},{6,22},{7,23},{8,24},{9,... | collective-permute-start | bytes 393224 | tf_op jit(solution)/shard_map/ppermute | solution.py:1063
  25.9 10.9 %collective-permute-start.9 = (bf16[1,64,1024]{2,1,0:T(8,128)(2,1)S(1)}, bf16[1,64,1024]{2,1,0:T(8,128)(2,1)S(1)}, u32[]{:S(2)}, u32[]{:S(2)}) collective-permute-start(bf16[1,64,1024]{2,1,0:T(8,128)(2,1)S(1)} %copy-done.22), channel_id=1, source_target_pairs={{0,24},{1,25},{2,26},{3,27},{4,28},{5,29},{6,30},{7,31},{8,16},{9,... | collective-permute-start | bytes 393224 | tf_op jit(solution)/shard_map/ppermute | solution.py:1063
  31.1 6.8 %collective-permute-start.5 = (bf16[2,64,1024]{2,1,0:T(8,128)(2,1)S(1)}, bf16[2,64,1024]{2,1,0:T(8,128)(2,1)S(1)}, u32[]{:S(2)}, u32[]{:S(2)}) collective-permute-start(bf16[2,64,1024]{2,1,0:T(8,128)(2,1)S(1)} %slice.16), channel_id=1, source_target_pairs={{0,2},{1,3},{2,0},{3,1},{4,6},{5,7},{6,4},{7,5},{8,10},{9,11},{10,... | collective-permute-start | bytes 786440 | tf_op jit(solution)/shard_map/ppermute | solution.py:1063
  34.4 6.4 %collective-permute-start.6 = (bf16[2,64,1024]{2,1,0:T(8,128)(2,1)S(1)}, bf16[2,64,1024]{2,1,0:T(8,128)(2,1)S(1)}, u32[]{:S(2)}, u32[]{:S(2)}) collective-permute-start(bf16[2,64,1024]{2,1,0:T(8,128)(2,1)S(1)} %slice.17), channel_id=1, source_target_pairs={{0,4},{1,5},{2,6},{3,7},{4,0},{5,1},{6,2},{7,3},{8,12},{9,13},{10,... | collective-permute-start | bytes 786440 | tf_op jit(solution)/shard_map/ppermute | solution.py:1063
  43.1 14.5 %collective-permute-start.11 = (bf16[4,64,1024]{2,1,0:T(8,128)(2,1)S(1)}, bf16[4,64,1024]{2,1,0:T(8,128)(2,1)S(1)}, u32[]{:S(2)}, u32[]{:S(2)}) collective-permute-start(bf16[4,64,1024]{2,1,0:T(8,128)(2,1)S(1)} %pad_maximum_fusion.1.rest_5_), channel_id=1, source_target_pairs={{0,2},{1,3},{2,0},{3,1},{4,6},{5,7},{6,4},{7,5},{8,10},{9,11},{10,... | collective-permute-start | bytes 1572872 | tf_op jit(solution)/shard_map/ppermute | solution.py:1063
  44.7 14.6 %collective-permute-start.12 = (bf16[4,64,1024]{2,1,0:T(8,128)(2,1)S(1)}, bf16[4,64,1024]{2,1,0:T(8,128)(2,1)S(1)}, u32[]{:S(2)}, u32[]{:S(2)}) collective-permute-start(bf16[4,64,1024]{2,1,0:T(8,128)(2,1)S(1)} %pad_maximum_fusion.1.rest_5_), channel_id=1, source_target_pairs={{0,4},{1,5},{2,6},{3,7},{4,0},{5,1},{6,2},{7,3},{8,12},{9,13},{10,... | collective-permute-start | bytes 1572872 | tf_op jit(solution)/shard_map/ppermute | solution.py:1063
  48.6 13.4 %all-to-all-start = ((bf16[16,32,128]{2,1,0:T(8,128)(2,1)}), bf16[16,32,128]{2,1,0:T(8,128)(2,1)S(1)}, u32[]{:S(2)}, u32[]{:S(2)}) async-start(bf16[16,32,128]{2,1,0:T(8,128)(2,1)} %bitcast.2), calls=%async_computation | async-start | bytes 262144 | tf_op jit(solution)/shard_map/all_to_all | solution.py:1060
  62.0 17.0 %collective-permute-start.13 = (bf16[4,64,1024]{2,1,0:T(8,128)(2,1)S(1)}, bf16[4,64,1024]{2,1,0:T(8,128)(2,1)}, u32[]{:S(2)}, u32[]{:S(2)}) collective-permute-start(bf16[4,64,1024]{2,1,0:T(8,128)(2,1)S(1)} %collective-permute-done.12.rest_7_), channel_id=1, source_target_pairs={{0,2},{1,3},{2,0},{3,1},{4,6},{5,7},{6,4},{7,5},{8,10},{9,11},{10,... | collective-permute-start | bytes 1572872 | tf_op jit(solution)/shard_map/ppermute | solution.py:1063
  63.2 14.7 %collective-permute-start.14 = (bf16[1,64,1024]{2,1,0:T(8,128)(2,1)S(1)}, bf16[1,64,1024]{2,1,0:T(8,128)(2,1)S(1)}, u32[]{:S(2)}, u32[]{:S(2)}) collective-permute-start(bf16[1,64,1024]{2,1,0:T(8,128)(2,1)S(1)} %unpack.1.mixed_ref), channel_id=1, source_target_pairs={{0,8},{1,9},{2,10},{3,11},{4,12},{5,13},{6,14},{7,15},{8,0},{9,1},... | collective-permute-start | bytes 393224 | tf_op jit(solution)/shard_map/ppermute | solution.py:1063
  63.5 14.5 %collective-permute-start.15 = (bf16[1,64,1024]{2,1,0:T(8,128)(2,1)S(1)}, bf16[1,64,1024]{2,1,0:T(8,128)(2,1)S(1)}, u32[]{:S(2)}, u32[]{:S(2)}) collective-permute-start(bf16[1,64,1024]{2,1,0:T(8,128)(2,1)S(1)} %unpack.1.mixed_ref), channel_id=1, source_target_pairs={{0,16},{1,17},{2,18},{3,19},{4,20},{5,21},{6,22},{7,23},{8,24},{9,... | collective-permute-start | bytes 393224 | tf_op jit(solution)/shard_map/ppermute | solution.py:1063
  64.6 13.3 %collective-permute-start.16 = (bf16[1,64,1024]{2,1,0:T(8,128)(2,1)S(1)}, bf16[1,64,1024]{2,1,0:T(8,128)(2,1)S(1)}, u32[]{:S(2)}, u32[]{:S(2)}) collective-permute-start(bf16[1,64,1024]{2,1,0:T(8,128)(2,1)S(1)} %unpack.1.mixed_ref), channel_id=1, source_target_pairs={{0,24},{1,25},{2,26},{3,27},{4,28},{5,29},{6,30},{7,31},{8,16},{9,... | collective-permute-start | bytes 393224 | tf_op jit(solution)/shard_map/ppermute | solution.py:1063
  79.0 13.7 %all-to-all-start.1 = ((bf16[16,72,128]{2,1,0:T(8,128)(2,1)}), bf16[16,72,128]{2,1,0:T(8,128)(2,1)S(1)}, u32[]{:S(2)}, u32[]{:S(2)}) async-start(bf16[16,72,128]{2,1,0:T(8,128)(2,1)} %get-tuple-element.113), calls=%async_computation.1 | async-start | bytes 589824 | tf_op jit(solution)/shard_map/all_to_all | solution.py:1060
  82.6 14.6 %collective-permute-start.19 = (bf16[4,64,1024]{2,1,0:T(8,128)(2,1)S(1)}, bf16[4,64,1024]{2,1,0:T(8,128)(2,1)S(1)}, u32[]{:S(2)}, u32[]{:S(2)}) collective-permute-start(bf16[4,64,1024]{2,1,0:T(8,128)(2,1)S(1)} %pad_maximum_fusion.2.rest_9_), channel_id=1, source_target_pairs={{0,4},{1,5},{2,6},{3,7},{4,0},{5,1},{6,2},{7,3},{8,12},{9,13},{10,... | collective-permute-start | bytes 1572872 | tf_op jit(solution)/shard_map/ppermute | solution.py:1063
  84.4 14.4 %collective-permute-start.18 = (bf16[4,64,1024]{2,1,0:T(8,128)(2,1)S(1)}, bf16[4,64,1024]{2,1,0:T(8,128)(2,1)}, u32[]{:S(2)}, u32[]{:S(2)}) collective-permute-start(bf16[4,64,1024]{2,1,0:T(8,128)(2,1)S(1)} %pad_maximum_fusion.2.rest_9_), channel_id=1, source_target_pairs={{0,2},{1,3},{2,0},{3,1},{4,6},{5,7},{6,4},{7,5},{8,10},{9,11},{10,... | collective-permute-start | bytes 1572872 | tf_op jit(solution)/shard_map/ppermute | solution.py:1063
  97.2 10.2 %collective-permute-start.20 = (bf16[2,64,1024]{2,1,0:T(8,128)(2,1)S(1)}, bf16[2,64,1024]{2,1,0:T(8,128)(2,1)S(1)}, u32[]{:S(2)}, u32[]{:S(2)}) collective-permute-start(bf16[2,64,1024]{2,1,0:T(8,128)(2,1)S(1)} %slice.18), channel_id=1, source_target_pairs={{0,2},{1,3},{2,0},{3,1},{4,6},{5,7},{6,4},{7,5},{8,10},{9,11},{10,... | collective-permute-start | bytes 786440 | tf_op jit(solution)/shard_map/ppermute | solution.py:1063
  99.7 7.7 %collective-permute-start.21 = (bf16[2,64,1024]{2,1,0:T(8,128)(2,1)S(1)}, bf16[2,64,1024]{2,1,0:T(8,128)(2,1)S(1)}, u32[]{:S(2)}, u32[]{:S(2)}) collective-permute-start(bf16[2,64,1024]{2,1,0:T(8,128)(2,1)S(1)} %slice.19), channel_id=1, source_target_pairs={{0,4},{1,5},{2,6},{3,7},{4,0},{5,1},{6,2},{7,3},{8,12},{9,13},{10,... | collective-permute-start | bytes 786440 | tf_op jit(solution)/shard_map/ppermute | solution.py:1063
  102.3 24.3 %all-to-all-start.2 = ((bf16[16,96,128]{2,1,0:T(8,128)(2,1)}), bf16[16,96,128]{2,1,0:T(8,128)(2,1)S(1)}, u32[]{:S(2)}, u32[]{:S(2)}) async-start(bf16[16,96,128]{2,1,0:T(8,128)(2,1)} %get-tuple-element.122.dqkv_ref), calls=%async_computation.2 | async-start | bytes 786432 | tf_op jit(solution)/shard_map/all_to_all | solution.py:1060
  126.6 22.9 %all-to-all-start.3 = ((bf16[16,136,128]{2,1,0:T(8,128)(2,1)}), bf16[16,136,128]{2,1,0:T(8,128)(2,1)S(1)}, u32[]{:S(2)}, u32[]{:S(2)}) async-start(bf16[16,136,128]{2,1,0:T(8,128)(2,1)} %merge.1), calls=%async_computation.3 | async-start | bytes 1114112 | tf_op jit(solution)/shard_map/all_to_all | solution.py:1060
  (33 other events, 365.8 us)

commit v6 on v5

--- a/solution.py
+++ b/solution.py
@@ -63,6 +63,7 @@
 
 def attend_core(factor, load_query, load_kv, members, blocks, key_rows, kpos_ref, qpos_ref, qlow_ref, mixed_ref, turned_ref, lse_ref):
     kv_turned = [jnp.transpose(load_kv(m, key_rows)) for m in range(members)]
+    columns = [key_columns(kpos_ref, m, key_rows) for m in range(members)]
     for b in range(blocks):
         extent = key_rows * (b + 1) // blocks
         packed = (load_query(b).astype(f32) * factor).astype(bf16)
@@ -72,7 +73,7 @@
         scores = []
         for m in range(members):
             score = nt(load_kv(m, extent), wide)
-            kpos = key_columns(kpos_ref, m, extent)
+            kpos = columns[m][:extent]
             score = jnp.where((kpos <= qpos) & (kpos >= qlow), score, masked_score)
             scores.append(score)
         peak = jnp.max(scores[0], axis=0, keepdims=True)
@@ -97,6 +98,7 @@
     dq_ref, add_dkv,
 ):
     kv_turned = [jnp.transpose(load_kv(m, key_rows)) for m in range(members)]
+    columns = [key_columns(kpos_ref, m, key_rows) for m in range(members)]
     for b in range(blocks - 1, -1, -1):
         extent = key_rows * (b + 1) // blocks
         rows = slice(b * BLOCK, (b + 1) * BLOCK)
@@ -117,7 +119,7 @@
         dquery = jnp.zeros((LANES, 2 * BLOCK), f32)
         for m in range(members):
             both = nt(load_kv(m, extent), wide)
-            kpos = key_columns(kpos_ref, m, extent)
+            kpos = columns[m][:extent]
             prob = jnp.exp(
                 jnp.where((kpos <= qpos) & (kpos >= qlow), both[:, : 2 * BLOCK] - lse, masked_score)
             )

time: 152 us -> 152 us (level)
  no operation moved by 1% of the time
where the time goes in v6:
time: 152 us; the launch traced here: 151 us
  Pallas kernels  61.9 us (41%)
  starting transfers between devices  49.5 us (33%)
  waiting for transfers between devices  27.1 us (18%)
  local copies, waits for them, and re-layouts  9.11 us (6%)
  other arithmetic  2.06 us (1%)
    pallas_call x13, Pallas kernels, call(): pl.pallas_call(kernel, out_shape=out_shape, in_specs=in_specs, out_specs=...  47.8 us
    ppermute x24, starting transfers between devices, across(): return lax.ppermute(value, 'seq', [(s, s ^ bits) for s in range(devices)])  28.4 us
    all_to_all x4, starting transfers between devices, swap(): lax.all_to_all(value, 'seq', split_axis=0, concat_axis=0, tiled=True, axi...  21.1 us
    ppermute x24, waiting for transfers between devices, across(): return lax.ppermute(value, 'seq', [(s, s ^ bits) for s in range(devices)])  19.9 us
    pallas_call x1, Pallas kernels, pairs(): pl.pallas_call(units_kernel, out_shape=(shaped((hidden_cols // 2, width),...  14.1 us
    all_to_all x4, waiting for transfers between devices, swap(): lax.all_to_all(value, 'seq', split_axis=0, concat_axis=0, tiled=True, axi...  7.14 us
  transfers between devices with their start and end apart: 28, of which 12 were waited for; matrix products, arithmetic and copies ran while one was open for 6% of the time, Pallas kernels for 37%

profile of v6, /device:TPU:0, one launch (start us, length us, event | category | flops | bytes accessed | tf_op | source)
XLA Modules:
  0.0 150.9 jit_solution(6712009225705423699)
XLA Ops:
  0.6 2.9 %fetch.1 = (bf16[1,128,1024]{2,1,0:T(8,128)(2,1)}, bf16[1,64,1024]{2,1,0:T(8,128)(2,1)}, bf16[1,64,1024]{2,1,0:T(8,128)(2,1)}) custom-call(s32[1]{0:T(128)} %bitcast.own_ref, s32[32]{0:T(128)} %counts_ref.13, s32[16,128]{1,0:T(8,128)} %bitcast.7, bf16[512,1024]{1,0:T(8,128)(2,1)} %old_ref.2, bf16[512,1024]{1,0:T(8,128)(2,1)} %old_ref.3), custom_call_target="tpu_custom_call" | custom-call | bytes 9900000 | tf_op jit(solution)/shard_map/fetch/pallas_call | solution.py:1018
  3.6 3.0 %collective-permute-start = (bf16[1,64,1024]{2,1,0:T(8,128)(2,1)}, bf16[1,64,1024]{2,1,0:T(8,128)(2,1)S(1)}, u32[]{:S(2)}, u32[]{:S(2)}) collective-permute-start(bf16[1,64,1024]{2,1,0:T(8,128)(2,1)} %get-tuple-element.78), channel_id=1, source_target_pairs={{0,8},{1,9},{2,10},{3,11},{4,12},{5,13},{6,14},{7,15},{8,0},{9,1},... | collective-permute-start | bytes 393224 | tf_op jit(solution)/shard_map/ppermute | solution.py:1065
  6.6 2.6 %collective-permute-start.1 = (bf16[1,64,1024]{2,1,0:T(8,128)(2,1)}, bf16[1,64,1024]{2,1,0:T(8,128)(2,1)S(1)}, u32[]{:S(2)}, u32[]{:S(2)}) collective-permute-start(bf16[1,64,1024]{2,1,0:T(8,128)(2,1)} %get-tuple-element.78), channel_id=1, source_target_pairs={{0,16},{1,17},{2,18},{3,19},{4,20},{5,21},{6,22},{7,23},{8,24},{9,... | collective-permute-start | bytes 393224 | tf_op jit(solution)/shard_map/ppermute | solution.py:1065
  9.2 6.6 %early.1.product_ref = f32[64,4096]{1,0:T(8,128)} custom-call(bf16[1,128,1024]{2,1,0:T(8,128)(2,1)} %get-tuple-element.77.both_ref.rows_ref, bf16[4096,1024]{1,0:T(8,128)(2,1)} %down_ref.5), custom_call_target="tpu_custom_call" | custom-call | bytes 16500000 | tf_op jit(solution)/shard_map/early/pallas_call | solution.py:1018
  15.9 3.9 %collective-permute-done.1 = bf16[1,64,1024]{2,1,0:T(8,128)(2,1)S(1)} collective-permute-done((bf16[1,64,1024]{2,1,0:T(8,128)(2,1)}, bf16[1,64,1024]{2,1,0:T(8,128)(2,1)S(1)}, u32[]{:S(2)}, u32[]{:S(2)}) %collective-permute-start.1) | collective-permute-done | bytes 131104 | tf_op jit(solution)/shard_map/ppermute | solution.py:1065
  22.9 2.0 %collective-permute-start.7 = (bf16[1,64,1024]{2,1,0:T(8,128)(2,1)S(1)}, bf16[1,64,1024]{2,1,0:T(8,128)(2,1)S(1)}, u32[]{:S(2)}, u32[]{:S(2)}) collective-permute-start(bf16[1,64,1024]{2,1,0:T(8,128)(2,1)S(1)} %copy-done.22), channel_id=1, source_target_pairs={{0,8},{1,9},{2,10},{3,11},{4,12},{5,13},{6,14},{7,15},{8,0},{9,1},... | collective-permute-start | bytes 393224 | tf_op jit(solution)/shard_map/ppermute | solution.py:1065
  28.4 2.7 %collective-permute-done.4.rest_2_ = bf16[4,64,1024]{2,1,0:T(8,128)(2,1)S(1)} collective-permute-done((bf16[4,64,1024]{2,1,0:T(8,128)(2,1)S(1)}, bf16[4,64,1024]{2,1,0:T(8,128)(2,1)S(1)}, u32[]{:S(2)}, u32[]{:S(2)}) %collective-permute-start.4) | collective-permute-done | bytes 524320 | tf_op jit(solution)/shard_map/ppermute | solution.py:1065
  37.9 2.9 %collective-permute-done.6.rest_4_ = bf16[2,64,1024]{2,1,0:T(8,128)(2,1)S(1)} collective-permute-done((bf16[2,64,1024]{2,1,0:T(8,128)(2,1)S(1)}, bf16[2,64,1024]{2,1,0:T(8,128)(2,1)S(1)}, u32[]{:S(2)}, u32[]{:S(2)}) %collective-permute-start.6) | collective-permute-done | bytes 262176 | tf_op jit(solution)/shard_map/ppermute | solution.py:1065
  40.8 2.2 %project.1.got_ref = bf16[16,104,128]{2,1,0:T(8,128)(2,1)S(1)} custom-call(s32[1]{0:T(128)} %bitcast.own_ref, s32[32]{0:T(128)S(1)} %copy-done.11, f32[3,1024]{1,0:T(4,128)S(1)} %maximum_convert_fusion.vectors_ref, bf16[1024,128]{1,0:T(8,128)(2,1)S(1)} %constant_dynamic-slice_fusion.7.wq, bf16[1024,128]{1,0:T(8,128)(2,1)S(1)} %get-tuple-element.91.wk, ...), custom_call_target="tpu_custom_call" | custom-call | bytes 13200000 | tf_op jit(solution)/shard_map/project/pallas_call | solution.py:1018
  44.9 3.9 %attend.1 = (bf16[512,128]{1,0:T(8,128)(2,1)}, f32[512,128]{1,0:T(8,128)S(1)}, f32[4,256]{1,0:T(4,128)S(1)}, f32[8,128]{1,0:T(8,128)S(1)}) custom-call(bf16[16,104,128]{2,1,0:T(8,128)(2,1)S(1)} %project.1.got_ref, bf16[16,104,128]{2,1,0:T(8,128)(2,1)S(1)} %collective-permute-done.10.other_ref, f32[2,1024]{1,0:T(2,128)S(1)} %get-tuple-element.98.kpos_ref, ...), custom_call_target="tpu_custom_call" | custom-call | bytes 16500000 | tf_op jit(solution)/shard_map/attend/pallas_call | solution.py:1018
  48.9 5.6 %all-to-all-start = ((bf16[16,32,128]{2,1,0:T(8,128)(2,1)}), bf16[16,32,128]{2,1,0:T(8,128)(2,1)S(1)}, u32[]{:S(2)}, u32[]{:S(2)}) async-start(bf16[16,32,128]{2,1,0:T(8,128)(2,1)} %bitcast.2), calls=%async_computation | async-start | bytes 262144 | tf_op jit(solution)/shard_map/all_to_all | solution.py:1062
  54.5 3.2 %collective-permute-done.11.rest_6_ = bf16[4,64,1024]{2,1,0:T(8,128)(2,1)S(1)} collective-permute-done((bf16[4,64,1024]{2,1,0:T(8,128)(2,1)S(1)}, bf16[4,64,1024]{2,1,0:T(8,128)(2,1)S(1)}, u32[]{:S(2)}, u32[]{:S(2)}) %collective-permute-start.11) | collective-permute-done | bytes 524320 | tf_op jit(solution)/shard_map/ppermute | solution.py:1065
  59.3 3.0 %all-to-all-done.got_ref = bf16[16,32,128]{2,1,0:T(8,128)(2,1)S(1)} async-done(((bf16[16,32,128]{2,1,0:T(8,128)(2,1)}), bf16[16,32,128]{2,1,0:T(8,128)(2,1)S(1)}, u32[]{:S(2)}, u32[]{:S(2)}) %all-to-all-start) | async-done | bytes 131104 | tf_op jit(solution)/shard_map/all_to_all | solution.py:1062
  64.9 3.0 %collective-permute-start.16 = (bf16[1,64,1024]{2,1,0:T(8,128)(2,1)S(1)}, bf16[1,64,1024]{2,1,0:T(8,128)(2,1)S(1)}, u32[]{:S(2)}, u32[]{:S(2)}) collective-permute-start(bf16[1,64,1024]{2,1,0:T(8,128)(2,1)S(1)} %unpack.1.mixed_ref), channel_id=1, source_target_pairs={{0,24},{1,25},{2,26},{3,27},{4,28},{5,29},{6,30},{7,31},{8,16},{9,... | collective-permute-start | bytes 393224 | tf_op jit(solution)/shard_map/ppermute | solution.py:1065
  67.9 10.3 %middle.1 = (bf16[16,72,128]{2,1,0:T(8,128)(2,1)}, bf16[64,4096]{1,0:T(8,128)(2,1)}, f32[64,1024]{1,0:T(8,128)}, f32[64,1024]{1,0:T(8,128)}, f32[64,128]{1,0:T(8,128)}) custom-call(s32[1]{0:T(128)} %bitcast.own_ref, s32[32]{0:T(128)} %counts_ref.13, bf16[1,64,1024]{2,1,0:T(8,128)(2,1)} %copy-done.4, f32[8,128]{1,0:T(8,128)} %copy-done.10, ...), custom_call_target="tpu_custom_call" | custom-call | bytes 36300000 | tf_op jit(solution)/shard_map/middle/pallas_call | solution.py:1018
  79.3 3.5 %all-to-all-start.1 = ((bf16[16,72,128]{2,1,0:T(8,128)(2,1)}), bf16[16,72,128]{2,1,0:T(8,128)(2,1)S(1)}, u32[]{:S(2)}, u32[]{:S(2)}) async-start(bf16[16,72,128]{2,1,0:T(8,128)(2,1)} %get-tuple-element.113), calls=%async_computation.1 | async-start | bytes 589824 | tf_op jit(solution)/shard_map/all_to_all | solution.py:1062
  86.1 6.8 %put.1 = bf16[512,1024]{1,0:T(8,128)(2,1)} custom-call(s32[1]{0:T(128)} %bitcast.own_ref, s32[32]{0:T(128)} %counts_ref.13, s32[16,128]{1,0:T(8,128)} %bitcast.8, f32[8,128]{1,0:T(8,128)} %copy-done.10, bf16[1,128,1024]{2,1,0:T(8,128)(2,1)} %get-tuple-element.77.both_ref.rows_ref, f32[3,1024]{1,0:T(4,128)} %copy-done.7, ...), custom_call_target="tpu_custom_call" | custom-call | bytes 19800000 | tf_op jit(solution)/shard_map/put/pallas_call | solution.py:1018
  93.0 3.8 %attend_back.1 = (bf16[512,128]{1,0:T(8,128)(2,1)S(1)}, f32[1024,128]{1,0:T(8,128)S(1)}, f32[1032,128]{1,0:T(8,128)S(1)}, f32[8,128]{1,0:T(8,128)S(1)}) custom-call(bf16[16,104,128]{2,1,0:T(8,128)(2,1)S(1)} %project.1.got_ref, bf16[16,104,128]{2,1,0:T(8,128)(2,1)S(1)} %collective-permute-done.10.other_ref, ...), custom_call_target="tpu_custom_call" | custom-call | bytes 19800000 | tf_op jit(solution)/shard_map/attend_back/pallas_call | solution.py:1018
  102.6 5.0 %all-to-all-start.2 = ((bf16[16,96,128]{2,1,0:T(8,128)(2,1)}), bf16[16,96,128]{2,1,0:T(8,128)(2,1)S(1)}, u32[]{:S(2)}, u32[]{:S(2)}) async-start(bf16[16,96,128]{2,1,0:T(8,128)(2,1)} %get-tuple-element.122.dqkv_ref), calls=%async_computation.2 | async-start | bytes 786432 | tf_op jit(solution)/shard_map/all_to_all | solution.py:1062
  108.5 14.1 %units.1 = (f32[128,1024]{1,0:T(8,128)}, bf16[128,1024]{1,0:T(8,128)(2,1)}, bf16[16,136,128]{2,1,0:T(8,128)(2,1)}, bf16[16,136,128]{2,1,0:T(8,128)(2,1)}) custom-call(s32[1]{0:T(128)} %bitcast.own_ref, s32[32]{0:T(128)} %counts_ref.13, bf16[16,72,128]{2,1,0:T(8,128)(2,1)} %copy-done.3, bf16[16,96,128]{2,1,0:T(8,128)(2,1)} %get-tuple-element.122.dqkv_ref, ...), custom_call_target="tpu_custom_call" | custom-call | bytes 52800000 | tf_op jit(solution)/shard_map/units/pallas_call | solution.py:1176
  122.7 2.2 %collective-permute-done.22.moved_ref = bf16[16,136,128]{2,1,0:T(8,128)(2,1)S(1)} collective-permute-done((bf16[16,136,128]{2,1,0:T(8,128)(2,1)}, bf16[16,136,128]{2,1,0:T(8,128)(2,1)S(1)}, u32[]{:S(2)}, u32[]{:S(2)}) %collective-permute-start.22) | collective-permute-done | bytes 557088 | tf_op jit(solution)/shard_map/ppermute | solution.py:1065
  126.9 6.9 %all-to-all-start.3 = ((bf16[16,136,128]{2,1,0:T(8,128)(2,1)}), bf16[16,136,128]{2,1,0:T(8,128)(2,1)S(1)}, u32[]{:S(2)}, u32[]{:S(2)}) async-start(bf16[16,136,128]{2,1,0:T(8,128)(2,1)} %merge.1), calls=%async_computation.3 | async-start | bytes 1114112 | tf_op jit(solution)/shard_map/all_to_all | solution.py:1062
  138.2 7.4 %rows.1 = bf16[512,1024]{1,0:T(8,128)(2,1)} custom-call(s32[1]{0:T(128)} %bitcast.own_ref, s32[32]{0:T(128)} %counts_ref.13, s32[16,128]{1,0:T(8,128)} %bitcast.9, bf16[16,96,128]{2,1,0:T(8,128)(2,1)} %copy-done.15, bf16[1,128,1024]{2,1,0:T(8,128)(2,1)} %get-tuple-element.77.both_ref.rows_ref, f32[64,1024]{1,0:T(8,128)} %get-tuple-element.123.dmiddle_ref, ...), custom_call_target="tpu_custom_call" | custom-call | bytes 23100000 | tf_op jit(solution)/shard_map/rows/pallas_call | solution.py:1018
  145.6 4.2 %all-to-all-done.3.got_ref = bf16[16,136,128]{2,1,0:T(8,128)(2,1)S(1)} async-done(((bf16[16,136,128]{2,1,0:T(8,128)(2,1)}), bf16[16,136,128]{2,1,0:T(8,128)(2,1)S(1)}, u32[]{:S(2)}, u32[]{:S(2)}) %all-to-all-start.3) | async-done | bytes 557088 | tf_op jit(solution)/shard_map/all_to_all | solution.py:1062
  (123 shorter events, 38.0 us)
Async XLA Ops:
  3.6 12.3 %collective-permute-start = (bf16[1,64,1024]{2,1,0:T(8,128)(2,1)}, bf16[1,64,1024]{2,1,0:T(8,128)(2,1)S(1)}, u32[]{:S(2)}, u32[]{:S(2)}) collective-permute-start(bf16[1,64,1024]{2,1,0:T(8,128)(2,1)} %get-tuple-element.78), channel_id=1, source_target_pairs={{0,8},{1,9},{2,10},{3,11},{4,12},{5,13},{6,14},{7,15},{8,0},{9,1},... | collective-permute-start | bytes 393224 | tf_op jit(solution)/shard_map/ppermute | solution.py:1065
  6.6 13.2 %collective-permute-start.1 = (bf16[1,64,1024]{2,1,0:T(8,128)(2,1)}, bf16[1,64,1024]{2,1,0:T(8,128)(2,1)S(1)}, u32[]{:S(2)}, u32[]{:S(2)}) collective-permute-start(bf16[1,64,1024]{2,1,0:T(8,128)(2,1)} %get-tuple-element.78), channel_id=1, source_target_pairs={{0,16},{1,17},{2,18},{3,19},{4,20},{5,21},{6,22},{7,23},{8,24},{9,... | collective-permute-start | bytes 393224 | tf_op jit(solution)/shard_map/ppermute | solution.py:1065
  9.2 10.6 %collective-permute-start.2 = (bf16[1,64,1024]{2,1,0:T(8,128)(2,1)}, bf16[1,64,1024]{2,1,0:T(8,128)(2,1)S(1)}, u32[]{:S(2)}, u32[]{:S(2)}) collective-permute-start(bf16[1,64,1024]{2,1,0:T(8,128)(2,1)} %get-tuple-element.78), channel_id=1, source_target_pairs={{0,24},{1,25},{2,26},{3,27},{4,28},{5,29},{6,30},{7,31},{8,16},{9,... | collective-permute-start | bytes 393224 | tf_op jit(solution)/shard_map/ppermute | solution.py:1065
  19.8 11.3 %collective-permute-start.4 = (bf16[4,64,1024]{2,1,0:T(8,128)(2,1)S(1)}, bf16[4,64,1024]{2,1,0:T(8,128)(2,1)S(1)}, u32[]{:S(2)}, u32[]{:S(2)}) collective-permute-start(bf16[4,64,1024]{2,1,0:T(8,128)(2,1)S(1)} %pad_maximum_fusion.rest_0_), channel_id=1, source_target_pairs={{0,4},{1,5},{2,6},{3,7},{4,0},{5,1},{6,2},{7,3},{8,12},{9,13},{10,... | collective-permute-start | bytes 1572872 | tf_op jit(solution)/shard_map/ppermute | solution.py:1065
  21.4 13.0 %collective-permute-start.3 = (bf16[4,64,1024]{2,1,0:T(8,128)(2,1)S(1)}, bf16[4,64,1024]{2,1,0:T(8,128)(2,1)S(1)}, u32[]{:S(2)}, u32[]{:S(2)}) collective-permute-start(bf16[4,64,1024]{2,1,0:T(8,128)(2,1)S(1)} %pad_maximum_fusion.rest_0_), channel_id=1, source_target_pairs={{0,2},{1,3},{2,0},{3,1},{4,6},{5,7},{6,4},{7,5},{8,10},{9,11},{10,... | collective-permute-start | bytes 1572872 | tf_op jit(solution)/shard_map/ppermute | solution.py:1065
  22.9 13.8 %collective-permute-start.7 = (bf16[1,64,1024]{2,1,0:T(8,128)(2,1)S(1)}, bf16[1,64,1024]{2,1,0:T(8,128)(2,1)S(1)}, u32[]{:S(2)}, u32[]{:S(2)}) collective-permute-start(bf16[1,64,1024]{2,1,0:T(8,128)(2,1)S(1)} %copy-done.22), channel_id=1, source_target_pairs={{0,8},{1,9},{2,10},{3,11},{4,12},{5,13},{6,14},{7,15},{8,0},{9,1},... | collective-permute-start | bytes 393224 | tf_op jit(solution)/shard_map/ppermute | solution.py:1065
  24.9 11.9 %collective-permute-start.8 = (bf16[1,64,1024]{2,1,0:T(8,128)(2,1)S(1)}, bf16[1,64,1024]{2,1,0:T(8,128)(2,1)S(1)}, u32[]{:S(2)}, u32[]{:S(2)}) collective-permute-start(bf16[1,64,1024]{2,1,0:T(8,128)(2,1)S(1)} %copy-done.22), channel_id=1, source_target_pairs={{0,16},{1,17},{2,18},{3,19},{4,20},{5,21},{6,22},{7,23},{8,24},{9,... | collective-permute-start | bytes 393224 | tf_op jit(solution)/shard_map/ppermute | solution.py:1065
  25.9 10.9 %collective-permute-start.9 = (bf16[1,64,1024]{2,1,0:T(8,128)(2,1)S(1)}, bf16[1,64,1024]{2,1,0:T(8,128)(2,1)S(1)}, u32[]{:S(2)}, u32[]{:S(2)}) collective-permute-start(bf16[1,64,1024]{2,1,0:T(8,128)(2,1)S(1)} %copy-done.22), channel_id=1, source_target_pairs={{0,24},{1,25},{2,26},{3,27},{4,28},{5,29},{6,30},{7,31},{8,16},{9,... | collective-permute-start | bytes 393224 | tf_op jit(solution)/shard_map/ppermute | solution.py:1065
  31.1 6.8 %collective-permute-start.5 = (bf16[2,64,1024]{2,1,0:T(8,128)(2,1)S(1)}, bf16[2,64,1024]{2,1,0:T(8,128)(2,1)S(1)}, u32[]{:S(2)}, u32[]{:S(2)}) collective-permute-start(bf16[2,64,1024]{2,1,0:T(8,128)(2,1)S(1)} %slice.16), channel_id=1, source_target_pairs={{0,2},{1,3},{2,0},{3,1},{4,6},{5,7},{6,4},{7,5},{8,10},{9,11},{10,... | collective-permute-start | bytes 786440 | tf_op jit(solution)/shard_map/ppermute | solution.py:1065
  34.4 6.4 %collective-permute-start.6 = (bf16[2,64,1024]{2,1,0:T(8,128)(2,1)S(1)}, bf16[2,64,1024]{2,1,0:T(8,128)(2,1)S(1)}, u32[]{:S(2)}, u32[]{:S(2)}) collective-permute-start(bf16[2,64,1024]{2,1,0:T(8,128)(2,1)S(1)} %slice.17), channel_id=1, source_target_pairs={{0,4},{1,5},{2,6},{3,7},{4,0},{5,1},{6,2},{7,3},{8,12},{9,13},{10,... | collective-permute-start | bytes 786440 | tf_op jit(solution)/shard_map/ppermute | solution.py:1065
  43.1 14.5 %collective-permute-start.11 = (bf16[4,64,1024]{2,1,0:T(8,128)(2,1)S(1)}, bf16[4,64,1024]{2,1,0:T(8,128)(2,1)S(1)}, u32[]{:S(2)}, u32[]{:S(2)}) collective-permute-start(bf16[4,64,1024]{2,1,0:T(8,128)(2,1)S(1)} %pad_maximum_fusion.1.rest_5_), channel_id=1, source_target_pairs={{0,2},{1,3},{2,0},{3,1},{4,6},{5,7},{6,4},{7,5},{8,10},{9,11},{10,... | collective-permute-start | bytes 1572872 | tf_op jit(solution)/shard_map/ppermute | solution.py:1065
  44.7 14.6 %collective-permute-start.12 = (bf16[4,64,1024]{2,1,0:T(8,128)(2,1)S(1)}, bf16[4,64,1024]{2,1,0:T(8,128)(2,1)S(1)}, u32[]{:S(2)}, u32[]{:S(2)}) collective-permute-start(bf16[4,64,1024]{2,1,0:T(8,128)(2,1)S(1)} %pad_maximum_fusion.1.rest_5_), channel_id=1, source_target_pairs={{0,4},{1,5},{2,6},{3,7},{4,0},{5,1},{6,2},{7,3},{8,12},{9,13},{10,... | collective-permute-start | bytes 1572872 | tf_op jit(solution)/shard_map/ppermute | solution.py:1065
  48.9 13.4 %all-to-all-start = ((bf16[16,32,128]{2,1,0:T(8,128)(2,1)}), bf16[16,32,128]{2,1,0:T(8,128)(2,1)S(1)}, u32[]{:S(2)}, u32[]{:S(2)}) async-start(bf16[16,32,128]{2,1,0:T(8,128)(2,1)} %bitcast.2), calls=%async_computation | async-start | bytes 262144 | tf_op jit(solution)/shard_map/all_to_all | solution.py:1062
  62.3 17.0 %collective-permute-start.13 = (bf16[4,64,1024]{2,1,0:T(8,128)(2,1)S(1)}, bf16[4,64,1024]{2,1,0:T(8,128)(2,1)}, u32[]{:S(2)}, u32[]{:S(2)}) collective-permute-start(bf16[4,64,1024]{2,1,0:T(8,128)(2,1)S(1)} %collective-permute-done.12.rest_7_), channel_id=1, source_target_pairs={{0,2},{1,3},{2,0},{3,1},{4,6},{5,7},{6,4},{7,5},{8,10},{9,11},{10,... | collective-permute-start | bytes 1572872 | tf_op jit(solution)/shard_map/ppermute | solution.py:1065
  63.5 14.7 %collective-permute-start.14 = (bf16[1,64,1024]{2,1,0:T(8,128)(2,1)S(1)}, bf16[1,64,1024]{2,1,0:T(8,128)(2,1)S(1)}, u32[]{:S(2)}, u32[]{:S(2)}) collective-permute-start(bf16[1,64,1024]{2,1,0:T(8,128)(2,1)S(1)} %unpack.1.mixed_ref), channel_id=1, source_target_pairs={{0,8},{1,9},{2,10},{3,11},{4,12},{5,13},{6,14},{7,15},{8,0},{9,1},... | collective-permute-start | bytes 393224 | tf_op jit(solution)/shard_map/ppermute | solution.py:1065
  63.8 14.5 %collective-permute-start.15 = (bf16[1,64,1024]{2,1,0:T(8,128)(2,1)S(1)}, bf16[1,64,1024]{2,1,0:T(8,128)(2,1)S(1)}, u32[]{:S(2)}, u32[]{:S(2)}) collective-permute-start(bf16[1,64,1024]{2,1,0:T(8,128)(2,1)S(1)} %unpack.1.mixed_ref), channel_id=1, source_target_pairs={{0,16},{1,17},{2,18},{3,19},{4,20},{5,21},{6,22},{7,23},{8,24},{9,... | collective-permute-start | bytes 393224 | tf_op jit(solution)/shard_map/ppermute | solution.py:1065
  64.9 13.3 %collective-permute-start.16 = (bf16[1,64,1024]{2,1,0:T(8,128)(2,1)S(1)}, bf16[1,64,1024]{2,1,0:T(8,128)(2,1)S(1)}, u32[]{:S(2)}, u32[]{:S(2)}) collective-permute-start(bf16[1,64,1024]{2,1,0:T(8,128)(2,1)S(1)} %unpack.1.mixed_ref), channel_id=1, source_target_pairs={{0,24},{1,25},{2,26},{3,27},{4,28},{5,29},{6,30},{7,31},{8,16},{9,... | collective-permute-start | bytes 393224 | tf_op jit(solution)/shard_map/ppermute | solution.py:1065
  79.3 13.7 %all-to-all-start.1 = ((bf16[16,72,128]{2,1,0:T(8,128)(2,1)}), bf16[16,72,128]{2,1,0:T(8,128)(2,1)S(1)}, u32[]{:S(2)}, u32[]{:S(2)}) async-start(bf16[16,72,128]{2,1,0:T(8,128)(2,1)} %get-tuple-element.113), calls=%async_computation.1 | async-start | bytes 589824 | tf_op jit(solution)/shard_map/all_to_all | solution.py:1062
  82.8 14.6 %collective-permute-start.19 = (bf16[4,64,1024]{2,1,0:T(8,128)(2,1)S(1)}, bf16[4,64,1024]{2,1,0:T(8,128)(2,1)S(1)}, u32[]{:S(2)}, u32[]{:S(2)}) collective-permute-start(bf16[4,64,1024]{2,1,0:T(8,128)(2,1)S(1)} %pad_maximum_fusion.2.rest_9_), channel_id=1, source_target_pairs={{0,4},{1,5},{2,6},{3,7},{4,0},{5,1},{6,2},{7,3},{8,12},{9,13},{10,... | collective-permute-start | bytes 1572872 | tf_op jit(solution)/shard_map/ppermute | solution.py:1065
  84.6 14.4 %collective-permute-start.18 = (bf16[4,64,1024]{2,1,0:T(8,128)(2,1)S(1)}, bf16[4,64,1024]{2,1,0:T(8,128)(2,1)}, u32[]{:S(2)}, u32[]{:S(2)}) collective-permute-start(bf16[4,64,1024]{2,1,0:T(8,128)(2,1)S(1)} %pad_maximum_fusion.2.rest_9_), channel_id=1, source_target_pairs={{0,2},{1,3},{2,0},{3,1},{4,6},{5,7},{6,4},{7,5},{8,10},{9,11},{10,... | collective-permute-start | bytes 1572872 | tf_op jit(solution)/shard_map/ppermute | solution.py:1065
  97.4 10.2 %collective-permute-start.20 = (bf16[2,64,1024]{2,1,0:T(8,128)(2,1)S(1)}, bf16[2,64,1024]{2,1,0:T(8,128)(2,1)S(1)}, u32[]{:S(2)}, u32[]{:S(2)}) collective-permute-start(bf16[2,64,1024]{2,1,0:T(8,128)(2,1)S(1)} %slice.18), channel_id=1, source_target_pairs={{0,2},{1,3},{2,0},{3,1},{4,6},{5,7},{6,4},{7,5},{8,10},{9,11},{10,... | collective-permute-start | bytes 786440 | tf_op jit(solution)/shard_map/ppermute | solution.py:1065
  100.0 7.7 %collective-permute-start.21 = (bf16[2,64,1024]{2,1,0:T(8,128)(2,1)S(1)}, bf16[2,64,1024]{2,1,0:T(8,128)(2,1)S(1)}, u32[]{:S(2)}, u32[]{:S(2)}) collective-permute-start(bf16[2,64,1024]{2,1,0:T(8,128)(2,1)S(1)} %slice.19), channel_id=1, source_target_pairs={{0,4},{1,5},{2,6},{3,7},{4,0},{5,1},{6,2},{7,3},{8,12},{9,13},{10,... | collective-permute-start | bytes 786440 | tf_op jit(solution)/shard_map/ppermute | solution.py:1065
  102.6 24.3 %all-to-all-start.2 = ((bf16[16,96,128]{2,1,0:T(8,128)(2,1)}), bf16[16,96,128]{2,1,0:T(8,128)(2,1)S(1)}, u32[]{:S(2)}, u32[]{:S(2)}) async-start(bf16[16,96,128]{2,1,0:T(8,128)(2,1)} %get-tuple-element.122.dqkv_ref), calls=%async_computation.2 | async-start | bytes 786432 | tf_op jit(solution)/shard_map/all_to_all | solution.py:1062
  126.9 22.9 %all-to-all-start.3 = ((bf16[16,136,128]{2,1,0:T(8,128)(2,1)}), bf16[16,136,128]{2,1,0:T(8,128)(2,1)S(1)}, u32[]{:S(2)}, u32[]{:S(2)}) async-start(bf16[16,136,128]{2,1,0:T(8,128)(2,1)} %merge.1), calls=%async_computation.3 | async-start | bytes 1114112 | tf_op jit(solution)/shard_map/all_to_all | solution.py:1062
  (33 other events, 366.9 us)
